TPU v7x, 32 devices: a whole 2x2x4 slice. The times are simulated.
32 devices in a mesh: row: 4 (over y, x), col: 8 (over z, core).
Axes of the slice: x: 2, y: 2, z: 4, core: 2. Of those that a mesh axis runs over, the one named last changes fastest.
Arguments:
- features: bfloat16 [8192, 128], P(('row', 'col')), may hold values from -6 to 6
- tiles: bfloat16 [4, 8, 48, 128, 128], P('row', 'col'), may hold values from 0 to 1.5, as said below
- tile_row: int32 [4, 8, 48], P('row', 'col'), may hold values from 0 to 15, as said below
- tile_col: int32 [4, 8, 48], P('row', 'col'), may hold values from 0 to 7, as said below
- tile_live: int32 [4, 8], P('row', 'col'), may hold values from 1 to 48, as said below
- w_first: bfloat16 [128, 256], replicated, may hold values from -0.5 to 0.5
- b_first: float32 [256], replicated, may hold values from -3 to 3
- w_second: bfloat16 [256, 172], replicated, may hold values from -0.375 to 0.375
- b_second: float32 [172], replicated, may hold values from -3 to 3
- grad_logits: bfloat16 [8192, 172], P(('row', 'col')), may hold values from -0.039794922 to 0.039794922
Outputs:
- logits: bfloat16 [8192, 172], P(('row', 'col'))
- grad_w1: float32 [128, 256], replicated
- grad_b1: float32 [256], replicated
- grad_w2: float32 [256, 172], replicated
- grad_b2: float32 [172], replicated
Inputs may be any that keep to these rules, and one draw needn't show every extreme that they name: `tiles`: each entry is zero (no edge) or an edge weight. `tile_row`: block rows are local to a device's grid row, below 2 * 8. `tile_col`: block columns are local to a device's grid column, below 2 * 4; the occupied slots of one device name distinct (row, column) pairs. Slots from tile_live onward are unused: whatever their tiles and indices hold is ignored. Some device has all 48 slots occupied.
All inputs are finite; a program needn't handle non-finite values.
Results may differ from a plain program's by a relative error of at most 0.0051.
Values may be sent and summed in bfloat16 or wider, within the bound.
No kernel may reach another device: no remote copies, remote signals or barrier semaphores. Data moves between devices by JAX's collectives and lax.ppermute only.
A program may use at most 64 MiB of HBM per device.

v0:
```python
import jax
import jax.numpy as jnp
from jax import lax
from jax.sharding import PartitionSpec as P


def activation(values):
    return jax.nn.gelu(values, approximate=True)


def block_product(
    tile_slots, index_pick, index_put, live_count, source_blocks, out_count, form, turns
):
    group = 8
    width = source_blocks.shape[-1]
    block_size = tile_slots.shape[-1]

    def advance(step_index, total):
        start = step_index * group
        tile_group = lax.dynamic_slice_in_dim(tile_slots, start, group, 0)
        pick = lax.dynamic_slice_in_dim(index_pick, start, group, 0)
        put = lax.dynamic_slice_in_dim(index_put, start, group, 0)
        picked = source_blocks[pick]
        product = jnp.einsum(form, tile_group, picked, preferred_element_type=jnp.float32)
        weight = (start + jnp.arange(group) < live_count).astype(jnp.float32)
        return total.at[put].add(product * weight[:, None, None])

    empty = jnp.zeros((out_count, block_size, width), jnp.float32)
    return lax.fori_loop(0, turns, advance, empty)


def local(
    features,
    tiles,
    tile_row,
    tile_col,
    tile_live,
    w_first,
    b_first,
    w_second,
    b_second,
    grad_logits,
):
    highest = lax.Precision.HIGHEST
    row_count = lax.axis_size("row")
    col_count = lax.axis_size("col")
    node_count = features.shape[0]
    block_size = tiles.shape[-1]
    own_blocks = node_count // block_size
    tile_slots = tiles[0, 0]
    rows_index = tile_row[0, 0]
    cols_index = tile_col[0, 0]
    live_count = tile_live[0, 0]
    slot_count = tile_slots.shape[0]
    turns = slot_count // 8
    row_blocks = col_count * own_blocks
    col_blocks = row_count * own_blocks
    live_mask = (jnp.arange(slot_count) < live_count).astype(jnp.float32)
    row_totals = jnp.sum(tile_slots, axis=2, dtype=jnp.float32) * live_mask[:, None]
    degree_part = jnp.zeros((row_blocks, block_size), jnp.float32).at[rows_index].add(row_totals)
    column_input = lax.all_gather(features, "row", axis=0, tiled=True)
    input_blocks = column_input.reshape(col_blocks, block_size, features.shape[1])
    first_part = block_product(
        tile_slots,
        cols_index,
        rows_index,
        live_count,
        input_blocks,
        row_blocks,
        "tij,tjf->tif",
        turns,
    )
    first_sum, degree_sum = (
        lax.psum_scatter(
            first_part.reshape(row_blocks * block_size, features.shape[1]),
            "col",
            scatter_dimension=0,
            tiled=True,
        ),
        lax.psum_scatter(
            degree_part.reshape(row_blocks * block_size), "col", scatter_dimension=0, tiled=True
        ),
    )
    degree = 1.0 + degree_sum
    agg1 = ((first_sum + features.astype(jnp.float32)) / degree[:, None]).astype(jnp.bfloat16)
    z_first = jnp.dot(agg1, w_first, preferred_element_type=jnp.float32) + b_first
    hidden = activation(z_first).astype(jnp.bfloat16)
    column_hidden = lax.all_gather(hidden, "row", axis=0, tiled=True)
    hidden_blocks = column_hidden.reshape(col_blocks, block_size, hidden.shape[1])
    second_part = block_product(
        tile_slots,
        cols_index,
        rows_index,
        live_count,
        hidden_blocks,
        row_blocks,
        "tij,tjf->tif",
        turns,
    )
    second_part = second_part.reshape(row_blocks * block_size, hidden.shape[1])
    w_second_float = w_second.astype(jnp.float32)
    hidden_float = hidden.astype(jnp.float32)
    second_sum = lax.psum_scatter(
        second_part.astype(jnp.bfloat16), "col", scatter_dimension=0, tiled=True
    ).astype(jnp.float32)
    projected = jnp.dot(second_sum + hidden_float, w_second_float, precision=highest)
    logits = (projected / degree[:, None] + b_second).astype(jnp.bfloat16)
    grad_float = grad_logits.astype(jnp.float32)
    grad_b2 = jnp.sum(grad_float, axis=0)
    scaled = (grad_float / degree[:, None]).astype(jnp.bfloat16)
    row_scaled = lax.all_gather(scaled, "col", axis=0, tiled=True)
    scaled_blocks = row_scaled.reshape(row_blocks, block_size, scaled.shape[1])
    back_part = block_product(
        tile_slots,
        rows_index,
        cols_index,
        live_count,
        scaled_blocks,
        col_blocks,
        "tij,tif->tjf",
        turns,
    )
    back_sum = lax.psum_scatter(
        back_part.reshape(col_blocks * block_size, scaled.shape[1]),
        "row",
        scatter_dimension=0,
        tiled=True,
    )
    q_field = back_sum + scaled.astype(jnp.float32)
    grad_w2 = jnp.dot(hidden_float.T, q_field, precision=highest)
    d_hidden = jnp.dot(q_field, w_second_float.T, precision=highest)
    d_first = jax.vjp(activation, z_first)[1](d_hidden)[0]
    d_half = d_first.astype(jnp.bfloat16)
    grad_w1 = jnp.dot(agg1.T, d_half, preferred_element_type=jnp.float32)
    grad_b1 = jnp.sum(d_first, axis=0)
    grad_w1, grad_b1, grad_w2, grad_b2 = lax.psum(
        (grad_w1, grad_b1, grad_w2, grad_b2), ("row", "col")
    )
    return (logits, grad_w1, grad_b1, grad_w2, grad_b2)


def solution(mesh):
    return jax.shard_map(
        local,
        mesh=mesh,
        in_specs=(
            P(("row", "col"), None),
            P("row", "col", None, None, None),
            P("row", "col", None),
            P("row", "col", None),
            P("row", "col"),
            P(),
            P(),
            P(),
            P(),
            P(("row", "col"), None),
        ),
        out_specs=(P(("row", "col"), None), P(), P(), P(), P()),
        check_vma=False,
    )
```

profile of v0, /device:TPU:0, one launch (start us, length us, event | category | flops | bytes accessed | tf_op | source)
XLA Modules:
  0.0 339.9 jit_solution(11211206294428952056)
XLA Ops:
  7.2 10.7 %all_gather.9 = bf16[1024,128]{1,0:T(8,128)(2,1)S(1)} all-gather(bf16[256,128]{1,0:T(8,128)(2,1)} %param.16), channel_id=1, replica_groups=mesh['row'=4,'col'=8] {'row'}, dimensions={0}, use_global_device_ids=true | all-gather | bytes 327680 | tf_op jit(solution)/shard_map/all_gather | solution.py:61
  18.1 25.6 %while.39 = (s32[]{:T(128)}, f32[16,128,128]{2,1,0:T(8,128)S(1)}, s32[48]{0:T(128)}, bf16[48,128,128]{2,1,0:T(8,128)(2,1)}, s32[48]{0:T(128)}, /*index=5*/bf16[8...) while((s32[]{:T(128)}, f32[16,128,128]{2,1,0:T(8,128)S(1)}, ...), condition=%wide.region_2.3_spmd, body=%wide.region_0.2_spmd.sunk | while | flops 33817676 | bytes 3150283 | solution.py:29
  46.0 1.9 convert_reduce_fusion
  48.8 15.2 %all-reduce = f32[2048]{0:T(1024)S(1)} all-reduce(f32[2048]{0:T(1024)S(1)} %bitcast.53), channel_id=3, replica_groups=mesh['row'=4,'col'=8] {'col'}, use_global_device_ids=true, to_apply=%region_6.0.clone | all-reduce | flops 2048 | bytes 16384
  65.4 16.6 %all_gather.11 = bf16[2048,172]{0,1:T(8,128)(2,1)S(1)} all-gather(bf16[256,172]{0,1:T(8,128)(2,1)S(1)} %get-tuple-element.447), channel_id=1, replica_groups=mesh['row'=4,'col'=8] {'col'}, dimensions={0}, use_global_device_ids=true | all-gather | bytes 792576 | tf_op jit(solution)/shard_map/all_gather | solution.py:111
  82.6 24.3 %while.41 = (s32[]{:T(128)}, f32[8,128,172]{1,2,0:T(8,128)S(1)}, s32[48]{0:T(128)S(1)}, bf16[48,128,128]{2,1,0:T(8,128)(2,1)}, s32[48]{0:T(128)S(1)}, /*index=5*...) while((s32[]{:T(128)}, f32[8,128,172]{1,2,0:T(8,128)S(1)}, ...), condition=%wide.region_13.14_spmd, body=%wide.region_11.13_spmd.sunk | while | flops 45442124 | bytes 4141515 | solution.py:29
  85.3 1.4 scatter_fusion.2
  88.1 1.3 convolution_multiply_fusion.8
  89.4 1.4 scatter_fusion.2
  92.1 1.3 convolution_multiply_fusion.8
  93.4 1.4 scatter_fusion.2
  96.2 1.3 convolution_multiply_fusion.8
  97.5 1.4 scatter_fusion.2
  101.5 1.4 scatter_fusion.2
  104.3 1.3 convolution_multiply_fusion.8
  105.6 1.4 scatter_fusion.2
  109.7 13.2 %all_gather.10 = bf16[1024,256]{1,0:T(8,128)(2,1)S(1)} all-gather(bf16[256,256]{1,0:T(8,128)(2,1)S(1)} %get-tuple-element.448), channel_id=1, replica_groups=mesh['row'=4,'col'=8] {'row'}, dimensions={0}, use_global_device_ids=true | all-gather | bytes 655360 | tf_op jit(solution)/shard_map/all_gather | solution.py:88
  123.0 1.6 broadcast_in_dim.70
  124.5 35.3 %while.40 = (s32[]{:T(128)}, f32[16,128,256]{2,1,0:T(8,128)}, s32[48]{0:T(128)S(1)}, bf16[48,128,128]{2,1,0:T(8,128)(2,1)}, s32[48]{0:T(128)S(1)}, /*index=5*/bf...) while((s32[]{:T(128)}, f32[16,128,256]{2,1,0:T(8,128)}, ...), condition=%wide.region_9.0_spmd, body=%wide.region_7.0_spmd.sunk | while | flops 67634256 | bytes 6033867 | solution.py:29
  127.1 3.2 scatter_fusion.1
  132.9 3.2 scatter_fusion.1
  138.7 3.3 scatter_fusion.1
  144.7 3.4 scatter_fusion.1
  150.6 3.3 scatter_fusion.1
  156.5 3.3 scatter_fusion.1
  159.9 2.7 convert_element_type.85
  162.7 1.5 fusion.27
  164.2 37.1 %all-reduce.1 = (f32[256]{0:T(256)}, f32[172]{0:T(256)}) all-reduce(f32[256]{0:T(256)S(1)} %get-tuple-element.450, f32[172]{0:T(256)S(1)} %get-tuple-element.446), channel_id=1, replica_groups=mesh['row'=4,'col'=8] {'row','col'}, use_global_device_ids=true, to_apply=%region_17.0 | all-reduce | flops 428 | bytes 3424 | tf_op jit(solution)/shard_map/psum | solution.py:136
  203.1 1.9 fusion.7
  205.0 125.2 %all-reduce.5.cloned.1.call-done = (f32[128,256]{1,0:T(8,128)}, f32[256,172]{0,1:T(8,128)}) async-done(((f32[128,256]{1,0:T(8,128)}, f32[256,172]{0,1:T(8,128)}), (f32[128,256]{1,0:T(8,128)}, f32[256,172]{0,1:T(8,128)})) %all-reduce.5.cloned.1.call-update) | async-done | bytes 307216 | tf_op jit(solution)/shard_map/psum | solution.py:136
  330.2 1.6 copy.50
  331.8 1.6 copy.51
  (141 shorter events, 59.7 us)
Async XLA Ops:
  7.2 155.5 %copy-start = (bf16[256,172]{0,1:T(8,128)(2,1)S(1)}, bf16[256,172]{0,1:T(8,128)(2,1)}, u32[]{:S(2)}) copy-start(bf16[256,172]{0,1:T(8,128)(2,1)} %param.23) | copy-start | bytes 264196
  7.2 101.2 %reduce-scatter.4.cloned.1.call-start = ((), (), s32[]{:S(2)}) async-start(), calls=%async_computation.3 | async-start | bytes 1179648 | tf_op jit(solution)/shard_map/reduce_scatter | solution.py:74
  43.7 1.0 copy-start.1
  43.7 20.3 %copy-start.10 = (u32[32]{0:T(128)S(1)}, u32[32]{0:T(128)}, u32[]{:S(2)}) copy-start(u32[32]{0:T(128)} %constant.138) | copy-start | bytes 388
  43.7 21.6 %copy-start.6 = (bf16[256,172]{0,1:T(8,128)(2,1)S(1)}, bf16[256,172]{0,1:T(8,128)(2,1)}, u32[]{:S(2)}) copy-start(bf16[256,172]{0,1:T(8,128)(2,1)} %param.25) | copy-start | bytes 264196
  44.7 118.0 %reduce-scatter.8.cloned.1.call-start = ((), (), s32[]{:S(2)}) async-start(), calls=%async_computation.5 | async-start | bytes 901120 | tf_op jit(solution)/shard_map/reduce_scatter | solution.py:123
  47.9 34.7 %copy-start.4 = (s32[48]{0:T(128)S(1)}, s32[48]{0:T(128)}, u32[]{:S(2)}) copy-start(s32[48]{0:T(128)} %get-tuple-element.722) | copy-start | bytes 580
  48.0 34.7 %copy-start.5 = (s32[48]{0:T(128)S(1)}, s32[48]{0:T(128)}, u32[]{:S(2)}) copy-start(s32[48]{0:T(128)} %get-tuple-element.724) | copy-start | bytes 580
  107.2 1.2 copy-start.2
  107.2 2.2 copy-start.7
  107.3 2.2 copy-start.8
  108.4 94.8 %reduce-scatter.6.cloned.1.call-start = ((), (), s32[]{:S(2)}) async-start(), calls=%async_computation.4 | async-start | bytes 1179648 | tf_op jit(solution)/shard_map/reduce_scatter | solution.py:103
  162.6 40.6 %copy-start.9 = (f32[172]{0:T(256)S(1)}, f32[172]{0:T(256)}, u32[]{:S(2)}) copy-start(f32[172]{0:T(256)} %param.24) | copy-start | bytes 2068
  162.6 167.6 %all-reduce.5.cloned.1.call-start = ((), (), s32[]{:S(2)}) async-start(), calls=%async_computation.6 | async-start | bytes 622592 | tf_op jit(solution)/shard_map/psum | solution.py:136
  162.7 39.5 %copy-start.3 = (f32[256,172]{0,1:T(8,128)S(1)}, f32[256,172]{0,1:T(8,128)}, u32[]{:S(2)}) copy-start(f32[256,172]{0,1:T(8,128)} %reduce-scatter.8.cloned.1.call-done) | copy-start | bytes 528388
Sparse Core Ops, SparseCore 0:
  44.8 33.7 reduce-scatter.3
  108.5 24.4 reduce-scatter.7
  162.7 29.5 reduce-scatter.5
  203.2 126.9 all-reduce.4
where the time goes:
time: 342 us; the launch traced here: 340 us
  waiting for transfers between devices  125 us (37%)
  blocking collectives  92.9 us (27%)
  other arithmetic  58.9 us (17%)
  matrix products  27.7 us (8%)
  local copies, waits for them, and re-layouts  18.8 us (5%)
  between operations  15.4 us (5%)
    psum x1, waiting for transfers between devices, local(): lax.psum((grad_w1, grad_b1, grad_w2, grad_b2), ('row', 'col'))  125 us
    psum x1, blocking collectives, local(): lax.psum((grad_w1, grad_b1, grad_w2, grad_b2), ('row', 'col'))  37.1 us
    scatter-add x18, other arithmetic, advance(): return total.at[put].add(product * weight[:, None, None])  34.3 us
    dot_general x18, matrix products, advance(): jnp.einsum(form, tile_group, picked, preferred_element_type=jnp.float32)  22.3 us
    all_gather x1, blocking collectives, local(): row_scaled = lax.all_gather(scaled, 'col', axis=0, tiled=True)  16.6 us
    unnamed x1, blocking collectives  15.2 us
    all_gather x1, blocking collectives, local(): column_hidden = lax.all_gather(hidden, 'row', axis=0, tiled=True)  13.2 us
    convert_element_type x18, other arithmetic, advance(): weight = (start + jnp.arange(group) < live_count).astype(jnp.float32)  11.7 us
  transfers between devices with their start and end apart: 4, of which 1 were waited for; matrix products, arithmetic and copies ran while one was open for 22% of the time, Pallas kernels for 0%

commit v1 on v0

v1 whole, which is shorter than its diff:
```python
import functools

import jax
import jax.numpy as jnp
from jax import lax
from jax.experimental import pallas as pl
from jax.experimental.pallas import tpu as pltpu
from jax.sharding import PartitionSpec as P

BF16 = jnp.bfloat16
F32 = jnp.float32


def exchange(value, axis, mask):
    count = lax.axis_size(axis)
    return lax.ppermute(value, axis, [(i, i ^ mask) for i in range(count)])


def swap_halves(value, parts):
    pairs = value.reshape((parts, 2, -1) + value.shape[1:])
    return jnp.concatenate([pairs[:, 1:], pairs[:, :1]], axis=1).reshape(value.shape)


def dense_kernel(own, row_ref, col_ref, live_ref, place_ref, tiles_ref, dense_ref, degree_ref):
    slots, block, _ = tiles_ref.shape
    half = dense_ref.shape[0] // (block * own * 2)
    r, c = place_ref[0], place_ref[1]
    dense_ref[...] = jnp.zeros_like(dense_ref)

    @pl.loop(0, live_ref[0])
    def _(slot):
        k = row_ref[slot]
        j = col_ref[slot]
        p = (k // own) ^ c
        at_row = ((p & 1) * half + (p >> 1)) * own + k % own
        at_col = ((j // own) ^ r) * own + j % own
        dense_ref[
            pl.ds(pl.multiple_of(at_row * block, block), block),
            pl.ds(pl.multiple_of(at_col * block, block), block),
        ] = tiles_ref[slot]

    rows, columns = dense_ref.shape
    ones = jnp.ones((8, columns), BF16)
    chunk = 256

    for start in range(0, rows, chunk):
        sums = lax.dot_general(
            ones,
            dense_ref[pl.ds(start, chunk), :],
            (((1,), (1,)), ((), ())),
            preferred_element_type=F32,
        )
        for part in range(chunk // block):
            degree_ref[pl.ds(start // block + part, 1), :] = sums[
                :1, part * block : (part + 1) * block
            ]


def dense_adjacency(tiles, tile_row, tile_col, tile_live, own, rows, columns):
    place = jnp.stack([lax.axis_index("row"), lax.axis_index("col")]).astype(jnp.int32)
    block = tiles.shape[-1]
    need = rows * columns * 2 + tiles.size * 2 + rows * 16
    smem = pl.BlockSpec(memory_space=pltpu.SMEM)
    vmem = pl.BlockSpec(memory_space=pltpu.VMEM)
    return pl.pallas_call(
        functools.partial(dense_kernel, own),
        out_shape=(
            jax.ShapeDtypeStruct((rows, columns), BF16),
            jax.ShapeDtypeStruct((rows // block, block), F32),
        ),
        in_specs=[smem, smem, smem, smem, vmem],
        out_specs=(vmem, vmem),
        compiler_params=pltpu.CompilerParams(vmem_limit_bytes=need + (8 << 20)),
        cost_estimate=pl.CostEstimate(
            flops=16 * rows * columns, bytes_accessed=rows * columns * 2 + tiles.size * 2, transcendentals=0
        ),
        name="dense_adjacency",
    )(tile_row, tile_col, tile_live, place, tiles)


def gather_row(value):
    count = lax.axis_size("row")
    return jnp.concatenate([value] + [exchange(value, "row", s) for s in range(1, count)], axis=0)


def gather_col(value):
    half = lax.axis_size("col") // 2
    pieces = [value] + [exchange(value, "col", 2 * s) for s in range(1, half)]
    near = jnp.concatenate(pieces, axis=0)
    return jnp.concatenate([near, exchange(near, "col", 1)], axis=0)


def scatter_col(part, nodes):
    half = lax.axis_size("col") // 2
    middle = part.shape[0] // 2
    other = exchange(part[middle:], "col", 1)
    near = part[:middle].astype(F32) + other.astype(F32)
    sent = near.astype(BF16)
    total = near[:nodes]
    for s in range(1, half):
        total = total + exchange(sent[s * nodes : (s + 1) * nodes], "col", 2 * s).astype(F32)
    return total


def total_col(value, own):
    count = lax.axis_size("col")
    value = value + swap_halves(exchange(value, "col", 1), 1)
    mask, parts = count // 2, 2
    while mask > 1:
        value = value + swap_halves(exchange(value, "col", mask), parts)
        mask, parts = mask // 2, parts * 2
    return value


def split(value):
    high = value.astype(BF16)
    return high, (value - high.astype(F32)).astype(BF16)


def total_all(values):
    rows = lax.axis_size("row")
    size = values.shape[0] // rows
    me = lax.axis_index("row")
    blocks = values.reshape((rows, size) + values.shape[1:])
    mine = lax.dynamic_index_in_dim(blocks, me, 0, keepdims=False)
    for s in range(1, rows):
        block = lax.dynamic_index_in_dim(blocks, me ^ s, 0, keepdims=False)
        mine = mine + exchange(block.astype(BF16), "row", s).astype(F32)
    mask = 1
    while mask < lax.axis_size("col"):
        mine = mine + exchange(mine, "col", mask)
        mask *= 2
    got = jnp.stack([mine] + [exchange(mine, "row", s) for s in range(1, rows)])
    return got[jnp.arange(rows) ^ me].reshape(values.shape)


def local(
    features,
    tiles,
    tile_row,
    tile_col,
    tile_live,
    w_first,
    b_first,
    w_second,
    b_second,
    grad_logits,
):
    row_count = lax.axis_size("row")
    col_count = lax.axis_size("col")
    nodes = features.shape[0]
    block = tiles.shape[-1]
    own = nodes // block
    hidden = w_first.shape[1]
    classes = w_second.shape[1]
    rows, columns = col_count * nodes, row_count * nodes

    inputs = gather_row(features)
    cotangents = gather_col(grad_logits)
    dense, degree_part = dense_adjacency(
        tiles[0, 0], tile_row[0, 0], tile_col[0, 0], tile_live[0], own, rows, columns
    )
    first_part = jnp.dot(dense, inputs, preferred_element_type=F32).astype(BF16)
    degree = 1.0 + total_col(degree_part, own).reshape(rows)
    own_degree = degree[:nodes, None]
    first_sum = scatter_col(first_part, nodes)
    agg1 = ((first_sum + features.astype(F32)) / own_degree).astype(BF16)

    scaled = (cotangents.astype(F32) / degree[:, None]).astype(BF16)
    q_part = lax.dot_general(dense, scaled, (((0,), (0,)), ((), ())), preferred_element_type=F32)
    q_part = q_part + jnp.pad(scaled[:nodes].astype(F32), ((0, columns - nodes), (0, 0)))

    agg_all = gather_row(agg1)
    z_first = jnp.dot(agg_all, w_first, preferred_element_type=F32) + b_first
    h_float, slope = jax.vjp(lambda z: jax.nn.gelu(z, approximate=True), z_first)
    h_all = h_float.astype(BF16)
    projected = jnp.dot(h_all, w_second, preferred_element_type=F32)
    second_part = jnp.dot(dense, projected.astype(BF16), preferred_element_type=F32).astype(BF16)
    second_sum = scatter_col(second_part, nodes)
    logits = ((second_sum + projected[:nodes]) / own_degree + b_second).astype(BF16)

    q_high, q_low = split(q_part)
    rows_first = (((0,), (0,)), ((), ()))
    grad_w2 = lax.dot_general(h_all, q_high, rows_first, preferred_element_type=F32)
    grad_w2 = grad_w2 + lax.dot_general(h_all, q_low, rows_first, preferred_element_type=F32)
    d_hidden = jnp.dot(q_high, w_second.T, preferred_element_type=F32)
    d_hidden = d_hidden + jnp.dot(q_low, w_second.T, preferred_element_type=F32)
    d_first = slope(d_hidden)[0]
    grad_w1 = lax.dot_general(agg_all, d_first.astype(BF16), rows_first, preferred_element_type=F32)
    grad_b1 = jnp.sum(d_first, axis=0)
    grad_b2 = jnp.sum(grad_logits.astype(F32), axis=0)

    fin = w_first.shape[0]
    pad = ((0, 0), (0, hidden - classes))
    biases = jnp.stack([grad_b1, jnp.pad(grad_b2, pad[1:])])
    extra = -(fin + hidden + 2) % (8 * row_count * 2)
    packed = jnp.concatenate(
        [grad_w1, jnp.pad(grad_w2, pad), biases, jnp.zeros((extra, hidden), F32)], axis=0
    )
    packed = total_all(packed)
    return (
        logits,
        packed[:fin],
        packed[fin + hidden],
        packed[fin : fin + hidden, :classes],
        packed[fin + hidden + 1, :classes],
    )


def solution(mesh):
    return jax.shard_map(
        local,
        mesh=mesh,
        in_specs=(
            P(("row", "col"), None),
            P("row", "col", None, None, None),
            P("row", "col", None),
            P("row", "col", None),
            P("row", "col"),
            P(),
            P(),
            P(),
            P(),
            P(("row", "col"), None),
        ),
        out_specs=(P(("row", "col"), None), P(), P(), P(), P()),
        check_vma=False,
    )
```

time: 342 us -> 94 us (0.27)
  waiting for transfers between devices: 125 us -> 30 us
  blocking collectives: 92.9 us -> 0 us
  other arithmetic: 58.9 us -> 2.47 us
  starting transfers between devices: 0.16 us -> 36.4 us
  matrix products: 27.7 us -> 11.1 us
  between operations: 15.4 us -> 1.77 us
  local copies, waits for them, and re-layouts: 18.8 us -> 9.63 us
    psum x1 -> x0, waiting for transfers between devices: 125 us -> none  [local(): lax.psum((grad_w1, grad_b1, grad_w2, grad_b2), ('row', 'col'))]
    all_gather x3 -> x0, blocking collectives: 40.6 us -> none  [the longest x1 16.6 us: local(): row_scaled = lax.all_gather(scaled, 'col', axis=0, tiled=True)]
    psum x1 -> x0, blocking collectives: 37.1 us -> none  [local(): lax.psum((grad_w1, grad_b1, grad_w2, grad_b2), ('row', 'col'))]
    ppermute x0 -> x30, starting transfers between devices: none -> 36.4 us  [exchange(): return lax.ppermute(value, axis, [(i, i ^ mask) for i in range(count)])]
    scatter-add x19 -> x0, other arithmetic: 35.1 us -> none  [the longest x18 34.3 us: advance(): return total.at[put].add(product * weight[:, None, None])]
    ppermute x0 -> x30, waiting for transfers between devices: none -> 30 us  [exchange(): return lax.ppermute(value, axis, [(i, i ^ mask) for i in range(count)])]
    dot_general x23 -> x10, matrix products: 27.7 us -> 11.1 us  [the longest x1 3.73 us: local(): jnp.dot(dense, projected.astype(BF16), preferred_element_type=F32)]
    unnamed x1 -> x0, blocking collectives: 15.2 us -> none
  transfers between devices with their start and end apart: 4 -> 30, of which waited for: 1 -> 14; matrix products, arithmetic and copies ran while one was open for 22% -> 13% of each run, Pallas kernels for 0% -> 0%
where the time goes in v1:
time: 94 us; the launch traced here: 93.9 us
  starting transfers between devices  36.4 us (39%)
  waiting for transfers between devices  30 us (32%)
  matrix products  11.1 us (12%)
  local copies, waits for them, and re-layouts  9.63 us (10%)
  Pallas kernels  2.55 us (3%)
  other arithmetic  2.47 us (3%)
  between operations  1.77 us (2%)
    ppermute x30, starting transfers between devices, exchange(): return lax.ppermute(value, axis, [(i, i ^ mask) for i in range(count)])  36.4 us
    ppermute x30, waiting for transfers between devices, exchange(): return lax.ppermute(value, axis, [(i, i ^ mask) for i in range(count)])  30 us
    unnamed x29, local copies, waits for them, and re-layouts  6.44 us
    dot_general x1, matrix products, local(): jnp.dot(dense, projected.astype(BF16), preferred_element_type=F32)  3.73 us
    dot_general x1, matrix products, local(): first_part = jnp.dot(dense, inputs, preferred_element_type=F32).astype(BF16)  3.48 us
    pallas_call x1, Pallas kernels, dense_adjacency(): pl.pallas_call(functools.partial(dense_kernel, own), out_shape=(jax.Shape...  2.55 us
  transfers between devices with their start and end apart: 30, of which 14 were waited for; matrix products, arithmetic and copies ran while one was open for 13% of the time, Pallas kernels for 0%

profile of v1, /device:TPU:0, one launch (start us, length us, event | category | flops | bytes accessed | tf_op | source)
XLA Modules:
  0.0 93.9 jit_solution(9809913946092375339)
XLA Ops:
  1.4 1.4 %copy-done.1 = bf16[1,1,48,128,128]{4,3,2,1,0:T(8,128)(2,1)S(1)} copy-done((bf16[1,1,48,128,128]{4,3,2,1,0:T(8,128)(2,1)S(1)}, bf16[1,1,48,128,128]{4,3,2,1,0:T(8,128)(2,1)}, u32[]{:S(2)}) %copy-start.1) | copy-done | bytes 1572888
  4.1 2.6 %dense_adjacency.1 = (bf16[2048,1024]{1,0:T(8,128)(2,1)S(1)}, f32[16,128]{1,0:T(8,128)S(1)}) custom-call(s32[48]{0:T(128)S(1)} %bitcast.56, s32[48]{0:T(128)S(1)} %bitcast.57, s32[1]{0:T(128)} %bitcast.54.live_ref, s32[2]{0:T(128)S(1)} %pad_add_fusion.place_ref, bf16[48,128,128]{2,1,0:T(8,128)(2,1)S(1)} %bitcast.55), custom_call_target="tpu_custom_call" | custom-call | flops 33554432 | bytes 5767168 | tf_op jit(solution)/shard_map/dense_adjacency/pallas_call | solution.py:65
  6.7 2.0 %copy-done.4 = bf16[2048,1024]{1,0:T(8,128)(2,1)} copy-done((bf16[2048,1024]{1,0:T(8,128)(2,1)}, bf16[2048,1024]{1,0:T(8,128)(2,1)S(1)}, u32[]{:S(2)}) %copy-start.4) | copy-done | bytes 4194328
  8.9 3.0 %collective-permute-start.17 = (bf16[256,172]{0,1:T(8,128)(2,1)}, bf16[256,172]{0,1:T(8,128)(2,1)S(1)}, u32[]{:S(2)}, u32[]{:S(2)}) collective-permute-start(bf16[256,172]{0,1:T(8,128)(2,1)} %param.19), channel_id=1, source_target_pairs={{0,2},{1,3},{2,0},{3,1},{4,6},{5,7},{6,4},{7,5},{8,10},{9,11},{10,... | collective-permute-start | bytes 264200 | tf_op jit(solution)/shard_map/ppermute | solution.py:16
  11.8 2.3 %collective-permute-start.18 = (bf16[256,172]{0,1:T(8,128)(2,1)}, bf16[256,172]{0,1:T(8,128)(2,1)S(1)}, u32[]{:S(2)}, u32[]{:S(2)}) collective-permute-start(bf16[256,172]{0,1:T(8,128)(2,1)} %param.19), channel_id=1, source_target_pairs={{0,4},{1,5},{2,6},{3,7},{4,0},{5,1},{6,2},{7,3},{8,12},{9,13},{10,... | collective-permute-start | bytes 264200 | tf_op jit(solution)/shard_map/ppermute | solution.py:16
  14.1 1.3 %collective-permute-start = (bf16[256,128]{1,0:T(8,128)(2,1)}, bf16[256,128]{1,0:T(8,128)(2,1)S(1)}, u32[]{:S(2)}, u32[]{:S(2)}) collective-permute-start(bf16[256,128]{1,0:T(8,128)(2,1)} %param.10), channel_id=1, source_target_pairs={{0,8},{8,0},{16,24},{24,16},{1,9},{9,1},{17,25},{25,17},{2,10},{10... | collective-permute-start | bytes 196616 | tf_op jit(solution)/shard_map/ppermute | solution.py:16
  15.3 1.9 %collective-permute-start.1 = (bf16[256,128]{1,0:T(8,128)(2,1)}, bf16[256,128]{1,0:T(8,128)(2,1)S(1)}, u32[]{:S(2)}, u32[]{:S(2)}) collective-permute-start(bf16[256,128]{1,0:T(8,128)(2,1)} %param.10), channel_id=1, source_target_pairs={{0,16},{8,24},{16,0},{24,8},{1,17},{9,25},{17,1},{25,9},{2,18},{10... | collective-permute-start | bytes 196616 | tf_op jit(solution)/shard_map/ppermute | solution.py:16
  17.7 1.0 %convert_reduce_fusion = f32[172]{0:T(256)S(1)} fusion(bf16[256,172]{0,1:T(8,128)(2,1)} %param.19), kind=kLoop, calls=%fused_computation.40 | loop fusion | flops 87892 | bytes 88752 | tf_op jit(solution)/shard_map/reduce_sum | solution.py:191
  18.7 3.2 %collective-permute-done.8 = f32[16,128]{1,0:T(8,128)S(1)} collective-permute-done((f32[16,128]{1,0:T(8,128)S(1)}, f32[16,128]{1,0:T(8,128)S(1)}, u32[]{:S(2)}, u32[]{:S(2)}) %collective-permute-start.8) | collective-permute-done | bytes 8224 | tf_op jit(solution)/shard_map/ppermute | solution.py:16
  23.7 1.9 %collective-permute-done.9 = f32[16,128]{1,0:T(8,128)S(1)} collective-permute-done((f32[16,128]{1,0:T(8,128)S(1)}, f32[16,128]{1,0:T(8,128)S(1)}, u32[]{:S(2)}, u32[]{:S(2)}) %collective-permute-start.9) | collective-permute-done | bytes 8224 | tf_op jit(solution)/shard_map/ppermute | solution.py:16
  26.0 2.8 %collective-permute-start.19 = (bf16[256,172]{0,1:T(8,128)(2,1)}, bf16[256,172]{0,1:T(8,128)(2,1)S(1)}, u32[]{:S(2)}, u32[]{:S(2)}) collective-permute-start(bf16[256,172]{0,1:T(8,128)(2,1)} %param.19), channel_id=1, source_target_pairs={{0,6},{1,7},{2,4},{3,5},{4,2},{5,3},{6,0},{7,1},{8,14},{9,15},{10,... | collective-permute-start | bytes 264200 | tf_op jit(solution)/shard_map/ppermute | solution.py:16
  28.8 2.2 %collective-permute-done.2 = bf16[256,128]{1,0:T(8,128)(2,1)S(1)} collective-permute-done((bf16[256,128]{1,0:T(8,128)(2,1)}, bf16[256,128]{1,0:T(8,128)(2,1)S(1)}, u32[]{:S(2)}, u32[]{:S(2)}) %collective-permute-start.2) | collective-permute-done | bytes 65568 | tf_op jit(solution)/shard_map/ppermute | solution.py:16
  31.0 3.5 %convolution_convert_fusion.1 = bf16[2048,128]{1,0:T(8,128)(2,1)S(1)} fusion(bf16[2048,1024]{1,0:T(8,128)(2,1)} %copy-done.4, bf16[256,128]{1,0:T(8,128)(2,1)S(1)} %collective-permute-done.2, bf16[256,128]{1,0:T(8,128)(2,1)S(1)} %collective-permute-done.1, bf16[256,128]{1,0:T(8,128)(2,1)S(1)} %collective-permute-done, bf16[256,128]{1,0:T(8,128)(2,1)} %param.10), kind=kOutput, calls=%fused_computation.2 | convolution fusion | flops 538181632 | bytes 4980736 | tf_op jit(solution)/shard_map/dot_general | solution.py:163
  37.3 3.3 %collective-permute-start.6 = (bf16[256,128]{1,0:T(8,128)(2,1)S(1)}, bf16[256,128]{1,0:T(8,128)(2,1)S(1)}, u32[]{:S(2)}, u32[]{:S(2)}) collective-permute-start(bf16[256,128]{1,0:T(8,128)(2,1)S(1)} %get-tuple-element.30), channel_id=1, source_target_pairs={{0,6},{1,7},{2,4},{3,5},{4,2},{5,3},{6,0},{7,1},{8,14},{9,15},{10,... | collective-permute-start | bytes 196616 | tf_op jit(solution)/shard_map/ppermute | solution.py:16
  41.2 4.0 %collective-permute-done.5 = bf16[256,128]{1,0:T(8,128)(2,1)S(1)} collective-permute-done((bf16[256,128]{1,0:T(8,128)(2,1)S(1)}, bf16[256,128]{1,0:T(8,128)(2,1)S(1)}, u32[]{:S(2)}, u32[]{:S(2)}) %collective-permute-start.5) | collective-permute-done | bytes 65568 | tf_op jit(solution)/shard_map/ppermute | solution.py:16
  46.8 2.1 %collective-permute-start.12 = (bf16[256,128]{1,0:T(8,128)(2,1)S(1)}, bf16[256,128]{1,0:T(8,128)(2,1)S(1)}, u32[]{:S(2)}, u32[]{:S(2)}) collective-permute-start(bf16[256,128]{1,0:T(8,128)(2,1)S(1)} %fusion.25), channel_id=1, source_target_pairs={{0,24},{8,16},{16,8},{24,0},{1,25},{9,17},{17,9},{25,1},{2,26},{10... | collective-permute-start | bytes 196616 | tf_op jit(solution)/shard_map/ppermute | solution.py:16
  50.5 1.5 %collective-permute-done.12 = bf16[256,128]{1,0:T(8,128)(2,1)S(1)} collective-permute-done((bf16[256,128]{1,0:T(8,128)(2,1)S(1)}, bf16[256,128]{1,0:T(8,128)(2,1)S(1)}, u32[]{:S(2)}, u32[]{:S(2)}) %collective-permute-start.12) | collective-permute-done | bytes 65568 | tf_op jit(solution)/shard_map/ppermute | solution.py:16
  53.4 0.9 fusion.47
  55.3 1.1 %collective-permute-start.21 = (bf16[112,256]{1,0:T(8,128)(2,1)S(1)}, bf16[112,256]{1,0:T(8,128)(2,1)S(1)}, u32[]{:S(2)}, u32[]{:S(2)}) collective-permute-start(bf16[112,256]{1,0:T(8,128)(2,1)S(1)} %get-tuple-element.23), channel_id=1, source_target_pairs={{0,8},{8,0},{16,24},{24,16},{1,9},{9,1},{17,25},{25,17},{2,10},{10... | collective-permute-start | bytes 172040 | tf_op jit(solution)/shard_map/ppermute | solution.py:16
  56.3 1.6 %collective-permute-start.22 = (bf16[112,256]{1,0:T(8,128)(2,1)S(1)}, bf16[112,256]{1,0:T(8,128)(2,1)S(1)}, u32[]{:S(2)}, u32[]{:S(2)}) collective-permute-start(bf16[112,256]{1,0:T(8,128)(2,1)S(1)} %get-tuple-element.25), channel_id=1, source_target_pairs={{0,16},{8,24},{16,0},{24,8},{1,17},{9,25},{17,1},{25,9},{2,18},{10... | collective-permute-start | bytes 172040 | tf_op jit(solution)/shard_map/ppermute | solution.py:16
  58.8 3.7 %convolution_convert_fusion = bf16[2048,172]{0,1:T(8,128)(2,1)S(1)} fusion(bf16[2048,1024]{1,0:T(8,128)(2,1)} %copy-done.4, f32[1024,172]{0,1:T(8,128)S(1)} %fusion.48), kind=kOutput, calls=%fused_computation.1 | convolution fusion | flops 721948672 | bytes 5603328 | tf_op jit(solution)/shard_map/dot_general | solution.py:178
  63.3 1.2 %collective-permute-done.24 = f32[112,256]{1,0:T(8,128)S(1)} collective-permute-done((f32[112,256]{1,0:T(8,128)S(1)}, f32[112,256]{1,0:T(8,128)S(1)}, u32[]{:S(2)}, u32[]{:S(2)}) %collective-permute-start.24) | collective-permute-done | bytes 114720 | tf_op jit(solution)/shard_map/ppermute | solution.py:16
  64.5 1.3 %collective-permute-start.25 = (f32[112,256]{1,0:T(8,128)S(1)}, f32[112,256]{1,0:T(8,128)S(1)}, u32[]{:S(2)}, u32[]{:S(2)}) collective-permute-start(f32[112,256]{1,0:T(8,128)S(1)} %add.161), channel_id=1, source_target_pairs={{0,2},{1,3},{2,0},{3,1},{4,6},{5,7},{6,4},{7,5},{8,10},{9,11},{10,... | collective-permute-start | bytes 344072 | tf_op jit(solution)/shard_map/ppermute | solution.py:16
  65.8 3.9 %collective-permute-done.25 = f32[112,256]{1,0:T(8,128)S(1)} collective-permute-done((f32[112,256]{1,0:T(8,128)S(1)}, f32[112,256]{1,0:T(8,128)S(1)}, u32[]{:S(2)}, u32[]{:S(2)}) %collective-permute-start.25) | collective-permute-done | bytes 114720 | tf_op jit(solution)/shard_map/ppermute | solution.py:16
  69.8 1.8 %collective-permute-start.26 = (f32[112,256]{1,0:T(8,128)S(1)}, f32[112,256]{1,0:T(8,128)S(1)}, u32[]{:S(2)}, u32[]{:S(2)}) collective-permute-start(f32[112,256]{1,0:T(8,128)S(1)} %add.162), channel_id=1, source_target_pairs={{0,4},{1,5},{2,6},{3,7},{4,0},{5,1},{6,2},{7,3},{8,12},{9,13},{10,... | collective-permute-start | bytes 344072 | tf_op jit(solution)/shard_map/ppermute | solution.py:16
  72.5 1.7 %collective-permute-start.15 = (bf16[256,172]{0,1:T(8,128)(2,1)S(1)}, bf16[256,172]{0,1:T(8,128)(2,1)S(1)}, u32[]{:S(2)}, u32[]{:S(2)}) collective-permute-start(bf16[256,172]{0,1:T(8,128)(2,1)S(1)} %get-tuple-element.28), channel_id=1, source_target_pairs={{0,4},{1,5},{2,6},{3,7},{4,0},{5,1},{6,2},{7,3},{8,12},{9,13},{10,... | collective-permute-start | bytes 264200 | tf_op jit(solution)/shard_map/ppermute | solution.py:16
  74.3 1.9 %collective-permute-start.16 = (bf16[256,172]{0,1:T(8,128)(2,1)S(1)}, bf16[256,172]{0,1:T(8,128)(2,1)S(1)}, u32[]{:S(2)}, u32[]{:S(2)}) collective-permute-start(bf16[256,172]{0,1:T(8,128)(2,1)S(1)} %get-tuple-element.27), channel_id=1, source_target_pairs={{0,6},{1,7},{2,4},{3,5},{4,2},{5,3},{6,0},{7,1},{8,14},{9,15},{10,... | collective-permute-start | bytes 264200 | tf_op jit(solution)/shard_map/ppermute | solution.py:16
  76.2 6.1 %collective-permute-done.26 = f32[112,256]{1,0:T(8,128)S(1)} collective-permute-done((f32[112,256]{1,0:T(8,128)S(1)}, f32[112,256]{1,0:T(8,128)S(1)}, u32[]{:S(2)}, u32[]{:S(2)}) %collective-permute-start.26) | collective-permute-done | bytes 114720 | tf_op jit(solution)/shard_map/ppermute | solution.py:16
  82.3 1.4 %collective-permute-start.27 = (f32[112,256]{1,0:T(8,128)S(1)}, f32[112,256]{1,0:T(8,128)S(1)}, u32[]{:S(2)}, u32[]{:S(2)}) collective-permute-start(f32[112,256]{1,0:T(8,128)S(1)} %add.163), channel_id=1, source_target_pairs={{0,8},{8,0},{16,24},{24,16},{1,9},{9,1},{17,25},{25,17},{2,10},{10... | collective-permute-start | bytes 344072 | tf_op jit(solution)/shard_map/ppermute | solution.py:16
  83.7 1.3 %collective-permute-start.28 = (f32[112,256]{1,0:T(8,128)S(1)}, f32[112,256]{1,0:T(8,128)S(1)}, u32[]{:S(2)}, u32[]{:S(2)}) collective-permute-start(f32[112,256]{1,0:T(8,128)S(1)} %add.163), channel_id=1, source_target_pairs={{0,16},{8,24},{16,0},{24,8},{1,17},{9,25},{17,1},{25,9},{2,18},{10... | collective-permute-start | bytes 344072 | tf_op jit(solution)/shard_map/ppermute | solution.py:16
  87.2 1.3 %collective-permute-done.28 = f32[112,256]{1,0:T(8,128)S(1)} collective-permute-done((f32[112,256]{1,0:T(8,128)S(1)}, f32[112,256]{1,0:T(8,128)S(1)}, u32[]{:S(2)}, u32[]{:S(2)}) %collective-permute-start.28) | collective-permute-done | bytes 114720 | tf_op jit(solution)/shard_map/ppermute | solution.py:16
  88.5 2.2 %collective-permute-done.29 = f32[112,256]{1,0:T(8,128)S(1)} collective-permute-done((f32[112,256]{1,0:T(8,128)S(1)}, f32[112,256]{1,0:T(8,128)S(1)}, u32[]{:S(2)}, u32[]{:S(2)}) %collective-permute-start.29) | collective-permute-done | bytes 114720 | tf_op jit(solution)/shard_map/ppermute | solution.py:16
  (110 shorter events, 20.9 us)
Async XLA Ops:
  0.6 49.4 %copy-start = (bf16[256,172]{0,1:T(8,128)(2,1)S(1)}, bf16[256,172]{0,1:T(8,128)(2,1)}, u32[]{:S(2)}) copy-start(bf16[256,172]{0,1:T(8,128)(2,1)} %param.17) | copy-start | bytes 264196
  4.1 30.5 %copy-start.6 = (bf16[256,172]{0,1:T(8,128)(2,1)S(1)}, bf16[256,172]{0,1:T(8,128)(2,1)}, u32[]{:S(2)}) copy-start(bf16[256,172]{0,1:T(8,128)(2,1)} %param.19) | copy-start | bytes 264196
  8.7 8.6 %collective-permute-start.7 = (f32[16,128]{1,0:T(8,128)S(1)}, f32[16,128]{1,0:T(8,128)S(1)}, u32[]{:S(2)}, u32[]{:S(2)}) collective-permute-start(f32[16,128]{1,0:T(8,128)S(1)} %get-tuple-element.8), channel_id=1, source_target_pairs={{0,1},{1,0},{2,3},{3,2},{4,5},{5,4},{6,7},{7,6},{8,9},{9,8},{10,11... | collective-permute-start | bytes 24584 | tf_op jit(solution)/shard_map/ppermute | solution.py:16
  8.9 25.7 %collective-permute-start.17 = (bf16[256,172]{0,1:T(8,128)(2,1)}, bf16[256,172]{0,1:T(8,128)(2,1)S(1)}, u32[]{:S(2)}, u32[]{:S(2)}) collective-permute-start(bf16[256,172]{0,1:T(8,128)(2,1)} %param.19), channel_id=1, source_target_pairs={{0,2},{1,3},{2,0},{3,1},{4,6},{5,7},{6,4},{7,5},{8,10},{9,11},{10,... | collective-permute-start | bytes 264200 | tf_op jit(solution)/shard_map/ppermute | solution.py:16
  11.8 22.8 %collective-permute-start.18 = (bf16[256,172]{0,1:T(8,128)(2,1)}, bf16[256,172]{0,1:T(8,128)(2,1)S(1)}, u32[]{:S(2)}, u32[]{:S(2)}) collective-permute-start(bf16[256,172]{0,1:T(8,128)(2,1)} %param.19), channel_id=1, source_target_pairs={{0,4},{1,5},{2,6},{3,7},{4,0},{5,1},{6,2},{7,3},{8,12},{9,13},{10,... | collective-permute-start | bytes 264200 | tf_op jit(solution)/shard_map/ppermute | solution.py:16
  14.1 11.9 %collective-permute-start = (bf16[256,128]{1,0:T(8,128)(2,1)}, bf16[256,128]{1,0:T(8,128)(2,1)S(1)}, u32[]{:S(2)}, u32[]{:S(2)}) collective-permute-start(bf16[256,128]{1,0:T(8,128)(2,1)} %param.10), channel_id=1, source_target_pairs={{0,8},{8,0},{16,24},{24,16},{1,9},{9,1},{17,25},{25,17},{2,10},{10... | collective-permute-start | bytes 196616 | tf_op jit(solution)/shard_map/ppermute | solution.py:16
  15.3 13.4 %collective-permute-start.1 = (bf16[256,128]{1,0:T(8,128)(2,1)}, bf16[256,128]{1,0:T(8,128)(2,1)S(1)}, u32[]{:S(2)}, u32[]{:S(2)}) collective-permute-start(bf16[256,128]{1,0:T(8,128)(2,1)} %param.10), channel_id=1, source_target_pairs={{0,16},{8,24},{16,0},{24,8},{1,17},{9,25},{17,1},{25,9},{2,18},{10... | collective-permute-start | bytes 196616 | tf_op jit(solution)/shard_map/ppermute | solution.py:16
  17.2 4.6 %collective-permute-start.8 = (f32[16,128]{1,0:T(8,128)S(1)}, f32[16,128]{1,0:T(8,128)S(1)}, u32[]{:S(2)}, u32[]{:S(2)}) collective-permute-start(f32[16,128]{1,0:T(8,128)S(1)} %fusion.31), channel_id=1, source_target_pairs={{0,4},{1,5},{2,6},{3,7},{4,0},{5,1},{6,2},{7,3},{8,12},{9,13},{10,... | collective-permute-start | bytes 24584 | tf_op jit(solution)/shard_map/ppermute | solution.py:16
  21.9 3.7 %collective-permute-start.9 = (f32[16,128]{1,0:T(8,128)S(1)}, f32[16,128]{1,0:T(8,128)S(1)}, u32[]{:S(2)}, u32[]{:S(2)}) collective-permute-start(f32[16,128]{1,0:T(8,128)S(1)} %add.135), channel_id=1, source_target_pairs={{0,2},{1,3},{2,0},{3,1},{4,6},{5,7},{6,4},{7,5},{8,10},{9,11},{10,... | collective-permute-start | bytes 24584 | tf_op jit(solution)/shard_map/ppermute | solution.py:16
  25.6 5.4 %collective-permute-start.2 = (bf16[256,128]{1,0:T(8,128)(2,1)}, bf16[256,128]{1,0:T(8,128)(2,1)S(1)}, u32[]{:S(2)}, u32[]{:S(2)}) collective-permute-start(bf16[256,128]{1,0:T(8,128)(2,1)} %param.10), channel_id=1, source_target_pairs={{0,24},{8,16},{16,8},{24,0},{1,25},{9,17},{17,9},{25,1},{2,26},{10... | collective-permute-start | bytes 196616 | tf_op jit(solution)/shard_map/ppermute | solution.py:16
  26.0 8.6 %collective-permute-start.19 = (bf16[256,172]{0,1:T(8,128)(2,1)}, bf16[256,172]{0,1:T(8,128)(2,1)S(1)}, u32[]{:S(2)}, u32[]{:S(2)}) collective-permute-start(bf16[256,172]{0,1:T(8,128)(2,1)} %param.19), channel_id=1, source_target_pairs={{0,6},{1,7},{2,4},{3,5},{4,2},{5,3},{6,0},{7,1},{8,14},{9,15},{10,... | collective-permute-start | bytes 264200 | tf_op jit(solution)/shard_map/ppermute | solution.py:16
  34.5 1.6 %collective-permute-start.3 = (bf16[1024,128]{1,0:T(8,128)(2,1)S(1)}, bf16[1024,128]{1,0:T(8,128)(2,1)S(1)}, u32[]{:S(2)}, u32[]{:S(2)}) collective-permute-start(bf16[1024,128]{1,0:T(8,128)(2,1)S(1)} %slice.108), channel_id=1, source_target_pairs={{0,1},{1,0},{2,3},{3,2},{4,5},{5,4},{6,7},{7,6},{8,9},{9,8},{10,11... | collective-permute-start | bytes 786440 | tf_op jit(solution)/shard_map/ppermute | solution.py:16
  34.6 14.3 %collective-permute-start.20 = (bf16[1024,172]{0,1:T(8,128)(2,1)S(1)}, bf16[1024,172]{0,1:T(8,128)(2,1)S(1)}, u32[]{:S(2)}, u32[]{:S(2)}) collective-permute-start(bf16[1024,172]{0,1:T(8,128)(2,1)S(1)} %pad_maximum_fusion.1), channel_id=1, source_target_pairs={{0,1},{1,0},{2,3},{3,2},{4,5},{5,4},{6,7},{7,6},{8,9},{9,8},{10,11... | collective-permute-start | bytes 1056776 | tf_op jit(solution)/shard_map/ppermute | solution.py:16
  36.2 5.0 %collective-permute-start.4 = (bf16[256,128]{1,0:T(8,128)(2,1)S(1)}, bf16[256,128]{1,0:T(8,128)(2,1)S(1)}, u32[]{:S(2)}, u32[]{:S(2)}) collective-permute-start(bf16[256,128]{1,0:T(8,128)(2,1)S(1)} %get-tuple-element.29), channel_id=1, source_target_pairs={{0,2},{1,3},{2,0},{3,1},{4,6},{5,7},{6,4},{7,5},{8,10},{9,11},{10,... | collective-permute-start | bytes 196616 | tf_op jit(solution)/shard_map/ppermute | solution.py:16
  37.0 8.3 %collective-permute-start.5 = (bf16[256,128]{1,0:T(8,128)(2,1)S(1)}, bf16[256,128]{1,0:T(8,128)(2,1)S(1)}, u32[]{:S(2)}, u32[]{:S(2)}) collective-permute-start(bf16[256,128]{1,0:T(8,128)(2,1)S(1)} %get-tuple-element.31), channel_id=1, source_target_pairs={{0,4},{1,5},{2,6},{3,7},{4,0},{5,1},{6,2},{7,3},{8,12},{9,13},{10,... | collective-permute-start | bytes 196616 | tf_op jit(solution)/shard_map/ppermute | solution.py:16
  37.3 7.9 %collective-permute-start.6 = (bf16[256,128]{1,0:T(8,128)(2,1)S(1)}, bf16[256,128]{1,0:T(8,128)(2,1)S(1)}, u32[]{:S(2)}, u32[]{:S(2)}) collective-permute-start(bf16[256,128]{1,0:T(8,128)(2,1)S(1)} %get-tuple-element.30), channel_id=1, source_target_pairs={{0,6},{1,7},{2,4},{3,5},{4,2},{5,3},{6,0},{7,1},{8,14},{9,15},{10,... | collective-permute-start | bytes 196616 | tf_op jit(solution)/shard_map/ppermute | solution.py:16
  45.3 5.1 %collective-permute-start.10 = (bf16[256,128]{1,0:T(8,128)(2,1)S(1)}, bf16[256,128]{1,0:T(8,128)(2,1)S(1)}, u32[]{:S(2)}, u32[]{:S(2)}) collective-permute-start(bf16[256,128]{1,0:T(8,128)(2,1)S(1)} %fusion.25), channel_id=1, source_target_pairs={{0,8},{8,0},{16,24},{24,16},{1,9},{9,1},{17,25},{25,17},{2,10},{10... | collective-permute-start | bytes 196616 | tf_op jit(solution)/shard_map/ppermute | solution.py:16
  46.0 4.5 %collective-permute-start.11 = (bf16[256,128]{1,0:T(8,128)(2,1)S(1)}, bf16[256,128]{1,0:T(8,128)(2,1)S(1)}, u32[]{:S(2)}, u32[]{:S(2)}) collective-permute-start(bf16[256,128]{1,0:T(8,128)(2,1)S(1)} %fusion.25), channel_id=1, source_target_pairs={{0,16},{8,24},{16,0},{24,8},{1,17},{9,25},{17,1},{25,9},{2,18},{10... | collective-permute-start | bytes 196616 | tf_op jit(solution)/shard_map/ppermute | solution.py:16
  46.8 5.2 %collective-permute-start.12 = (bf16[256,128]{1,0:T(8,128)(2,1)S(1)}, bf16[256,128]{1,0:T(8,128)(2,1)S(1)}, u32[]{:S(2)}, u32[]{:S(2)}) collective-permute-start(bf16[256,128]{1,0:T(8,128)(2,1)S(1)} %fusion.25), channel_id=1, source_target_pairs={{0,24},{8,16},{16,8},{24,0},{1,25},{9,17},{17,9},{25,1},{2,26},{10... | collective-permute-start | bytes 196616 | tf_op jit(solution)/shard_map/ppermute | solution.py:16
  55.3 7.4 %collective-permute-start.21 = (bf16[112,256]{1,0:T(8,128)(2,1)S(1)}, bf16[112,256]{1,0:T(8,128)(2,1)S(1)}, u32[]{:S(2)}, u32[]{:S(2)}) collective-permute-start(bf16[112,256]{1,0:T(8,128)(2,1)S(1)} %get-tuple-element.23), channel_id=1, source_target_pairs={{0,8},{8,0},{16,24},{24,16},{1,9},{9,1},{17,25},{25,17},{2,10},{10... | collective-permute-start | bytes 172040 | tf_op jit(solution)/shard_map/ppermute | solution.py:16
  56.3 6.3 %collective-permute-start.22 = (bf16[112,256]{1,0:T(8,128)(2,1)S(1)}, bf16[112,256]{1,0:T(8,128)(2,1)S(1)}, u32[]{:S(2)}, u32[]{:S(2)}) collective-permute-start(bf16[112,256]{1,0:T(8,128)(2,1)S(1)} %get-tuple-element.25), channel_id=1, source_target_pairs={{0,16},{8,24},{16,0},{24,8},{1,17},{9,25},{17,1},{25,9},{2,18},{10... | collective-permute-start | bytes 172040 | tf_op jit(solution)/shard_map/ppermute | solution.py:16
  58.0 5.1 %collective-permute-start.23 = (bf16[112,256]{1,0:T(8,128)(2,1)S(1)}, bf16[112,256]{1,0:T(8,128)(2,1)S(1)}, u32[]{:S(2)}, u32[]{:S(2)}) collective-permute-start(bf16[112,256]{1,0:T(8,128)(2,1)S(1)} %get-tuple-element.24), channel_id=1, source_target_pairs={{0,24},{8,16},{16,8},{24,0},{1,25},{9,17},{17,9},{25,1},{2,26},{10... | collective-permute-start | bytes 172040 | tf_op jit(solution)/shard_map/ppermute | solution.py:16
  62.6 9.0 %collective-permute-start.13 = (bf16[1024,172]{0,1:T(8,128)(2,1)S(1)}, bf16[1024,172]{0,1:T(8,128)(2,1)S(1)}, u32[]{:S(2)}, u32[]{:S(2)}) collective-permute-start(bf16[1024,172]{0,1:T(8,128)(2,1)S(1)} %slice.121), channel_id=1, source_target_pairs={{0,1},{1,0},{2,3},{3,2},{4,5},{5,4},{6,7},{7,6},{8,9},{9,8},{10,11... | collective-permute-start | bytes 1056776 | tf_op jit(solution)/shard_map/ppermute | solution.py:16
  63.1 1.4 %collective-permute-start.24 = (f32[112,256]{1,0:T(8,128)S(1)}, f32[112,256]{1,0:T(8,128)S(1)}, u32[]{:S(2)}, u32[]{:S(2)}) collective-permute-start(f32[112,256]{1,0:T(8,128)S(1)} %fusion.27), channel_id=1, source_target_pairs={{0,1},{1,0},{2,3},{3,2},{4,5},{5,4},{6,7},{7,6},{8,9},{9,8},{10,11... | collective-permute-start | bytes 344072 | tf_op jit(solution)/shard_map/ppermute | solution.py:16
  64.5 5.3 %collective-permute-start.25 = (f32[112,256]{1,0:T(8,128)S(1)}, f32[112,256]{1,0:T(8,128)S(1)}, u32[]{:S(2)}, u32[]{:S(2)}) collective-permute-start(f32[112,256]{1,0:T(8,128)S(1)} %add.161), channel_id=1, source_target_pairs={{0,2},{1,3},{2,0},{3,1},{4,6},{5,7},{6,4},{7,5},{8,10},{9,11},{10,... | collective-permute-start | bytes 344072 | tf_op jit(solution)/shard_map/ppermute | solution.py:16
  69.8 12.5 %collective-permute-start.26 = (f32[112,256]{1,0:T(8,128)S(1)}, f32[112,256]{1,0:T(8,128)S(1)}, u32[]{:S(2)}, u32[]{:S(2)}) collective-permute-start(f32[112,256]{1,0:T(8,128)S(1)} %add.162), channel_id=1, source_target_pairs={{0,4},{1,5},{2,6},{3,7},{4,0},{5,1},{6,2},{7,3},{8,12},{9,13},{10,... | collective-permute-start | bytes 344072 | tf_op jit(solution)/shard_map/ppermute | solution.py:16
  71.7 13.3 %collective-permute-start.14 = (bf16[256,172]{0,1:T(8,128)(2,1)S(1)}, bf16[256,172]{0,1:T(8,128)(2,1)S(1)}, u32[]{:S(2)}, u32[]{:S(2)}) collective-permute-start(bf16[256,172]{0,1:T(8,128)(2,1)S(1)} %get-tuple-element.26), channel_id=1, source_target_pairs={{0,2},{1,3},{2,0},{3,1},{4,6},{5,7},{6,4},{7,5},{8,10},{9,11},{10,... | collective-permute-start | bytes 264200 | tf_op jit(solution)/shard_map/ppermute | solution.py:16
  72.5 13.3 %collective-permute-start.15 = (bf16[256,172]{0,1:T(8,128)(2,1)S(1)}, bf16[256,172]{0,1:T(8,128)(2,1)S(1)}, u32[]{:S(2)}, u32[]{:S(2)}) collective-permute-start(bf16[256,172]{0,1:T(8,128)(2,1)S(1)} %get-tuple-element.28), channel_id=1, source_target_pairs={{0,4},{1,5},{2,6},{3,7},{4,0},{5,1},{6,2},{7,3},{8,12},{9,13},{10,... | collective-permute-start | bytes 264200 | tf_op jit(solution)/shard_map/ppermute | solution.py:16
  74.3 11.6 %collective-permute-start.16 = (bf16[256,172]{0,1:T(8,128)(2,1)S(1)}, bf16[256,172]{0,1:T(8,128)(2,1)S(1)}, u32[]{:S(2)}, u32[]{:S(2)}) collective-permute-start(bf16[256,172]{0,1:T(8,128)(2,1)S(1)} %get-tuple-element.27), channel_id=1, source_target_pairs={{0,6},{1,7},{2,4},{3,5},{4,2},{5,3},{6,0},{7,1},{8,14},{9,15},{10,... | collective-permute-start | bytes 264200 | tf_op jit(solution)/shard_map/ppermute | solution.py:16
  82.3 4.9 %collective-permute-start.27 = (f32[112,256]{1,0:T(8,128)S(1)}, f32[112,256]{1,0:T(8,128)S(1)}, u32[]{:S(2)}, u32[]{:S(2)}) collective-permute-start(f32[112,256]{1,0:T(8,128)S(1)} %add.163), channel_id=1, source_target_pairs={{0,8},{8,0},{16,24},{24,16},{1,9},{9,1},{17,25},{25,17},{2,10},{10... | collective-permute-start | bytes 344072 | tf_op jit(solution)/shard_map/ppermute | solution.py:16
  83.7 4.8 %collective-permute-start.28 = (f32[112,256]{1,0:T(8,128)S(1)}, f32[112,256]{1,0:T(8,128)S(1)}, u32[]{:S(2)}, u32[]{:S(2)}) collective-permute-start(f32[112,256]{1,0:T(8,128)S(1)} %add.163), channel_id=1, source_target_pairs={{0,16},{8,24},{16,0},{24,8},{1,17},{9,25},{17,1},{25,9},{2,18},{10... | collective-permute-start | bytes 344072 | tf_op jit(solution)/shard_map/ppermute | solution.py:16
  85.0 5.7 %collective-permute-start.29 = (f32[112,256]{1,0:T(8,128)S(1)}, f32[112,256]{1,0:T(8,128)S(1)}, u32[]{:S(2)}, u32[]{:S(2)}) collective-permute-start(f32[112,256]{1,0:T(8,128)S(1)} %add.163), channel_id=1, source_target_pairs={{0,24},{8,16},{16,8},{24,0},{1,25},{9,17},{17,9},{25,1},{2,26},{10... | collective-permute-start | bytes 344072 | tf_op jit(solution)/shard_map/ppermute | solution.py:16
  (10 other events, 81.9 us)

commit v2 on v1

v2 whole, which is shorter than its diff:
```python
import functools

import jax
import jax.numpy as jnp
from jax import lax
from jax.experimental import pallas as pl
from jax.experimental.pallas import tpu as pltpu
from jax.sharding import PartitionSpec as P

BF16 = jnp.bfloat16
F32 = jnp.float32
LANES = 128
SMEM = pl.BlockSpec(memory_space=pltpu.SMEM)
VMEM = pl.BlockSpec(memory_space=pltpu.VMEM)
ANY = pl.BlockSpec(memory_space=pl.ANY)


def exchange(value, axis, mask):
    count = lax.axis_size(axis)
    return lax.ppermute(value, axis, [(i, i ^ mask) for i in range(count)])


def call(kernel, name, outs, in_specs, args, scratch=(), flops=0):
    size = sum(a.size * a.dtype.itemsize for a in args)
    size += sum(o.size * o.dtype.itemsize for o in outs)
    grant = size + (12 << 20)
    return pl.pallas_call(
        kernel,
        out_shape=tuple(outs),
        in_specs=in_specs,
        out_specs=tuple(VMEM for _ in outs),
        scratch_shapes=scratch,
        compiler_params=pltpu.CompilerParams(vmem_limit_bytes=min(grant, 60 << 20)),
        cost_estimate=pl.CostEstimate(flops=flops, bytes_accessed=size, transcendentals=0),
        name=name,
    )(*args)


def shaped(shape, dtype):
    return jax.ShapeDtypeStruct(shape, dtype)


def product(left, right, contract=((1,), (0,))):
    return lax.dot_general(left, right, (contract, ((), ())), preferred_element_type=F32)


def split(value):
    high = value.astype(BF16)
    return high, (value - high.astype(F32)).astype(BF16)


def dense_kernel(own, row_ref, col_ref, live_ref, place_ref, tiles_ref, after_ref, dense_ref, degree_ref):
    block = tiles_ref.shape[1]
    rows, columns = dense_ref.shape
    half = rows // (block * own * 2)
    r, c = place_ref[0], place_ref[1]
    dense_ref[...] = jnp.zeros_like(dense_ref)

    @pl.loop(0, live_ref[0])
    def _(slot):
        k = row_ref[slot]
        j = col_ref[slot]
        p = (k // own) ^ c
        at_row = ((p & 1) * half + (p >> 1)) * own + k % own
        at_col = ((j // own) ^ r) * own + j % own
        dense_ref[
            pl.ds(pl.multiple_of(at_row * block, block), block),
            pl.ds(pl.multiple_of(at_col * block, block), block),
        ] = tiles_ref[slot]

    ones = jnp.ones((8, columns), BF16)
    for start in range(0, rows, 2 * block):
        sums = product(ones, dense_ref[pl.ds(start, 2 * block), :], ((1,), (1,)))
        for part in range(2):
            degree_ref[pl.ds(start // block + part, 1), :] = sums[:1, part * block : (part + 1) * block]


def first_kernel(spans, dense_ref, *refs):
    pieces, (send_ref, keep_ref, held) = refs[:spans], refs[spans:]
    nodes = pieces[0].shape[0]
    for s in range(spans):
        held[pl.ds(s * nodes, nodes), :] = pieces[s][...]
    half = keep_ref.shape[0] // nodes

    @pl.loop(0, half)
    def _(s):
        at = pl.multiple_of(s * nodes, nodes)
        send_ref[pl.ds(at, nodes), :] = product(
            dense_ref[pl.ds(pl.multiple_of((half + s) * nodes, nodes), nodes), :], held[...]
        ).astype(BF16)
        keep_ref[pl.ds(at, nodes), :] = product(dense_ref[pl.ds(at, nodes), :], held[...])


def back_kernel(spans, dense_ref, near_ref, other_ref, degree_ref, *refs):
    own_ref, wide_ref = refs[:2]
    sends, turned = refs[2 : 1 + spans], refs[-1]
    classes = own_ref.shape[0]
    rows = dense_ref.shape[0]
    nodes = own_ref.shape[1]
    block = LANES
    packed = nodes + block
    half = rows // nodes // 2
    blocks = degree_ref.shape[0]
    tail = other_ref[pl.ds(half * packed, 2 * blocks), :].astype(F32)
    far = tail[:blocks] + tail[blocks:]
    far = jnp.concatenate([far[blocks // 2 :], far[: blocks // 2]], axis=0)
    degree = (1.0 + (degree_ref[...] + far)).T
    lane = lax.broadcasted_iota(jnp.int32, (block, block), 1)
    for q in range(2 * half):
        source = near_ref if q < half else other_ref
        base = (q % half) * packed
        even = jnp.broadcast_to(degree[:, 2 * q : 2 * q + 1], (block, block))
        odd = jnp.broadcast_to(degree[:, 2 * q + 1 : 2 * q + 2], (block, block))
        if q == 0:
            wide_ref[:block, :] = even
            wide_ref[block:, :] = odd
        rest = source[pl.ds(base + nodes, block), :].astype(F32)
        rolled = pltpu.roll(rest, block // 2, 1)
        low = lane < block // 2
        parts = (
            (source[pl.ds(base, block), :].astype(F32) / even, jnp.where(low, rest / even, 0.0)),
            (source[pl.ds(base + block, block), :].astype(F32) / odd, jnp.where(low, rolled / odd, 0.0)),
        )
        for b, (first, second) in enumerate(parts):
            at = pl.ds(q * nodes + b * block, block)
            turned[:block, at] = first.T.astype(BF16)
            turned[block:, at] = second.T[: classes - block].astype(BF16)
    for s in range(spans):
        part = product(turned[...], dense_ref[:, s * nodes : (s + 1) * nodes])
        if s == 0:
            own_ref[...] = part + turned[:, :nodes].astype(F32)
        else:
            sends[s - 1][...] = part.astype(BF16)


def gelu_parts(z):
    scale = 0.7978845608028654
    t = jnp.tanh(scale * (z + 0.044715 * (z * z * z)))
    value = 0.5 * z * (1.0 + t)
    slope = 0.5 * (1.0 + t) + 0.5 * z * (1.0 - t * t) * (scale * (1.0 + 3.0 * 0.044715 * (z * z)))
    return value, slope


def grad_kernel(half, spans, place_ref, near_ref, *refs):
    got, refs = refs[: half - 1], refs[half - 1 :]
    features_ref, wide_ref, own_ref, refs = refs[0], refs[1], refs[2], refs[3:]
    back, refs = refs[: spans - 1], refs[spans - 1 :]
    w1_ref, b1_ref, w2_ref, g_ref, refs = refs[0], refs[1], refs[2], refs[3], refs[4:]
    agg_ref, mine_ref, refs = refs[0], refs[1], refs[2:]
    sends, total = refs[: spans - 1], refs[-1]
    nodes = features_ref.shape[0]
    fin, hidden = w1_ref.shape
    rank = place_ref[0]
    acc = near_ref[...]
    for ref in got:
        acc = acc + ref[...].astype(F32)
    agg = ((acc + features_ref[...].astype(F32)) / wide_ref[...]).astype(BF16)
    agg_ref[...] = agg
    z = product(agg, w1_ref[...]) + b1_ref[...]
    value, slope = gelu_parts(z)
    h = value.astype(BF16)
    q = own_ref[...]
    for ref in back:
        q = q + ref[...].astype(F32)
    classes = q.shape[0]
    q = jnp.concatenate([q, jnp.zeros((2 * LANES - classes, nodes), F32)], axis=0).T
    q_high, q_low = split(q)
    w2 = w2_ref[...]
    d_first = (product(q_high, w2, ((1,), (1,))) + product(q_low, w2, ((1,), (1,)))) * slope
    turned = h.astype(F32).T.astype(BF16)
    grad_w2 = product(turned, q_high) + product(turned, q_low)
    grad_w1 = product(agg.astype(F32).T.astype(BF16), d_first.astype(BF16))
    grad_b1 = jnp.sum(d_first, axis=0, keepdims=True)
    cots = g_ref[...].astype(F32)
    left = jnp.sum(cots[:nodes], axis=0, keepdims=True)
    right = jnp.sum(cots[nodes:], axis=0, keepdims=True)
    right = right + jnp.concatenate([right[:, LANES // 2 :], right[:, : LANES // 2]], axis=1)
    a, b = fin // spans, hidden // spans
    size = total.shape[1] // 2
    total[...] = jnp.zeros_like(total)
    for t in range(spans):
        for lanes in range(2):
            at = slice(lanes * LANES, (lanes + 1) * LANES)
            total[t, lanes * size : lanes * size + a, :] = grad_w1[t * a : (t + 1) * a, at]
            total[t, lanes * size + a : lanes * size + a + b, :] = grad_w2[t * b : (t + 1) * b, at]
    total[0, a + b : a + b + 1, :] = grad_b1[:, :LANES]
    total[0, a + b + 1 : a + b + 2, :] = left
    total[0, size + a + b : size + a + b + 1, :] = grad_b1[:, LANES:]
    total[0, size + a + b + 1 : size + a + b + 2, :] = right
    mine_ref[...] = total[rank]
    for s in range(1, spans):
        sends[s - 1][:nodes, :] = agg
        sends[s - 1][nodes:, :] = total[rank ^ s].astype(BF16)


def second_kernel(spans, dense_ref, agg_ref, mine_ref, *refs):
    got, refs = refs[: spans - 1], refs[spans - 1 :]
    w1_ref, b1_ref, w2_ref, send_ref, keep_ref, even_ref, odd_ref = refs
    nodes = agg_ref.shape[0]
    block = LANES
    packed = nodes + block
    half = dense_ref.shape[0] // nodes // 2
    mine = mine_ref[...]
    for s in range(spans):
        piece = agg_ref[...] if s == 0 else got[s - 1][:nodes, :]
        if s > 0:
            mine = mine + got[s - 1][nodes:, :].astype(F32)
        value, _ = gelu_parts(product(piece, w1_ref[...]) + b1_ref[...])
        hidden = product(value.astype(BF16), w2_ref[...])
        at = pl.ds(s * nodes, nodes)
        rolled = pltpu.roll(hidden[:, block:], block // 2, 1)
        even_ref[at, :] = hidden.astype(BF16)
        odd_ref[at, :block] = hidden[:, :block].astype(BF16)
        odd_ref[at, block:] = rolled.astype(BF16)
        if s == 0:
            first = (hidden[:, :block], hidden[:block, block:] + rolled[block:])
    rounded = mine.astype(BF16)
    send_ref[half * packed :, :] = rounded
    keep_ref[half * packed :, :] = rounded.astype(F32)

    def rows_of(place):
        at = pl.multiple_of(place * nodes, nodes)
        even = product(dense_ref[pl.ds(at, block), :], even_ref[...])
        odd = product(dense_ref[pl.ds(pl.multiple_of(at + block, block), block), :], odd_ref[...])
        return even, odd

    @pl.loop(0, half)
    def _(s):
        at = pl.multiple_of(s * packed, block)
        even, odd = rows_of(half + s)
        send_ref[pl.ds(at, block), :] = even[:, :block].astype(BF16)
        send_ref[pl.ds(at + block, block), :] = odd[:, :block].astype(BF16)
        send_ref[pl.ds(at + 2 * block, block), :] = (even[:, block:] + odd[:, block:]).astype(BF16)
        even, odd = rows_of(s)
        keep_ref[pl.ds(at, block), :] = even[:, :block]
        keep_ref[pl.ds(at + block, block), :] = odd[:, :block]
        keep_ref[pl.ds(at + 2 * block, block), :] = even[:, block:] + odd[:, block:]

    keep_ref[:nodes, :] += first[0]
    keep_ref[nodes:packed, :] += first[1]


def last_kernel(spans, place_ref, *refs):
    got, (w1_ref, b1_ref, w2_ref, b2_ref) = refs[:spans], refs[spans:]
    fin, hidden = w1_ref.shape
    classes = w2_ref.shape[1]
    a, b = fin // spans, hidden // spans
    size = got[0].shape[0] // 2
    for s in range(spans):
        t = place_ref[0] ^ s
        share = got[s][...].astype(F32)
        left, right = share[:size], share[size:]
        at = pl.ds(pl.multiple_of(t * a, a), a)
        w1_ref[at, :LANES] = left[:a]
        w1_ref[at, LANES:] = right[:a]
        at = pl.ds(pl.multiple_of(t * b, b), b)
        w2_ref[at, :LANES] = left[a : a + b]
        w2_ref[at, LANES:] = right[a : a + b, : classes - LANES]

        @pl.when(t == 0)
        def _():
            b1_ref[:, :LANES] = left[a + b : a + b + 1]
            b1_ref[:, LANES:] = right[a + b : a + b + 1]
            b2_ref[:, :LANES] = left[a + b + 1 : a + b + 2]
            b2_ref[:, LANES:] = right[a + b + 1 : a + b + 2, : classes - LANES]


def pack(value):
    block = LANES
    room = ((0, 0), (0, block // 2 - (value.shape[1] - block)))
    rest = jnp.pad(value[:, block:], room)
    return jnp.concatenate(
        [value[:, :block], jnp.concatenate([rest[:block], rest[block:]], axis=1)], axis=0
    )


def tree_sum(values):
    while len(values) > 1:
        values = [a + b for a, b in zip(values[::2], values[1::2])]
    return values[0]


def swap_pairs(value, parts):
    pairs = value.reshape((parts, 2, -1) + value.shape[1:])
    return jnp.concatenate([pairs[:, 1:], pairs[:, :1]], axis=1).reshape(value.shape)


def local(
    features,
    tiles,
    tile_row,
    tile_col,
    tile_live,
    w_first,
    b_first,
    w_second,
    b_second,
    grad_logits,
):
    row_count = lax.axis_size("row")
    col_count = lax.axis_size("col")
    half = col_count // 2
    nodes, fin = features.shape
    block = tiles.shape[-1]
    own = nodes // block
    hidden = w_first.shape[1]
    classes = w_second.shape[1]
    rows, columns = col_count * nodes, row_count * nodes
    packed = nodes + block
    place = jnp.stack([lax.axis_index("row"), lax.axis_index("col")]).astype(jnp.int32)
    bias = b_first[None, :]
    w2_wide = jnp.pad(w_second, ((0, 0), (0, 2 * LANES - classes)))

    inputs = [features] + [exchange(features, "row", s) for s in range(1, row_count)]
    g_own = pack(grad_logits)
    near_g = jnp.concatenate(
        [g_own] + [exchange(g_own, "col", 2 * s) for s in range(1, half)], axis=0
    )
    dense, degree = call(
        functools.partial(dense_kernel, own),
        "dense_adjacency",
        [shaped((rows, columns), BF16), shaped((rows // block, block), F32)],
        [SMEM, SMEM, SMEM, SMEM, VMEM, ANY],
        [tile_row[0, 0], tile_col[0, 0], tile_live[0], place, tiles[0, 0], inputs[1]],
        flops=16 * rows * columns,
    )
    mask, parts = half, 2
    while mask > 1:
        degree = degree + swap_pairs(exchange(degree, "col", mask), parts)
        mask, parts = mask // 2, parts * 2
    other_g = exchange(jnp.concatenate((near_g,) + split(degree), axis=0), "col", 1)

    send, keep = call(
        functools.partial(first_kernel, row_count),
        "first_product",
        [shaped((rows // 2, fin), BF16), shaped((rows // 2, fin), F32)],
        [VMEM] * (1 + row_count),
        [dense] + inputs,
        scratch=[pltpu.VMEM((columns, fin), BF16)],
        flops=2 * rows * columns * fin,
    )
    near = keep + exchange(send, "col", 1).astype(F32)
    sent = near.astype(BF16)
    got = [exchange(sent[s * nodes : (s + 1) * nodes], "col", 2 * s) for s in range(1, half)]

    tall = -(-classes // 16) * 16
    back = call(
        functools.partial(back_kernel, row_count),
        "back_product",
        [shaped((tall, nodes), F32), shaped((nodes, LANES), F32)]
        + [shaped((tall, nodes), BF16)] * (row_count - 1),
        [VMEM] * 4,
        [dense, near_g, other_g, degree],
        scratch=[pltpu.VMEM((tall, rows), BF16)],
        flops=2 * rows * columns * tall,
    )
    q_own, wide = back[:2]
    q_got = [exchange(back[1 + s], "row", s) for s in range(1, row_count)]

    size = 2 * (fin // row_count + hidden // row_count + 16)
    out = call(
        functools.partial(grad_kernel, half, row_count),
        "gradients",
        [shaped((nodes, fin), BF16), shaped((size, LANES), F32)]
        + [shaped((nodes + size, LANES), BF16)] * (row_count - 1),
        [SMEM] + [VMEM] * (half + 3 + row_count - 1 + 4),
        [place, near[:nodes]] + got + [features, wide, q_own] + q_got + [w_first, bias, w2_wide, g_own],
        scratch=[pltpu.VMEM((row_count, size, LANES), F32)],
        flops=10 * nodes * hidden * LANES,
    )
    agg, mine = out[:2]
    rounds = [exchange(out[1 + s], "row", s) for s in range(1, row_count)]

    send, keep = call(
        functools.partial(second_kernel, row_count),
        "second_product",
        [shaped((half * packed + size, LANES), BF16), shaped((half * packed + size, LANES), F32)],
        [VMEM] * (3 + row_count - 1 + 3),
        [dense, agg, mine] + rounds + [w_first, bias, w2_wide],
        scratch=[pltpu.VMEM((columns, 2 * LANES), BF16)] * 2,
        flops=2 * rows * columns * hidden,
    )
    near = keep + exchange(send, "col", 1).astype(F32)
    sent = near.astype(BF16)
    tail = sent[half * packed :]
    got = [
        exchange(jnp.concatenate([sent[s * packed : (s + 1) * packed], tail], axis=0), "col", 2 * s)
        for s in range(1, half)
    ]
    shares = tree_sum([tail.astype(F32)] + [value[packed:].astype(F32) for value in got]).astype(BF16)
    shares = [shares] + [exchange(shares, "row", s) for s in range(1, row_count)]
    total = near[:packed]
    for value in got:
        total = total + value[:packed].astype(F32)
    rest = total[nodes:]
    cut = classes - block
    rest = jnp.concatenate([rest[:, :cut], rest[:, block // 2 : block // 2 + cut]], axis=0)
    logits = jnp.concatenate([total[:nodes], rest], axis=1)
    logits = (logits / wide[:, :1] + b_second).astype(BF16)
    grad_w1, grad_b1, grad_w2, grad_b2 = call(
        functools.partial(last_kernel, row_count),
        "place_gradients",
        [shaped((fin, hidden), F32), shaped((1, hidden), F32), shaped((hidden, classes), F32), shaped((1, classes), F32)],
        [SMEM] + [VMEM] * row_count,
        [place] + shares,
    )
    return logits, grad_w1, grad_b1[0], grad_w2, grad_b2[0]


def solution(mesh):
    return jax.shard_map(
        local,
        mesh=mesh,
        in_specs=(
            P(("row", "col"), None),
            P("row", "col", None, None, None),
            P("row", "col", None),
            P("row", "col", None),
            P("row", "col"),
            P(),
            P(),
            P(),
            P(),
            P(("row", "col"), None),
        ),
        out_specs=(P(("row", "col"), None), P(), P(), P(), P()),
        check_vma=False,
    )
```

time: 94 us -> 86.6 us (0.921)
  matrix products: 11.1 us -> 0 us
  Pallas kernels: 2.55 us -> 10.4 us
  starting transfers between devices: 36.4 us -> 30.5 us
  waiting for transfers between devices: 30 us -> 33.4 us
  other arithmetic: 2.47 us -> 0.72 us
    dot_general x10 -> x0, matrix products: 11.1 us -> none  [the longest x1 3.73 us: local(): jnp.dot(dense, projected.astype(BF16), preferred_element_type=F32)]
    pallas_call x1 -> x6, Pallas kernels: 2.55 us -> 10.4 us  [call(): pl.pallas_call(kernel, out_shape=tuple(outs), in_specs=in_specs, out_spec...]
    ppermute x30 -> x26, starting transfers between devices: 36.4 us -> 30.5 us  [exchange(): return lax.ppermute(value, axis, [(i, i ^ mask) for i in range(count)])]
    ppermute x30 -> x26, waiting for transfers between devices: 30 us -> 33.4 us  [exchange(): return lax.ppermute(value, axis, [(i, i ^ mask) for i in range(count)])]
    unnamed x29 -> x31, local copies, waits for them, and re-layouts: 6.44 us -> 7.75 us
    reduce_sum x1 -> x0, other arithmetic: 1 us -> none  [local(): grad_b2 = jnp.sum(grad_logits.astype(F32), axis=0)]
  transfers between devices with their start and end apart: 30 -> 26, of which waited for: 14 -> 14; matrix products, arithmetic and copies ran while one was open for 13% -> 4% of each run, Pallas kernels for 0% -> 6%
where the time goes in v2:
time: 86.6 us; the launch traced here: 86.3 us
  waiting for transfers between devices  33.4 us (39%)
  starting transfers between devices  30.5 us (35%)
  Pallas kernels  10.4 us (12%)
  local copies, waits for them, and re-layouts  9.63 us (11%)
  between operations  1.62 us (2%)
    ppermute x26, waiting for transfers between devices, exchange(): return lax.ppermute(value, axis, [(i, i ^ mask) for i in range(count)])  33.4 us
    ppermute x26, starting transfers between devices, exchange(): return lax.ppermute(value, axis, [(i, i ^ mask) for i in range(count)])  30.5 us
    pallas_call x6, Pallas kernels, call(): pl.pallas_call(kernel, out_shape=tuple(outs), in_specs=in_specs, out_spec...  10.4 us
    unnamed x31, local copies, waits for them, and re-layouts  7.75 us
  transfers between devices with their start and end apart: 26, of which 14 were waited for; matrix products, arithmetic and copies ran while one was open for 4% of the time, Pallas kernels for 6%

profile of v2, /device:TPU:0, one launch (start us, length us, event | category | flops | bytes accessed | tf_op | source)
XLA Modules:
  0.0 86.3 jit_solution(16440731756573784204)
XLA Ops:
  0.6 3.0 %collective-permute-start = (bf16[256,128]{1,0:T(8,128)(2,1)}, bf16[256,128]{1,0:T(8,128)(2,1)S(1)}, u32[]{:S(2)}, u32[]{:S(2)}) collective-permute-start(bf16[256,128]{1,0:T(8,128)(2,1)} %refs_3_.2), channel_id=1, source_target_pairs={{0,8},{8,0},{16,24},{24,16},{1,9},{9,1},{17,25},{25,17},{2,10},{10... | collective-permute-start | bytes 196616 | tf_op jit(solution)/shard_map/ppermute | solution.py:20
  3.6 1.5 %collective-permute-start.1 = (bf16[256,128]{1,0:T(8,128)(2,1)}, bf16[256,128]{1,0:T(8,128)(2,1)S(1)}, u32[]{:S(2)}, u32[]{:S(2)}) collective-permute-start(bf16[256,128]{1,0:T(8,128)(2,1)} %refs_3_.2), channel_id=1, source_target_pairs={{0,16},{8,24},{16,0},{24,8},{1,17},{9,25},{17,1},{25,9},{2,18},{10... | collective-permute-start | bytes 196616 | tf_op jit(solution)/shard_map/ppermute | solution.py:20
  7.1 2.1 %collective-permute-start.7 = (bf16[384,128]{1,0:T(8,128)(2,1)S(1)}, bf16[384,128]{1,0:T(8,128)(2,1)S(1)}, u32[]{:S(2)}, u32[]{:S(2)}) collective-permute-start(bf16[384,128]{1,0:T(8,128)(2,1)S(1)} %maximum_maximum_fusion.refs_12_), channel_id=1, source_target_pairs={{0,2},{1,3},{2,0},{3,1},{4,6},{5,7},{6,4},{7,5},{8,10},{9,11},{10,... | collective-permute-start | bytes 294920 | tf_op jit(solution)/shard_map/ppermute | solution.py:20
  9.2 2.6 %collective-permute-start.8 = (bf16[384,128]{1,0:T(8,128)(2,1)S(1)}, bf16[384,128]{1,0:T(8,128)(2,1)S(1)}, u32[]{:S(2)}, u32[]{:S(2)}) collective-permute-start(bf16[384,128]{1,0:T(8,128)(2,1)S(1)} %maximum_maximum_fusion.refs_12_), channel_id=1, source_target_pairs={{0,4},{1,5},{2,6},{3,7},{4,0},{5,1},{6,2},{7,3},{8,12},{9,13},{10,... | collective-permute-start | bytes 294920 | tf_op jit(solution)/shard_map/ppermute | solution.py:20
  12.6 1.4 %copy-done.2 = bf16[1,1,48,128,128]{4,3,2,1,0:T(8,128)(2,1)S(1)} copy-done((bf16[1,1,48,128,128]{4,3,2,1,0:T(8,128)(2,1)S(1)}, bf16[1,1,48,128,128]{4,3,2,1,0:T(8,128)(2,1)}, u32[]{:S(2)}) %copy-start.2) | copy-done | bytes 1572888
  15.3 2.1 %dense_adjacency.1 = (bf16[2048,1024]{1,0:T(8,128)(2,1)S(1)}, f32[16,128]{1,0:T(8,128)S(1)}) custom-call(s32[48]{0:T(128)S(1)} %bitcast.17, s32[48]{0:T(128)S(1)} %bitcast.18, s32[1]{0:T(128)} %bitcast.13.live_ref, s32[2]{0:T(128)S(1)} %pad_add_fusion.place_ref, bf16[48,128,128]{2,1,0:T(8,128)(2,1)S(1)} %bitcast.14, ...), custom_call_target="tpu_custom_call" | custom-call | flops 33554432 | bytes 5841292 | tf_op jit(solution)/shard_map/dense_adjacency/pallas_call | solution.py:27
  18.0 4.0 %collective-permute-done.10 = f32[16,128]{1,0:T(8,128)S(1)} collective-permute-done((f32[16,128]{1,0:T(8,128)S(1)}, f32[16,128]{1,0:T(8,128)S(1)}, u32[]{:S(2)}, u32[]{:S(2)}) %collective-permute-start.10) | collective-permute-done | bytes 8224 | tf_op jit(solution)/shard_map/ppermute | solution.py:20
  24.4 1.7 %first_product.1 = (bf16[1024,128]{1,0:T(8,128)(2,1)S(1)}, f32[1024,128]{1,0:T(8,128)S(1)}) custom-call(bf16[2048,1024]{1,0:T(8,128)(2,1)S(1)} %get-tuple-element.25.dense_ref, bf16[256,128]{1,0:T(8,128)(2,1)S(1)} %copy-done.3, bf16[256,128]{1,0:T(8,128)(2,1)S(1)} %collective-permute-done.after_ref.refs_1_, ...), custom_call_target="tpu_custom_call" | custom-call | flops 536870912 | bytes 5242880 | tf_op jit(solution)/shard_map/first_product/pallas_call | solution.py:27
  26.6 1.9 %collective-permute-done.9 = bf16[384,128]{1,0:T(8,128)(2,1)S(1)} collective-permute-done((bf16[384,128]{1,0:T(8,128)(2,1)S(1)}, bf16[384,128]{1,0:T(8,128)(2,1)S(1)}, u32[]{:S(2)}, u32[]{:S(2)}) %collective-permute-start.9) | collective-permute-done | bytes 98336 | tf_op jit(solution)/shard_map/ppermute | solution.py:20
  29.4 1.0 %collective-permute-done.12.other_ref = bf16[1568,128]{1,0:T(8,128)(2,1)S(1)} collective-permute-done((bf16[1568,128]{1,0:T(8,128)(2,1)S(1)}, bf16[1568,128]{1,0:T(8,128)(2,1)S(1)}, u32[]{:S(2)}, u32[]{:S(2)}) %collective-permute-start.12) | collective-permute-done | bytes 401440 | tf_op jit(solution)/shard_map/ppermute | solution.py:20
  30.4 1.6 %back_product.1 = (f32[176,256]{1,0:T(8,128)S(1)}, f32[256,128]{1,0:T(8,128)S(1)}, bf16[176,256]{1,0:T(8,128)(2,1)S(1)}, bf16[176,256]{1,0:T(8,128)(2,1)S(1)}, bf16[176,256]{1,0:T(8,128)(2,1)S(1)}) custom-call(bf16[2048,1024]{1,0:T(8,128)(2,1)S(1)} %get-tuple-element.25.dense_ref, bf16[1536,128]{1,0:T(8,128)(2,1)S(1)} %get-tuple-element.79.near_ref, ...), custom_call_target="tpu_custom_call" | custom-call | flops 738197504 | bytes 5578752 | tf_op jit(solution)/shard_map/back_product/pallas_call | solution.py:27
  32.0 2.4 %collective-permute-start.13 = (bf16[176,256]{1,0:T(8,128)(2,1)S(1)}, bf16[176,256]{1,0:T(8,128)(2,1)S(1)}, u32[]{:S(2)}, u32[]{:S(2)}) collective-permute-start(bf16[176,256]{1,0:T(8,128)(2,1)S(1)} %get-tuple-element.31), channel_id=1, source_target_pairs={{0,8},{8,0},{16,24},{24,16},{1,9},{9,1},{17,25},{25,17},{2,10},{10... | collective-permute-start | bytes 270344 | tf_op jit(solution)/shard_map/ppermute | solution.py:20
  36.0 1.0 %collective-permute-start.5 = (bf16[256,128]{1,0:T(8,128)(2,1)S(1)}, bf16[256,128]{1,0:T(8,128)(2,1)S(1)}, u32[]{:S(2)}, u32[]{:S(2)}) collective-permute-start(bf16[256,128]{1,0:T(8,128)(2,1)S(1)} %get-tuple-element.74), channel_id=1, source_target_pairs={{0,4},{1,5},{2,6},{3,7},{4,0},{5,1},{6,2},{7,3},{8,12},{9,13},{10,... | collective-permute-start | bytes 196616 | tf_op jit(solution)/shard_map/ppermute | solution.py:20
  37.0 1.8 %collective-permute-start.6 = (bf16[256,128]{1,0:T(8,128)(2,1)S(1)}, bf16[256,128]{1,0:T(8,128)(2,1)S(1)}, u32[]{:S(2)}, u32[]{:S(2)}) collective-permute-start(bf16[256,128]{1,0:T(8,128)(2,1)S(1)} %get-tuple-element.73), channel_id=1, source_target_pairs={{0,6},{1,7},{2,4},{3,5},{4,2},{5,3},{6,0},{7,1},{8,14},{9,15},{10,... | collective-permute-start | bytes 196616 | tf_op jit(solution)/shard_map/ppermute | solution.py:20
  39.0 5.0 %collective-permute-done.5.refs_1_ = bf16[256,128]{1,0:T(8,128)(2,1)S(1)} collective-permute-done((bf16[256,128]{1,0:T(8,128)(2,1)S(1)}, bf16[256,128]{1,0:T(8,128)(2,1)S(1)}, u32[]{:S(2)}, u32[]{:S(2)}) %collective-permute-start.5) | collective-permute-done | bytes 65568 | tf_op jit(solution)/shard_map/ppermute | solution.py:20
  44.0 1.2 %gradients.1 = (bf16[256,128]{1,0:T(8,128)(2,1)S(1)}, f32[224,128]{1,0:T(8,128)S(1)}, bf16[480,128]{1,0:T(8,128)(2,1)S(1)}, bf16[480,128]{1,0:T(8,128)(2,1)S(1)}, bf16[480,128]{1,0:T(8,128)(2,1)S(1)}) custom-call(s32[2]{0:T(128)S(1)} %pad_add_fusion.place_ref, f32[256,128]{1,0:T(8,128)S(1)} %slice.109.near_ref, ...), custom_call_target="tpu_custom_call" | custom-call | flops 83886080 | bytes 1819656 | tf_op jit(solution)/shard_map/gradients/pallas_call | solution.py:27
  45.2 1.7 %collective-permute-start.16 = (bf16[480,128]{1,0:T(8,128)(2,1)S(1)}, bf16[480,128]{1,0:T(8,128)(2,1)S(1)}, u32[]{:S(2)}, u32[]{:S(2)}) collective-permute-start(bf16[480,128]{1,0:T(8,128)(2,1)S(1)} %get-tuple-element.36), channel_id=1, source_target_pairs={{0,8},{8,0},{16,24},{24,16},{1,9},{9,1},{17,25},{25,17},{2,10},{10... | collective-permute-start | bytes 368648 | tf_op jit(solution)/shard_map/ppermute | solution.py:20
  47.5 1.2 %collective-permute-start.18 = (bf16[480,128]{1,0:T(8,128)(2,1)S(1)}, bf16[480,128]{1,0:T(8,128)(2,1)S(1)}, u32[]{:S(2)}, u32[]{:S(2)}) collective-permute-start(bf16[480,128]{1,0:T(8,128)(2,1)S(1)} %get-tuple-element.38), channel_id=1, source_target_pairs={{0,24},{8,16},{16,8},{24,0},{1,25},{9,17},{17,9},{25,1},{2,26},{10... | collective-permute-start | bytes 368648 | tf_op jit(solution)/shard_map/ppermute | solution.py:20
  48.7 2.3 %collective-permute-done.16.refs_0_ = bf16[480,128]{1,0:T(8,128)(2,1)S(1)} collective-permute-done((bf16[480,128]{1,0:T(8,128)(2,1)S(1)}, bf16[480,128]{1,0:T(8,128)(2,1)S(1)}, u32[]{:S(2)}, u32[]{:S(2)}) %collective-permute-start.16) | collective-permute-done | bytes 122912 | tf_op jit(solution)/shard_map/ppermute | solution.py:20
  51.8 1.5 %collective-permute-done.18.refs_2_ = bf16[480,128]{1,0:T(8,128)(2,1)S(1)} collective-permute-done((bf16[480,128]{1,0:T(8,128)(2,1)S(1)}, bf16[480,128]{1,0:T(8,128)(2,1)S(1)}, u32[]{:S(2)}, u32[]{:S(2)}) %collective-permute-start.18) | collective-permute-done | bytes 122912 | tf_op jit(solution)/shard_map/ppermute | solution.py:20
  53.3 2.2 %copy-done.1 = bf16[2048,1024]{1,0:T(8,128)(2,1)S(1)} copy-done((bf16[2048,1024]{1,0:T(8,128)(2,1)S(1)}, bf16[2048,1024]{1,0:T(8,128)(2,1)}, u32[]{:S(2)}) %copy-start.1) | copy-done | bytes 4194328
  55.5 2.6 %second_product.1 = (bf16[1760,128]{1,0:T(8,128)(2,1)S(1)}, f32[1760,128]{1,0:T(8,128)S(1)}) custom-call(bf16[2048,1024]{1,0:T(8,128)(2,1)S(1)} %copy-done.1, bf16[256,128]{1,0:T(8,128)(2,1)S(1)} %get-tuple-element.34.agg_ref, f32[224,128]{1,0:T(8,128)S(1)} %get-tuple-element.35.mine_ref, bf16[480,128]{1,0:T(8,128)(2,1)S(1)} %collective-permute-done.16.refs_0_, ...), custom_call_target="tpu_custom_call" | custom-call | flops 1073741824 | bytes 6292480 | tf_op jit(solution)/shard_map/second_product/pallas_call | solution.py:27
  58.2 1.8 %collective-permute-done.19 = bf16[1760,128]{1,0:T(8,128)(2,1)S(1)} collective-permute-done((bf16[1760,128]{1,0:T(8,128)(2,1)S(1)}, bf16[1760,128]{1,0:T(8,128)(2,1)S(1)}, u32[]{:S(2)}, u32[]{:S(2)}) %collective-permute-start.19) | collective-permute-done | bytes 450592 | tf_op jit(solution)/shard_map/ppermute | solution.py:20
  60.1 1.8 %collective-permute-start.22 = (bf16[608,128]{1,0:T(8,128)(2,1)S(1)}, bf16[608,128]{1,0:T(8,128)(2,1)S(1)}, u32[]{:S(2)}, u32[]{:S(2)}) collective-permute-start(bf16[608,128]{1,0:T(8,128)(2,1)S(1)} %concatenate.46), channel_id=1, source_target_pairs={{0,6},{1,7},{2,4},{3,5},{4,2},{5,3},{6,0},{7,1},{8,14},{9,15},{10,... | collective-permute-start | bytes 466952 | tf_op jit(solution)/shard_map/ppermute | solution.py:20
  62.0 1.6 %collective-permute-start.21 = (bf16[608,128]{1,0:T(8,128)(2,1)S(1)}, bf16[608,128]{1,0:T(8,128)(2,1)S(1)}, u32[]{:S(2)}, u32[]{:S(2)}) collective-permute-start(bf16[608,128]{1,0:T(8,128)(2,1)S(1)} %get-tuple-element.91), channel_id=1, source_target_pairs={{0,4},{1,5},{2,6},{3,7},{4,0},{5,1},{6,2},{7,3},{8,12},{9,13},{10,... | collective-permute-start | bytes 466952 | tf_op jit(solution)/shard_map/ppermute | solution.py:20
  63.5 1.2 %collective-permute-start.20 = (bf16[608,128]{1,0:T(8,128)(2,1)S(1)}, bf16[608,128]{1,0:T(8,128)(2,1)S(1)}, u32[]{:S(2)}, u32[]{:S(2)}) collective-permute-start(bf16[608,128]{1,0:T(8,128)(2,1)S(1)} %get-tuple-element.90), channel_id=1, source_target_pairs={{0,2},{1,3},{2,0},{3,1},{4,6},{5,7},{6,4},{7,5},{8,10},{9,11},{10,... | collective-permute-start | bytes 466952 | tf_op jit(solution)/shard_map/ppermute | solution.py:20
  64.8 4.2 %collective-permute-done.22 = bf16[608,128]{1,0:T(8,128)(2,1)S(1)} collective-permute-done((bf16[608,128]{1,0:T(8,128)(2,1)S(1)}, bf16[608,128]{1,0:T(8,128)(2,1)S(1)}, u32[]{:S(2)}, u32[]{:S(2)}) %collective-permute-start.22) | collective-permute-done | bytes 155680 | tf_op jit(solution)/shard_map/ppermute | solution.py:20
  69.0 8.5 %collective-permute-done.21 = bf16[608,128]{1,0:T(8,128)(2,1)S(1)} collective-permute-done((bf16[608,128]{1,0:T(8,128)(2,1)S(1)}, bf16[608,128]{1,0:T(8,128)(2,1)S(1)}, u32[]{:S(2)}, u32[]{:S(2)}) %collective-permute-start.21) | collective-permute-done | bytes 155680 | tf_op jit(solution)/shard_map/ppermute | solution.py:20
  78.0 1.2 %collective-permute-start.24 = (bf16[224,128]{1,0:T(8,128)(2,1)S(1)}, bf16[224,128]{1,0:T(8,128)(2,1)S(1)}, u32[]{:S(2)}, u32[]{:S(2)}) collective-permute-start(bf16[224,128]{1,0:T(8,128)(2,1)S(1)} %add_convert_fusion.refs_0_), channel_id=1, source_target_pairs={{0,16},{8,24},{16,0},{24,8},{1,17},{9,25},{17,1},{25,9},{2,18},{10... | collective-permute-start | bytes 172040 | tf_op jit(solution)/shard_map/ppermute | solution.py:20
  79.2 2.0 %collective-permute-start.25 = (bf16[224,128]{1,0:T(8,128)(2,1)S(1)}, bf16[224,128]{1,0:T(8,128)(2,1)S(1)}, u32[]{:S(2)}, u32[]{:S(2)}) collective-permute-start(bf16[224,128]{1,0:T(8,128)(2,1)S(1)} %add_convert_fusion.refs_0_), channel_id=1, source_target_pairs={{0,24},{8,16},{16,8},{24,0},{1,25},{9,17},{17,9},{25,1},{2,26},{10... | collective-permute-start | bytes 172040 | tf_op jit(solution)/shard_map/ppermute | solution.py:20
  82.7 1.6 %collective-permute-done.25.refs_3_ = bf16[224,128]{1,0:T(8,128)(2,1)S(1)} collective-permute-done((bf16[224,128]{1,0:T(8,128)(2,1)S(1)}, bf16[224,128]{1,0:T(8,128)(2,1)S(1)}, u32[]{:S(2)}, u32[]{:S(2)}) %collective-permute-start.25) | collective-permute-done | bytes 57376 | tf_op jit(solution)/shard_map/ppermute | solution.py:20
  84.3 1.3 %place_gradients.1 = (f32[128,256]{1,0:T(8,128)}, f32[1,256]{1,0:T(1,128)}, f32[256,172]{1,0:T(8,128)S(1)}, f32[1,172]{1,0:T(1,128)}) custom-call(s32[2]{0:T(128)S(1)} %pad_add_fusion.place_ref, bf16[224,128]{1,0:T(8,128)(2,1)S(1)} %add_convert_fusion.refs_0_, bf16[224,128]{1,0:T(8,128)(2,1)S(1)} %collective-permute-done.23.refs_1_, ...), custom_call_target="tpu_custom_call" | custom-call | bytes 538296 | tf_op jit(solution)/shard_map/place_gradients/pallas_call | solution.py:27
  (85 shorter events, 13.8 us)
Async XLA Ops:
  0.6 11.9 %collective-permute-start = (bf16[256,128]{1,0:T(8,128)(2,1)}, bf16[256,128]{1,0:T(8,128)(2,1)S(1)}, u32[]{:S(2)}, u32[]{:S(2)}) collective-permute-start(bf16[256,128]{1,0:T(8,128)(2,1)} %refs_3_.2), channel_id=1, source_target_pairs={{0,8},{8,0},{16,24},{24,16},{1,9},{9,1},{17,25},{25,17},{2,10},{10... | collective-permute-start | bytes 196616 | tf_op jit(solution)/shard_map/ppermute | solution.py:20
  3.6 19.1 %collective-permute-start.1 = (bf16[256,128]{1,0:T(8,128)(2,1)}, bf16[256,128]{1,0:T(8,128)(2,1)S(1)}, u32[]{:S(2)}, u32[]{:S(2)}) collective-permute-start(bf16[256,128]{1,0:T(8,128)(2,1)} %refs_3_.2), channel_id=1, source_target_pairs={{0,16},{8,24},{16,0},{24,8},{1,17},{9,25},{17,1},{25,9},{2,18},{10... | collective-permute-start | bytes 196616 | tf_op jit(solution)/shard_map/ppermute | solution.py:20
  5.2 18.4 %collective-permute-start.2 = (bf16[256,128]{1,0:T(8,128)(2,1)}, bf16[256,128]{1,0:T(8,128)(2,1)S(1)}, u32[]{:S(2)}, u32[]{:S(2)}) collective-permute-start(bf16[256,128]{1,0:T(8,128)(2,1)} %refs_3_.2), channel_id=1, source_target_pairs={{0,24},{8,16},{16,8},{24,0},{1,25},{9,17},{17,9},{25,1},{2,26},{10... | collective-permute-start | bytes 196616 | tf_op jit(solution)/shard_map/ppermute | solution.py:20
  7.1 19.4 %collective-permute-start.7 = (bf16[384,128]{1,0:T(8,128)(2,1)S(1)}, bf16[384,128]{1,0:T(8,128)(2,1)S(1)}, u32[]{:S(2)}, u32[]{:S(2)}) collective-permute-start(bf16[384,128]{1,0:T(8,128)(2,1)S(1)} %maximum_maximum_fusion.refs_12_), channel_id=1, source_target_pairs={{0,2},{1,3},{2,0},{3,1},{4,6},{5,7},{6,4},{7,5},{8,10},{9,11},{10,... | collective-permute-start | bytes 294920 | tf_op jit(solution)/shard_map/ppermute | solution.py:20
  9.2 17.4 %collective-permute-start.8 = (bf16[384,128]{1,0:T(8,128)(2,1)S(1)}, bf16[384,128]{1,0:T(8,128)(2,1)S(1)}, u32[]{:S(2)}, u32[]{:S(2)}) collective-permute-start(bf16[384,128]{1,0:T(8,128)(2,1)S(1)} %maximum_maximum_fusion.refs_12_), channel_id=1, source_target_pairs={{0,4},{1,5},{2,6},{3,7},{4,0},{5,1},{6,2},{7,3},{8,12},{9,13},{10,... | collective-permute-start | bytes 294920 | tf_op jit(solution)/shard_map/ppermute | solution.py:20
  17.3 14.7 %copy-start = (bf16[2048,1024]{1,0:T(8,128)(2,1)}, bf16[2048,1024]{1,0:T(8,128)(2,1)S(1)}, u32[]{:S(2)}) copy-start(bf16[2048,1024]{1,0:T(8,128)(2,1)S(1)} %get-tuple-element.25.dense_ref) | copy-start | bytes 12582916
  17.3 4.7 %collective-permute-start.10 = (f32[16,128]{1,0:T(8,128)S(1)}, f32[16,128]{1,0:T(8,128)S(1)}, u32[]{:S(2)}, u32[]{:S(2)}) collective-permute-start(f32[16,128]{1,0:T(8,128)S(1)} %get-tuple-element.28), channel_id=1, source_target_pairs={{0,4},{1,5},{2,6},{3,7},{4,0},{5,1},{6,2},{7,3},{8,12},{9,13},{10,... | collective-permute-start | bytes 24584 | tf_op jit(solution)/shard_map/ppermute | solution.py:20
  22.0 6.5 %collective-permute-start.9 = (bf16[384,128]{1,0:T(8,128)(2,1)S(1)}, bf16[384,128]{1,0:T(8,128)(2,1)S(1)}, u32[]{:S(2)}, u32[]{:S(2)}) collective-permute-start(bf16[384,128]{1,0:T(8,128)(2,1)S(1)} %maximum_maximum_fusion.refs_12_), channel_id=1, source_target_pairs={{0,6},{1,7},{2,4},{3,5},{4,2},{5,3},{6,0},{7,1},{8,14},{9,15},{10,... | collective-permute-start | bytes 294920 | tf_op jit(solution)/shard_map/ppermute | solution.py:20
  22.8 3.7 %collective-permute-start.11 = (f32[16,128]{1,0:T(8,128)S(1)}, f32[16,128]{1,0:T(8,128)S(1)}, u32[]{:S(2)}, u32[]{:S(2)}) collective-permute-start(f32[16,128]{1,0:T(8,128)S(1)} %add.43), channel_id=1, source_target_pairs={{0,2},{1,3},{2,0},{3,1},{4,6},{5,7},{6,4},{7,5},{8,10},{9,11},{10,... | collective-permute-start | bytes 24584 | tf_op jit(solution)/shard_map/ppermute | solution.py:20
  26.1 12.7 %copy-start.9 = (bf16[256,172]{0,1:T(8,128)(2,1)S(1)}, bf16[256,172]{0,1:T(8,128)(2,1)}, u32[]{:S(2)}) copy-start(bf16[256,172]{0,1:T(8,128)(2,1)} %param.17) | copy-start | bytes 264196
  26.1 2.6 %collective-permute-start.3 = (bf16[1024,128]{1,0:T(8,128)(2,1)S(1)}, bf16[1024,128]{1,0:T(8,128)(2,1)S(1)}, u32[]{:S(2)}, u32[]{:S(2)}) collective-permute-start(bf16[1024,128]{1,0:T(8,128)(2,1)S(1)} %get-tuple-element.27), channel_id=1, source_target_pairs={{0,1},{1,0},{2,3},{3,2},{4,5},{5,4},{6,7},{7,6},{8,9},{9,8},{10,11... | collective-permute-start | bytes 786440 | tf_op jit(solution)/shard_map/ppermute | solution.py:20
  26.5 17.4 %copy-start.4 = (bf16[256,128]{1,0:T(8,128)(2,1)S(1)}, bf16[256,128]{1,0:T(8,128)(2,1)}, u32[]{:S(2)}) copy-start(bf16[256,128]{1,0:T(8,128)(2,1)} %refs_3_.2) | copy-start | bytes 196612
  26.6 17.4 %copy-start.5 = (bf16[128,256]{1,0:T(8,128)(2,1)S(1)}, bf16[128,256]{1,0:T(8,128)(2,1)}, u32[]{:S(2)}) copy-start(bf16[128,256]{1,0:T(8,128)(2,1)} %refs_3_.3) | copy-start | bytes 196612
  26.6 17.4 %copy-start.6 = (f32[256]{0:T(256)S(1)}, f32[256]{0:T(256)}, u32[]{:S(2)}) copy-start(f32[256]{0:T(256)} %param.16) | copy-start | bytes 3076
  28.6 1.8 %collective-permute-start.12 = (bf16[1568,128]{1,0:T(8,128)(2,1)S(1)}, bf16[1568,128]{1,0:T(8,128)(2,1)S(1)}, u32[]{:S(2)}, u32[]{:S(2)}) collective-permute-start(bf16[1568,128]{1,0:T(8,128)(2,1)S(1)} %constant_dynamic-update-slice_fusion.5), channel_id=1, source_target_pairs={{0,1},{1,0},{2,3},{3,2},{4,5},{5,4},{6,7},{7,6},{8,9},{9,8},{10,11... | collective-permute-start | bytes 1204232 | tf_op jit(solution)/shard_map/ppermute | solution.py:20
  28.8 8.2 %collective-permute-start.4 = (bf16[256,128]{1,0:T(8,128)(2,1)S(1)}, bf16[256,128]{1,0:T(8,128)(2,1)S(1)}, u32[]{:S(2)}, u32[]{:S(2)}) collective-permute-start(bf16[256,128]{1,0:T(8,128)(2,1)S(1)} %get-tuple-element.75), channel_id=1, source_target_pairs={{0,2},{1,3},{2,0},{3,1},{4,6},{5,7},{6,4},{7,5},{8,10},{9,11},{10,... | collective-permute-start | bytes 196616 | tf_op jit(solution)/shard_map/ppermute | solution.py:20
  32.0 11.9 %collective-permute-start.13 = (bf16[176,256]{1,0:T(8,128)(2,1)S(1)}, bf16[176,256]{1,0:T(8,128)(2,1)S(1)}, u32[]{:S(2)}, u32[]{:S(2)}) collective-permute-start(bf16[176,256]{1,0:T(8,128)(2,1)S(1)} %get-tuple-element.31), channel_id=1, source_target_pairs={{0,8},{8,0},{16,24},{24,16},{1,9},{9,1},{17,25},{25,17},{2,10},{10... | collective-permute-start | bytes 270344 | tf_op jit(solution)/shard_map/ppermute | solution.py:20
  34.4 9.5 %collective-permute-start.14 = (bf16[176,256]{1,0:T(8,128)(2,1)S(1)}, bf16[176,256]{1,0:T(8,128)(2,1)S(1)}, u32[]{:S(2)}, u32[]{:S(2)}) collective-permute-start(bf16[176,256]{1,0:T(8,128)(2,1)S(1)} %get-tuple-element.32), channel_id=1, source_target_pairs={{0,16},{8,24},{16,0},{24,8},{1,17},{9,25},{17,1},{25,9},{2,18},{10... | collective-permute-start | bytes 270344 | tf_op jit(solution)/shard_map/ppermute | solution.py:20
  35.0 8.9 %collective-permute-start.15 = (bf16[176,256]{1,0:T(8,128)(2,1)S(1)}, bf16[176,256]{1,0:T(8,128)(2,1)S(1)}, u32[]{:S(2)}, u32[]{:S(2)}) collective-permute-start(bf16[176,256]{1,0:T(8,128)(2,1)S(1)} %get-tuple-element.33), channel_id=1, source_target_pairs={{0,24},{8,16},{16,8},{24,0},{1,25},{9,17},{17,9},{25,1},{2,26},{10... | collective-permute-start | bytes 270344 | tf_op jit(solution)/shard_map/ppermute | solution.py:20
  36.0 8.0 %collective-permute-start.5 = (bf16[256,128]{1,0:T(8,128)(2,1)S(1)}, bf16[256,128]{1,0:T(8,128)(2,1)S(1)}, u32[]{:S(2)}, u32[]{:S(2)}) collective-permute-start(bf16[256,128]{1,0:T(8,128)(2,1)S(1)} %get-tuple-element.74), channel_id=1, source_target_pairs={{0,4},{1,5},{2,6},{3,7},{4,0},{5,1},{6,2},{7,3},{8,12},{9,13},{10,... | collective-permute-start | bytes 196616 | tf_op jit(solution)/shard_map/ppermute | solution.py:20
  37.0 7.0 %collective-permute-start.6 = (bf16[256,128]{1,0:T(8,128)(2,1)S(1)}, bf16[256,128]{1,0:T(8,128)(2,1)S(1)}, u32[]{:S(2)}, u32[]{:S(2)}) collective-permute-start(bf16[256,128]{1,0:T(8,128)(2,1)S(1)} %get-tuple-element.73), channel_id=1, source_target_pairs={{0,6},{1,7},{2,4},{3,5},{4,2},{5,3},{6,0},{7,1},{8,14},{9,15},{10,... | collective-permute-start | bytes 196616 | tf_op jit(solution)/shard_map/ppermute | solution.py:20
  45.2 5.9 %collective-permute-start.16 = (bf16[480,128]{1,0:T(8,128)(2,1)S(1)}, bf16[480,128]{1,0:T(8,128)(2,1)S(1)}, u32[]{:S(2)}, u32[]{:S(2)}) collective-permute-start(bf16[480,128]{1,0:T(8,128)(2,1)S(1)} %get-tuple-element.36), channel_id=1, source_target_pairs={{0,8},{8,0},{16,24},{24,16},{1,9},{9,1},{17,25},{25,17},{2,10},{10... | collective-permute-start | bytes 368648 | tf_op jit(solution)/shard_map/ppermute | solution.py:20
  46.9 4.9 %collective-permute-start.17 = (bf16[480,128]{1,0:T(8,128)(2,1)S(1)}, bf16[480,128]{1,0:T(8,128)(2,1)S(1)}, u32[]{:S(2)}, u32[]{:S(2)}) collective-permute-start(bf16[480,128]{1,0:T(8,128)(2,1)S(1)} %get-tuple-element.37), channel_id=1, source_target_pairs={{0,16},{8,24},{16,0},{24,8},{1,17},{9,25},{17,1},{25,9},{2,18},{10... | collective-permute-start | bytes 368648 | tf_op jit(solution)/shard_map/ppermute | solution.py:20
  47.5 5.8 %collective-permute-start.18 = (bf16[480,128]{1,0:T(8,128)(2,1)S(1)}, bf16[480,128]{1,0:T(8,128)(2,1)S(1)}, u32[]{:S(2)}, u32[]{:S(2)}) collective-permute-start(bf16[480,128]{1,0:T(8,128)(2,1)S(1)} %get-tuple-element.38), channel_id=1, source_target_pairs={{0,24},{8,16},{16,8},{24,0},{1,25},{9,17},{17,9},{25,1},{2,26},{10... | collective-permute-start | bytes 368648 | tf_op jit(solution)/shard_map/ppermute | solution.py:20
  55.5 25.8 %copy-start.10 = (f32[172]{0:T(256)S(1)}, f32[172]{0:T(256)}, u32[]{:S(2)}) copy-start(f32[172]{0:T(256)} %param.18) | copy-start | bytes 2068
  58.1 1.9 %collective-permute-start.19 = (bf16[1760,128]{1,0:T(8,128)(2,1)S(1)}, bf16[1760,128]{1,0:T(8,128)(2,1)S(1)}, u32[]{:S(2)}, u32[]{:S(2)}) collective-permute-start(bf16[1760,128]{1,0:T(8,128)(2,1)S(1)} %get-tuple-element.40), channel_id=1, source_target_pairs={{0,1},{1,0},{2,3},{3,2},{4,5},{5,4},{6,7},{7,6},{8,9},{9,8},{10,11... | collective-permute-start | bytes 1351688 | tf_op jit(solution)/shard_map/ppermute | solution.py:20
  60.1 8.9 %collective-permute-start.22 = (bf16[608,128]{1,0:T(8,128)(2,1)S(1)}, bf16[608,128]{1,0:T(8,128)(2,1)S(1)}, u32[]{:S(2)}, u32[]{:S(2)}) collective-permute-start(bf16[608,128]{1,0:T(8,128)(2,1)S(1)} %concatenate.46), channel_id=1, source_target_pairs={{0,6},{1,7},{2,4},{3,5},{4,2},{5,3},{6,0},{7,1},{8,14},{9,15},{10,... | collective-permute-start | bytes 466952 | tf_op jit(solution)/shard_map/ppermute | solution.py:20
  62.0 15.5 %collective-permute-start.21 = (bf16[608,128]{1,0:T(8,128)(2,1)S(1)}, bf16[608,128]{1,0:T(8,128)(2,1)S(1)}, u32[]{:S(2)}, u32[]{:S(2)}) collective-permute-start(bf16[608,128]{1,0:T(8,128)(2,1)S(1)} %get-tuple-element.91), channel_id=1, source_target_pairs={{0,4},{1,5},{2,6},{3,7},{4,0},{5,1},{6,2},{7,3},{8,12},{9,13},{10,... | collective-permute-start | bytes 466952 | tf_op jit(solution)/shard_map/ppermute | solution.py:20
  63.5 14.0 %collective-permute-start.20 = (bf16[608,128]{1,0:T(8,128)(2,1)S(1)}, bf16[608,128]{1,0:T(8,128)(2,1)S(1)}, u32[]{:S(2)}, u32[]{:S(2)}) collective-permute-start(bf16[608,128]{1,0:T(8,128)(2,1)S(1)} %get-tuple-element.90), channel_id=1, source_target_pairs={{0,2},{1,3},{2,0},{3,1},{4,6},{5,7},{6,4},{7,5},{8,10},{9,11},{10,... | collective-permute-start | bytes 466952 | tf_op jit(solution)/shard_map/ppermute | solution.py:20
  77.7 4.6 %collective-permute-start.23 = (bf16[224,128]{1,0:T(8,128)(2,1)S(1)}, bf16[224,128]{1,0:T(8,128)(2,1)S(1)}, u32[]{:S(2)}, u32[]{:S(2)}) collective-permute-start(bf16[224,128]{1,0:T(8,128)(2,1)S(1)} %add_convert_fusion.refs_0_), channel_id=1, source_target_pairs={{0,8},{8,0},{16,24},{24,16},{1,9},{9,1},{17,25},{25,17},{2,10},{10... | collective-permute-start | bytes 172040 | tf_op jit(solution)/shard_map/ppermute | solution.py:20
  78.0 4.7 %collective-permute-start.24 = (bf16[224,128]{1,0:T(8,128)(2,1)S(1)}, bf16[224,128]{1,0:T(8,128)(2,1)S(1)}, u32[]{:S(2)}, u32[]{:S(2)}) collective-permute-start(bf16[224,128]{1,0:T(8,128)(2,1)S(1)} %add_convert_fusion.refs_0_), channel_id=1, source_target_pairs={{0,16},{8,24},{16,0},{24,8},{1,17},{9,25},{17,1},{25,9},{2,18},{10... | collective-permute-start | bytes 172040 | tf_op jit(solution)/shard_map/ppermute | solution.py:20
  79.2 5.1 %collective-permute-start.25 = (bf16[224,128]{1,0:T(8,128)(2,1)S(1)}, bf16[224,128]{1,0:T(8,128)(2,1)S(1)}, u32[]{:S(2)}, u32[]{:S(2)}) collective-permute-start(bf16[224,128]{1,0:T(8,128)(2,1)S(1)} %add_convert_fusion.refs_0_), channel_id=1, source_target_pairs={{0,24},{8,16},{16,8},{24,0},{1,25},{9,17},{17,9},{25,1},{2,26},{10... | collective-permute-start | bytes 172040 | tf_op jit(solution)/shard_map/ppermute | solution.py:20
  (5 other events, 5.7 us)

commit v3 on v0

v3 whole, which is shorter than its diff:
```python
import functools

import jax
import jax.numpy as jnp
from jax import lax
from jax.experimental import pallas as pl
from jax.experimental.pallas import tpu as pltpu
from jax.sharding import PartitionSpec as P

BF16 = jnp.bfloat16
F32 = jnp.float32
LANES = 128
SMEM = pl.BlockSpec(memory_space=pltpu.SMEM)
VMEM = pl.BlockSpec(memory_space=pltpu.VMEM)
ANY = pl.BlockSpec(memory_space=pl.ANY)


def exchange(value, axis, mask):
    count = lax.axis_size(axis)
    return lax.ppermute(value, axis, [(i, i ^ mask) for i in range(count)])


def call(kernel, name, outs, in_specs, args, scratch=()):
    size = sum(a.size * a.dtype.itemsize for a in args)
    size += sum(o.size * o.dtype.itemsize for o in outs)
    grant = size + (6 << 20)
    return pl.pallas_call(
        kernel,
        out_shape=tuple(outs),
        in_specs=in_specs,
        out_specs=tuple(VMEM for _ in outs),
        scratch_shapes=scratch,
        compiler_params=pltpu.CompilerParams(vmem_limit_bytes=min(grant, 60 << 20)),
        name=name,
    )(*args)


def shaped(shape, dtype):
    return jax.ShapeDtypeStruct(shape, dtype)


def product(left, right, contract=((1,), (0,))):
    return lax.dot_general(left, right, (contract, ((), ())), preferred_element_type=F32)


def split(value):
    high = value.astype(BF16)
    return high, (value - high.astype(F32)).astype(BF16)


def dense_kernel(own, index_ref, tiles_ref, after_ref, dense_ref, degree_ref):
    slots, block, _ = tiles_ref.shape
    rows, columns = dense_ref.shape
    half = rows // (block * own * 2)
    r, c = index_ref[2 * slots + 1], index_ref[2 * slots + 2]
    dense_ref[...] = jnp.zeros_like(dense_ref)

    @pl.loop(0, index_ref[2 * slots])
    def _(slot):
        k = index_ref[slot]
        j = index_ref[slots + slot]
        p = (k // own) ^ c
        at_row = ((p & 1) * half + (p >> 1)) * own + k % own
        at_col = ((j // own) ^ r) * own + j % own
        dense_ref[
            pl.ds(pl.multiple_of(at_row * block, block), block),
            pl.ds(pl.multiple_of(at_col * block, block), block),
        ] = tiles_ref[slot]

    ones = jnp.ones((8, columns), BF16)
    for start in range(0, rows, 2 * block):
        sums = product(ones, dense_ref[pl.ds(start, 2 * block), :], ((1,), (1,)))
        for part in range(2):
            degree_ref[pl.ds(start // block + part, 1), :] = sums[:1, part * block : (part + 1) * block]


def first_kernel(spans, dense_ref, degree_ref, g_ref, far_ref, *refs):
    pieces, (send_ref, keep_ref, pair_ref, held) = refs[:spans], refs[spans:]
    pair_ref[0] = g_ref[...]
    pair_ref[1] = far_ref[...]
    nodes = pieces[0].shape[0]
    for s in range(spans):
        held[pl.ds(s * nodes, nodes), :] = pieces[s][...]
    half = keep_ref.shape[0] // nodes
    blocks = degree_ref.shape[0]
    high, low = split(degree_ref[...])
    send_ref[pl.ds(half * nodes, blocks), :] = high
    send_ref[pl.ds(half * nodes + blocks, blocks), :] = low

    @pl.loop(0, half)
    def _(s):
        at = pl.multiple_of(s * nodes, nodes)
        send_ref[pl.ds(at, nodes), :] = product(
            dense_ref[pl.ds(pl.multiple_of((half + s) * nodes, nodes), nodes), :], held[...]
        ).astype(BF16)
        keep_ref[pl.ds(at, nodes), :] = product(dense_ref[pl.ds(at, nodes), :], held[...])


def near_kernel(half, keep_ref, other_ref, part_ref, own_ref, degree_ref, *sends):
    nodes = own_ref.shape[0]
    blocks = part_ref.shape[0]
    tail = other_ref[pl.ds(half * nodes, blocks), :].astype(F32)
    tail = tail + other_ref[pl.ds(half * nodes + blocks, blocks), :].astype(F32)
    degree = part_ref[...] + jnp.concatenate([tail[blocks // 2 :], tail[: blocks // 2]], axis=0)
    degree_ref[...] = degree
    high, low = split(degree)
    own_ref[...] = keep_ref[:nodes, :] + other_ref[:nodes, :].astype(F32)
    for s in range(1, half):
        at = slice(s * nodes, (s + 1) * nodes)
        sends[s - 1][:nodes, :] = (keep_ref[at, :] + other_ref[at, :].astype(F32)).astype(BF16)
        sends[s - 1][nodes : nodes + blocks, :] = high
        sends[s - 1][nodes + blocks :, :] = low


def swapped(value, half, mask):
    own = value.shape[0] // (2 * half)
    order = [h * half + (s ^ mask) for h in range(2) for s in range(half)]
    return jnp.concatenate([value[q * own : (q + 1) * own] for q in order], axis=0)


def agg_kernel(half, near_ref, part_ref, features_ref, left_ref, right_ref, *refs):
    got, (agg_ref, degree_ref, joined_ref) = refs[: half - 1], refs[half - 1 :]
    joined_ref[: half // 2] = left_ref[...]
    joined_ref[half // 2 :] = right_ref[...]
    nodes = features_ref.shape[0]
    block = LANES
    blocks = degree_ref.shape[0]
    total = near_ref[...]
    degree = part_ref[...]
    for s, ref in enumerate(got):
        total = total + ref[:nodes, :].astype(F32)
        tail = ref[nodes : nodes + blocks, :].astype(F32) + ref[nodes + blocks :, :].astype(F32)
        degree = degree + swapped(tail, half, s + 1)
    degree = 1.0 + degree
    degree_ref[...] = degree
    upright = degree.T
    total = total + features_ref[...].astype(F32)
    for b in range(nodes // block):
        at = slice(b * block, (b + 1) * block)
        agg_ref[at, :] = (total[at] / upright[:, b : b + 1]).astype(BF16)


def tree_sum(values):
    while len(values) > 1:
        values = [a + b for a, b in zip(values[::2], values[1::2])]
    return values[0]


def gelu_parts(z):
    scale = 0.7978845608028654
    t = jnp.tanh(scale * (z + 0.044715 * (z * z * z)))
    value = 0.5 * z * (1.0 + t)
    slope = 0.5 * (1.0 + t) + 0.5 * z * (1.0 - t * t) * (scale * (1.0 + 3.0 * 0.044715 * (z * z)))
    return value, slope


def second_kernel(spans, dense_ref, after_ref, *refs):
    pieces, refs = refs[:spans], refs[spans:]
    w1_ref, b1_ref, w2_ref, send_ref, keep_ref, held = refs
    nodes = pieces[0].shape[0]
    half, tall, _ = keep_ref.shape
    classes = w2_ref.shape[0]
    for s in range(spans):
        value, _ = gelu_parts(product(pieces[s][...], w1_ref[...]) + b1_ref[...])
        hidden = product(w2_ref[...], value.astype(BF16), ((1,), (1,)))
        if tall > classes:
            hidden = jnp.concatenate([hidden, jnp.zeros((tall - classes, nodes), F32)], axis=0)
        held[:, s * nodes : (s + 1) * nodes] = hidden.astype(BF16)
        if s == 0:
            first = hidden

    @pl.loop(0, half)
    def _(s):
        at = pl.multiple_of((half + s) * nodes, nodes)
        send_ref[s] = product(held[...], dense_ref[pl.ds(at, nodes), :], ((1,), (1,))).astype(BF16)
        at = pl.multiple_of(s * nodes, nodes)
        keep_ref[s] = product(held[...], dense_ref[pl.ds(at, nodes), :], ((1,), (1,)))

    keep_ref[0] += first


def grad_kernel(spans, count, place_ref, dense_ref, degree_ref, *refs):
    pieces, refs = refs[:spans], refs[spans:]
    cots, refs = refs[:count], refs[count:]
    w1_ref, b1_ref, w2_ref, mine_ref, refs = refs[0], refs[1], refs[2], refs[3], refs[4:]
    sends, turned, total = refs[: spans - 1], refs[-2], refs[-1]
    fin, hidden = w1_ref.shape
    block = LANES
    tall = turned.shape[0]
    rank = place_ref[0]
    nodes = pieces[0].shape[0]
    classes = w2_ref.shape[0]
    for q in range(count):
        ref, at = cots[q]
        degree = jnp.concatenate([degree_ref[2 * q : 2 * q + 1, :], degree_ref[2 * q + 1 : 2 * q + 2, :]], axis=1)
        scaled = (ref[...] if at is None else ref[at]).astype(F32) / degree
        if tall > classes:
            scaled = jnp.concatenate([scaled, jnp.zeros((tall - classes, nodes), F32)], axis=0)
        turned[:, q * nodes : (q + 1) * nodes] = scaled.astype(BF16)
    w2 = jnp.concatenate([w2_ref[...].astype(F32), jnp.zeros((2 * block - classes, hidden), F32)], axis=0).astype(BF16)
    grad_w1 = jnp.zeros((fin, hidden), F32)
    grad_w2 = jnp.zeros((tall, hidden), F32)
    grad_b1 = jnp.zeros((1, hidden), F32)
    for s in range(spans):
        agg = pieces[s][...]
        value, slope = gelu_parts(product(agg, w1_ref[...]) + b1_ref[...])
        q = product(turned[...], dense_ref[:, s * nodes : (s + 1) * nodes])
        if s == 0:
            q = q + turned[:, :nodes].astype(F32)
        high, low = split(q)
        h = value.astype(BF16)
        grad_w2 = grad_w2 + product(high, h) + product(low, h)
        high, low = split(jnp.concatenate([q, jnp.zeros((2 * block - tall, nodes), F32)], axis=0).T)
        d_first = (product(high, w2) + product(low, w2)) * slope
        grad_w1 = grad_w1 + product(agg.astype(F32).T.astype(BF16), d_first.astype(BF16))
        grad_b1 = grad_b1 + jnp.sum(d_first, axis=0, keepdims=True)
    own = cots[0][0][...] if cots[0][1] is None else cots[0][0][cots[0][1]]
    grad_b2 = product(jnp.ones((8, nodes), BF16), own, ((1,), (1,)))[:1]
    a = fin // spans
    b = total.shape[1] - a - 16
    total[...] = jnp.zeros_like(total)
    for t in range(spans):
        total[t, :a, :] = grad_w1[t * a : (t + 1) * a]
        have = min(b, tall - t * b)
        if have > 0:
            total[t, a : a + have, :] = grad_w2[t * b : t * b + have]
    total[0, a + b : a + b + 1, :] = grad_b1
    total[0, a + b + 1 : a + b + 2, :classes] = grad_b2
    mine_ref[...] = total[rank]
    for s in range(1, spans):
        sends[s - 1][...] = total[rank ^ s].astype(BF16)


def core_kernel(half, keep_ref, other_ref, mine_ref, far_ref, own_ref, share_ref, *sends):
    share_ref[...] = (mine_ref[...] + far_ref[...]).astype(BF16)
    own_ref[...] = keep_ref[0] + other_ref[0].astype(F32)
    for s in range(1, half):
        sends[s - 1][...] = (keep_ref[s] + other_ref[s].astype(F32)).astype(BF16)


def last_kernel(spans, half, place_ref, total_ref, degree_ref, bias_ref, *refs):
    parts, refs = refs[: half - 1], refs[half - 1 :]
    got, (logits_ref, w1_ref, b1_ref, w2_ref, b2_ref, tall_ref) = refs[:spans], refs[spans:]
    total = total_ref[...]
    for ref in parts:
        total = total + ref[...].astype(F32)
    nodes = total.shape[1]
    classes = logits_ref.shape[0]
    degree = jnp.concatenate([degree_ref[b : b + 1, :] for b in range(nodes // LANES)], axis=1)
    bias = jnp.concatenate([bias_ref[...], jnp.zeros((1, 2 * LANES - classes), F32)], axis=1)
    bias = jnp.broadcast_to(bias, (8, 2 * LANES)).T
    logits_ref[...] = (total[:classes] / degree + bias[:classes, :1]).astype(BF16)
    fin, hidden = w1_ref.shape
    classes = w2_ref.shape[0]
    a = fin // spans
    b = got[0].shape[0] - a - 16
    for s in range(spans):
        t = place_ref[0] ^ s
        share = got[s][...].astype(F32)
        w1_ref[pl.ds(pl.multiple_of(t * a, a), a), :] = share[:a]
        tall_ref[pl.ds(pl.multiple_of(t * b, b), b), :] = share[a : a + b]

        @pl.when(t == 0)
        def _():
            b1_ref[...] = share[a + b : a + b + 1]
            b2_ref[...] = share[a + b + 1 : a + b + 2, :classes]

    w2_ref[...] = tall_ref[:classes, :]


def local(
    features,
    tiles,
    tile_row,
    tile_col,
    tile_live,
    w_first,
    b_first,
    w_second,
    b_second,
    grad_logits,
):
    row_count = lax.axis_size("row")
    col_count = lax.axis_size("col")
    half = col_count // 2
    nodes, fin = features.shape
    block = tiles.shape[-1]
    own = nodes // block
    hidden = w_first.shape[1]
    classes = w_second.shape[1]
    tall = -(-classes // 16) * 16
    rows, columns = col_count * nodes, row_count * nodes
    blocks = rows // block
    place = jnp.stack([lax.axis_index("row"), lax.axis_index("col")]).astype(jnp.int32)
    index = jnp.concatenate([tile_row[0, 0], tile_col[0, 0], tile_live[0], place])
    bias = b_first[None, :]
    w2 = w_second.T
    g_own = grad_logits.T

    inputs = [features] + [exchange(features, "row", s) for s in range(1, row_count)]
    far_g = exchange(g_own, "col", half)
    order = [0]
    mask = half
    while mask > 1:
        order = order + [s ^ (mask // 2) for s in order]
        mask //= 2

    dense, degree = call(
        functools.partial(dense_kernel, own),
        "dense_adjacency",
        [shaped((rows, columns), BF16), shaped((blocks, block), F32)],
        [SMEM, VMEM, ANY],
        [index, tiles[0, 0], inputs[1]],
    )
    send, keep, left = call(
        functools.partial(first_kernel, row_count),
        "first_product",
        [
            shaped((rows // 2 + 2 * blocks, fin), BF16),
            shaped((rows // 2, fin), F32),
            shaped((2, classes, nodes), BF16),
        ],
        [VMEM] * (4 + row_count),
        [dense, degree, g_own, far_g] + inputs,
        scratch=[pltpu.VMEM((columns, fin), BF16)],
    )
    other = exchange(send, "col", 1)
    mask = half // 2
    while mask > 2:
        left = jnp.concatenate([left, exchange(left, "col", mask)], axis=0)
        mask //= 2
    right = exchange(left, "col", mask)
    out = call(
        functools.partial(near_kernel, half),
        "first_core_sum",
        [shaped((nodes, fin), F32), shaped((blocks, block), F32)]
        + [shaped((nodes + 2 * blocks, fin), BF16)] * (half - 1),
        [VMEM] * 3,
        [keep, other, degree],
    )
    got = [exchange(out[1 + s], "col", 2 * s) for s in range(1, half)]
    agg, degree, near_g = call(
        functools.partial(agg_kernel, half),
        "first_aggregate",
        [shaped((nodes, fin), BF16), shaped((blocks, block), F32), shaped((half, classes, nodes), BF16)],
        [VMEM] * (5 + half - 1),
        [out[0], out[1], features, left, right] + got,
    )
    pieces = [agg] + [exchange(agg, "row", s) for s in range(1, row_count)]
    other_g = exchange(near_g, "col", 1)

    size = fin // row_count + -(-classes // (16 * row_count)) * 16 + 16
    out = call(
        lambda *refs: grad_kernel(
            row_count,
            col_count,
            *refs[: 3 + row_count],
            *((refs[3 + row_count + h], order.index(s)) for h in range(2) for s in range(half)),
            *refs[5 + row_count :],
        ),
        "gradients",
        [shaped((size, hidden), F32)] + [shaped((size, hidden), BF16)] * (row_count - 1),
        [SMEM] + [VMEM] * (2 + row_count + 2 + 3),
        [place, dense, degree] + pieces + [near_g, other_g, w_first, bias, w2],
        scratch=[pltpu.VMEM((tall, rows), BF16), pltpu.VMEM((row_count, size, hidden), F32)],
    )
    mine = out[0]
    for s in range(1, row_count):
        mine = mine + exchange(out[s], "row", s).astype(F32)

    send, keep = call(
        functools.partial(second_kernel, row_count),
        "second_product",
        [shaped((half, tall, nodes), BF16), shaped((half, tall, nodes), F32)],
        [VMEM, ANY] + [VMEM] * (row_count + 3),
        [dense, out[0]] + pieces + [w_first, bias, w2],
        scratch=[pltpu.VMEM((tall, columns), BF16)],
    )
    out = call(
        functools.partial(core_kernel, half),
        "second_core_sum",
        [shaped((tall, nodes), F32), shaped((size, hidden), BF16)] + [shaped((tall, nodes), BF16)] * (half - 1),
        [VMEM] * 4,
        [keep, exchange(send, "col", 1), mine, exchange(mine, "col", 1)],
    )
    shares = [out[1].astype(F32)] + [exchange(out[1], "col", 2 * s).astype(F32) for s in range(1, half)]
    share = tree_sum(shares).astype(BF16)
    parts = [exchange(out[1 + s], "col", 2 * s) for s in range(1, half)]
    shares = [share] + [exchange(share, "row", s) for s in range(1, row_count)]
    logits, grad_w1, grad_b1, grad_w2, grad_b2 = call(
        functools.partial(last_kernel, row_count, half),
        "results",
        [
            shaped((classes, nodes), BF16),
            shaped((fin, hidden), F32),
            shaped((1, hidden), F32),
            shaped((classes, hidden), F32),
            shaped((1, classes), F32),
        ],
        [SMEM] + [VMEM] * (3 + half - 1 + row_count),
        [place, out[0], degree, b_second[None, :]] + parts + shares,
        scratch=[pltpu.VMEM(((size - fin // row_count - 16) * row_count, hidden), F32)],
    )
    return logits.T, grad_w1, grad_b1[0], grad_w2.T, grad_b2[0]


def solution(mesh):
    return jax.shard_map(
        local,
        mesh=mesh,
        in_specs=(
            P(("row", "col"), None),
            P("row", "col", None, None, None),
            P("row", "col", None),
            P("row", "col", None),
            P("row", "col"),
            P(),
            P(),
            P(),
            P(),
            P(("row", "col"), None),
        ),
        out_specs=(P(("row", "col"), None), P(), P(), P(), P()),
        check_vma=False,
    )
```

time: 342 us -> 68.1 us (0.20)
  waiting for transfers between devices: 125 us -> 15.7 us
  blocking collectives: 92.9 us -> 0 us
  other arithmetic: 58.9 us -> 0.13 us
  starting transfers between devices: 0.16 us -> 33.8 us
  matrix products: 27.7 us -> 0 us
  local copies, waits for them, and re-layouts: 18.8 us -> 3.9 us
  between operations: 15.4 us -> 1.45 us
  Pallas kernels: 0 us -> 13.2 us
    psum x1 -> x0, waiting for transfers between devices: 125 us -> none  [local(): lax.psum((grad_w1, grad_b1, grad_w2, grad_b2), ('row', 'col'))]
    all_gather x3 -> x0, blocking collectives: 40.6 us -> none  [the longest x1 16.6 us: local(): row_scaled = lax.all_gather(scaled, 'col', axis=0, tiled=True)]
    psum x1 -> x0, blocking collectives: 37.1 us -> none  [local(): lax.psum((grad_w1, grad_b1, grad_w2, grad_b2), ('row', 'col'))]
    scatter-add x19 -> x0, other arithmetic: 35.1 us -> none  [the longest x18 34.3 us: advance(): return total.at[put].add(product * weight[:, None, None])]
    ppermute x0 -> x27, starting transfers between devices: none -> 33.8 us  [exchange(): return lax.ppermute(value, axis, [(i, i ^ mask) for i in range(count)])]
    dot_general x23 -> x0, matrix products: 27.7 us -> none  [the longest x18 22.3 us: advance(): jnp.einsum(form, tile_group, picked, preferred_element_type=jnp.float32)]
    ppermute x0 -> x27, waiting for transfers between devices: none -> 15.7 us  [exchange(): return lax.ppermute(value, axis, [(i, i ^ mask) for i in range(count)])]
    convert_element_type x21 -> x1, other arithmetic: 15.4 us -> 0.03 us  [local(): share = tree_sum(shares).astype(BF16)]
  transfers between devices with their start and end apart: 4 -> 27, of which waited for: 1 -> 13; matrix products, arithmetic and copies ran while one was open for 22% -> 1% of each run, Pallas kernels for 0% -> 8%
where the time goes in v3:
time: 68.1 us; the launch traced here: 68.2 us
  starting transfers between devices  33.8 us (50%)
  waiting for transfers between devices  15.7 us (23%)
  Pallas kernels  13.2 us (19%)
  local copies, waits for them, and re-layouts  3.9 us (6%)
  between operations  1.45 us (2%)
    ppermute x27, starting transfers between devices, exchange(): return lax.ppermute(value, axis, [(i, i ^ mask) for i in range(count)])  33.8 us
    ppermute x27, waiting for transfers between devices, exchange(): return lax.ppermute(value, axis, [(i, i ^ mask) for i in range(count)])  15.7 us
    pallas_call x8, Pallas kernels, call(): pl.pallas_call(kernel, out_shape=tuple(outs), in_specs=in_specs, out_spec...  13.2 us
    unnamed x14, local copies, waits for them, and re-layouts  3.15 us
  transfers between devices with their start and end apart: 27, of which 13 were waited for; matrix products, arithmetic and copies ran while one was open for 1% of the time, Pallas kernels for 8%

profile of v3, /device:TPU:0, one launch (start us, length us, event | category | flops | bytes accessed | tf_op | source)
XLA Modules:
  0.0 68.2 jit_solution(9382963852650368392)
XLA Ops:
  0.6 4.1 %collective-permute-start.1 = (bf16[172,256]{1,0:T(8,128)(2,1)}, bf16[172,256]{1,0:T(8,128)(2,1)S(1)}, u32[]{:S(2)}, u32[]{:S(2)}) collective-permute-start(bf16[172,256]{1,0:T(8,128)(2,1)} %bitcast.18), channel_id=1, source_target_pairs={{0,4},{1,5},{2,6},{3,7},{4,0},{5,1},{6,2},{7,3},{8,12},{9,13},{10,... | collective-permute-start | bytes 264200 | tf_op jit(solution)/shard_map/ppermute | solution.py:20
  4.7 1.5 %collective-permute-start = (bf16[256,128]{1,0:T(8,128)(2,1)}, bf16[256,128]{1,0:T(8,128)(2,1)S(1)}, u32[]{:S(2)}, u32[]{:S(2)}) collective-permute-start(bf16[256,128]{1,0:T(8,128)(2,1)} %features_ref.1), channel_id=1, source_target_pairs={{0,8},{8,0},{16,24},{24,16},{1,9},{9,1},{17,25},{25,17},{2,10},{10... | collective-permute-start | bytes 196616 | tf_op jit(solution)/shard_map/ppermute | solution.py:20
  6.2 1.5 %collective-permute-start.3 = (bf16[256,128]{1,0:T(8,128)(2,1)}, bf16[256,128]{1,0:T(8,128)(2,1)S(1)}, u32[]{:S(2)}, u32[]{:S(2)}) collective-permute-start(bf16[256,128]{1,0:T(8,128)(2,1)} %features_ref.1), channel_id=1, source_target_pairs={{0,24},{8,16},{16,8},{24,0},{1,25},{9,17},{17,9},{25,1},{2,26},{10... | collective-permute-start | bytes 196616 | tf_op jit(solution)/shard_map/ppermute | solution.py:20
  9.6 1.4 %copy-done = bf16[1,1,48,128,128]{4,3,2,1,0:T(8,128)(2,1)S(1)} copy-done((bf16[1,1,48,128,128]{4,3,2,1,0:T(8,128)(2,1)S(1)}, bf16[1,1,48,128,128]{4,3,2,1,0:T(8,128)(2,1)}, u32[]{:S(2)}) %copy-start) | copy-done | bytes 1572888
  11.1 2.7 %dense_adjacency.1 = (bf16[2048,1024]{1,0:T(8,128)(2,1)S(1)}, f32[16,128]{1,0:T(8,128)S(1)}) custom-call(s32[99]{0:T(128)S(1)} %concatenate.4.index_ref, bf16[48,128,128]{2,1,0:T(8,128)(2,1)S(1)} %bitcast.15, bf16[256,128]{1,0:T(8,128)(2,1)S(1)} %collective-permute-done.after_ref.refs_1_), custom_call_target="tpu_custom_call" | custom-call | tf_op jit(solution)/shard_map/dense_adjacency/pallas_call | solution.py:27
  15.5 1.7 %first_product.1 = (bf16[1056,128]{1,0:T(8,128)(2,1)S(1)}, f32[1024,128]{1,0:T(8,128)S(1)}, bf16[2,172,256]{2,1,0:T(8,128)(2,1)S(1)}) custom-call(bf16[2048,1024]{1,0:T(8,128)(2,1)S(1)} %get-tuple-element.34.dense_ref.refs_1_, f32[16,128]{1,0:T(8,128)S(1)} %get-tuple-element.35.degree_ref.part_ref, bf16[172,256]{1,0:T(8,128)(2,1)S(1)} %bitcast.19, ...), custom_call_target="tpu_custom_call" | custom-call | tf_op jit(solution)/shard_map/first_product/pallas_call | solution.py:27
  19.9 1.3 %collective-permute-start.7 = (bf16[288,128]{1,0:T(8,128)(2,1)S(1)}, bf16[288,128]{1,0:T(8,128)(2,1)S(1)}, u32[]{:S(2)}, u32[]{:S(2)}) collective-permute-start(bf16[288,128]{1,0:T(8,128)(2,1)S(1)} %get-tuple-element.42), channel_id=1, source_target_pairs={{0,4},{1,5},{2,6},{3,7},{4,0},{5,1},{6,2},{7,3},{8,12},{9,13},{10,... | collective-permute-start | bytes 221192 | tf_op jit(solution)/shard_map/ppermute | solution.py:20
  21.2 2.2 %collective-permute-start.8 = (bf16[288,128]{1,0:T(8,128)(2,1)S(1)}, bf16[288,128]{1,0:T(8,128)(2,1)S(1)}, u32[]{:S(2)}, u32[]{:S(2)}) collective-permute-start(bf16[288,128]{1,0:T(8,128)(2,1)S(1)} %get-tuple-element.43), channel_id=1, source_target_pairs={{0,6},{1,7},{2,4},{3,5},{4,2},{5,3},{6,0},{7,1},{8,14},{9,15},{10,... | collective-permute-start | bytes 221192 | tf_op jit(solution)/shard_map/ppermute | solution.py:20
  23.4 3.0 %collective-permute-done.5.right_ref = bf16[2,172,256]{2,1,0:T(8,128)(2,1)S(1)} collective-permute-done((bf16[2,172,256]{2,1,0:T(8,128)(2,1)S(1)}, bf16[2,172,256]{2,1,0:T(8,128)(2,1)S(1)}, u32[]{:S(2)}, u32[]{:S(2)}) %collective-permute-start.5) | collective-permute-done | bytes 176160 | tf_op jit(solution)/shard_map/ppermute | solution.py:20
  26.3 1.4 %collective-permute-done.6.refs_0_ = bf16[288,128]{1,0:T(8,128)(2,1)S(1)} collective-permute-done((bf16[288,128]{1,0:T(8,128)(2,1)S(1)}, bf16[288,128]{1,0:T(8,128)(2,1)S(1)}, u32[]{:S(2)}, u32[]{:S(2)}) %collective-permute-start.6) | collective-permute-done | bytes 73760 | tf_op jit(solution)/shard_map/ppermute | solution.py:20
  27.7 1.3 %collective-permute-done.8.refs_2_ = bf16[288,128]{1,0:T(8,128)(2,1)S(1)} collective-permute-done((bf16[288,128]{1,0:T(8,128)(2,1)S(1)}, bf16[288,128]{1,0:T(8,128)(2,1)S(1)}, u32[]{:S(2)}, u32[]{:S(2)}) %collective-permute-start.8) | collective-permute-done | bytes 73760 | tf_op jit(solution)/shard_map/ppermute | solution.py:20
  29.4 2.6 %collective-permute-start.11 = (bf16[256,128]{1,0:T(8,128)(2,1)S(1)}, bf16[256,128]{1,0:T(8,128)(2,1)S(1)}, u32[]{:S(2)}, u32[]{:S(2)}) collective-permute-start(bf16[256,128]{1,0:T(8,128)(2,1)S(1)} %get-tuple-element.45.refs_3_.refs_0_), channel_id=1, source_target_pairs={{0,24},{8,16},{16,8},{24,0},{1,25},{9,17},{17,9},{25,1},{2,26},{10... | collective-permute-start | bytes 196616 | tf_op jit(solution)/shard_map/ppermute | solution.py:20
  32.0 1.0 %collective-permute-start.10 = (bf16[256,128]{1,0:T(8,128)(2,1)S(1)}, bf16[256,128]{1,0:T(8,128)(2,1)S(1)}, u32[]{:S(2)}, u32[]{:S(2)}) collective-permute-start(bf16[256,128]{1,0:T(8,128)(2,1)S(1)} %get-tuple-element.45.refs_3_.refs_0_), channel_id=1, source_target_pairs={{0,16},{8,24},{16,0},{24,8},{1,17},{9,25},{17,1},{25,9},{2,18},{10... | collective-permute-start | bytes 196616 | tf_op jit(solution)/shard_map/ppermute | solution.py:20
  33.3 1.5 %collective-permute-done.11.refs_6_.refs_3_ = bf16[256,128]{1,0:T(8,128)(2,1)S(1)} collective-permute-done((bf16[256,128]{1,0:T(8,128)(2,1)S(1)}, bf16[256,128]{1,0:T(8,128)(2,1)S(1)}, u32[]{:S(2)}, u32[]{:S(2)}) %collective-permute-start.11) | collective-permute-done | bytes 65568 | tf_op jit(solution)/shard_map/ppermute | solution.py:20
  34.8 1.5 %collective-permute-done.10.refs_5_.refs_2_ = bf16[256,128]{1,0:T(8,128)(2,1)S(1)} collective-permute-done((bf16[256,128]{1,0:T(8,128)(2,1)S(1)}, bf16[256,128]{1,0:T(8,128)(2,1)S(1)}, u32[]{:S(2)}, u32[]{:S(2)}) %collective-permute-start.10) | collective-permute-done | bytes 65568 | tf_op jit(solution)/shard_map/ppermute | solution.py:20
  36.2 1.0 %collective-permute-done.9.refs_4_.refs_1_ = bf16[256,128]{1,0:T(8,128)(2,1)S(1)} collective-permute-done((bf16[256,128]{1,0:T(8,128)(2,1)S(1)}, bf16[256,128]{1,0:T(8,128)(2,1)S(1)}, u32[]{:S(2)}, u32[]{:S(2)}) %collective-permute-start.9) | collective-permute-done | bytes 65568 | tf_op jit(solution)/shard_map/ppermute | solution.py:20
  37.3 4.2 %gradients.1 = (f32[96,256]{1,0:T(8,128)S(1)}, bf16[96,256]{1,0:T(8,128)(2,1)S(1)}, bf16[96,256]{1,0:T(8,128)(2,1)S(1)}, bf16[96,256]{1,0:T(8,128)(2,1)S(1)}) custom-call(s32[2]{0:T(128)S(1)} %pad_add_fusion.refs_0_.place_ref, bf16[2048,1024]{1,0:T(8,128)(2,1)S(1)} %get-tuple-element.34.dense_ref.refs_1_, ...), custom_call_target="tpu_custom_call" | custom-call | tf_op jit(solution)/shard_map/gradients/pallas_call | solution.py:27
  41.5 1.1 %collective-permute-start.14 = (bf16[96,256]{1,0:T(8,128)(2,1)S(1)}, bf16[96,256]{1,0:T(8,128)(2,1)S(1)}, u32[]{:S(2)}, u32[]{:S(2)}) collective-permute-start(bf16[96,256]{1,0:T(8,128)(2,1)S(1)} %get-tuple-element.50), channel_id=1, source_target_pairs={{0,8},{8,0},{16,24},{24,16},{1,9},{9,1},{17,25},{25,17},{2,10},{10... | collective-permute-start | bytes 147464 | tf_op jit(solution)/shard_map/ppermute | solution.py:20
  42.6 1.2 %collective-permute-start.15 = (bf16[96,256]{1,0:T(8,128)(2,1)S(1)}, bf16[96,256]{1,0:T(8,128)(2,1)S(1)}, u32[]{:S(2)}, u32[]{:S(2)}) collective-permute-start(bf16[96,256]{1,0:T(8,128)(2,1)S(1)} %get-tuple-element.51), channel_id=1, source_target_pairs={{0,16},{8,24},{16,0},{24,8},{1,17},{9,25},{17,1},{25,9},{2,18},{10... | collective-permute-start | bytes 147464 | tf_op jit(solution)/shard_map/ppermute | solution.py:20
  43.8 1.2 %collective-permute-start.16 = (bf16[96,256]{1,0:T(8,128)(2,1)S(1)}, bf16[96,256]{1,0:T(8,128)(2,1)S(1)}, u32[]{:S(2)}, u32[]{:S(2)}) collective-permute-start(bf16[96,256]{1,0:T(8,128)(2,1)S(1)} %get-tuple-element.52), channel_id=1, source_target_pairs={{0,24},{8,16},{16,8},{24,0},{1,25},{9,17},{17,9},{25,1},{2,26},{10... | collective-permute-start | bytes 147464 | tf_op jit(solution)/shard_map/ppermute | solution.py:20
  45.0 2.7 %second_product.1 = (bf16[4,176,256]{2,1,0:T(8,128)(2,1)S(1)}, f32[4,176,256]{2,1,0:T(8,128)S(1)}) custom-call(bf16[2048,1024]{1,0:T(8,128)(2,1)S(1)} %get-tuple-element.34.dense_ref.refs_1_, f32[96,256]{1,0:T(8,128)S(1)} %get-tuple-element.47.after_ref, bf16[256,128]{1,0:T(8,128)(2,1)S(1)} %get-tuple-element.45.refs_3_.refs_0_, ...), custom_call_target="tpu_custom_call" | custom-call | tf_op jit(solution)/shard_map/second_product/pallas_call | solution.py:27
  48.9 1.3 %collective-permute-done.17.far_ref = f32[96,256]{1,0:T(8,128)S(1)} collective-permute-done((f32[96,256]{1,0:T(8,128)S(1)}, f32[96,256]{1,0:T(8,128)S(1)}, u32[]{:S(2)}, u32[]{:S(2)}) %collective-permute-start.17) | collective-permute-done | bytes 98336 | tf_op jit(solution)/shard_map/ppermute | solution.py:20
  50.3 3.0 %collective-permute-start.23 = (bf16[96,256]{1,0:T(8,128)(2,1)S(1)}, bf16[96,256]{1,0:T(8,128)(2,1)S(1)}, u32[]{:S(2)}, u32[]{:S(2)}) collective-permute-start(bf16[96,256]{1,0:T(8,128)(2,1)S(1)} %get-tuple-element.57), channel_id=1, source_target_pairs={{0,6},{1,7},{2,4},{3,5},{4,2},{5,3},{6,0},{7,1},{8,14},{9,15},{10,... | collective-permute-start | bytes 147464 | tf_op jit(solution)/shard_map/ppermute | solution.py:20
  53.3 1.4 %collective-permute-start.21 = (bf16[96,256]{1,0:T(8,128)(2,1)S(1)}, bf16[96,256]{1,0:T(8,128)(2,1)S(1)}, u32[]{:S(2)}, u32[]{:S(2)}) collective-permute-start(bf16[96,256]{1,0:T(8,128)(2,1)S(1)} %get-tuple-element.57), channel_id=1, source_target_pairs={{0,2},{1,3},{2,0},{3,1},{4,6},{5,7},{6,4},{7,5},{8,10},{9,11},{10,... | collective-permute-start | bytes 147464 | tf_op jit(solution)/shard_map/ppermute | solution.py:20
  55.3 2.9 %collective-permute-start.19 = (bf16[176,256]{1,0:T(8,128)(2,1)S(1)}, bf16[176,256]{1,0:T(8,128)(2,1)S(1)}, u32[]{:S(2)}, u32[]{:S(2)}) collective-permute-start(bf16[176,256]{1,0:T(8,128)(2,1)S(1)} %get-tuple-element.55), channel_id=1, source_target_pairs={{0,4},{1,5},{2,6},{3,7},{4,0},{5,1},{6,2},{7,3},{8,12},{9,13},{10,... | collective-permute-start | bytes 270344 | tf_op jit(solution)/shard_map/ppermute | solution.py:20
  58.3 1.5 %collective-permute-start.20 = (bf16[176,256]{1,0:T(8,128)(2,1)S(1)}, bf16[176,256]{1,0:T(8,128)(2,1)S(1)}, u32[]{:S(2)}, u32[]{:S(2)}) collective-permute-start(bf16[176,256]{1,0:T(8,128)(2,1)S(1)} %get-tuple-element.56), channel_id=1, source_target_pairs={{0,6},{1,7},{2,4},{3,5},{4,2},{5,3},{6,0},{7,1},{8,14},{9,15},{10,... | collective-permute-start | bytes 270344 | tf_op jit(solution)/shard_map/ppermute | solution.py:20
  60.0 1.3 %collective-permute-start.26 = (bf16[96,256]{1,0:T(8,128)(2,1)S(1)}, bf16[96,256]{1,0:T(8,128)(2,1)S(1)}, u32[]{:S(2)}, u32[]{:S(2)}) collective-permute-start(bf16[96,256]{1,0:T(8,128)(2,1)S(1)} %add_convert_fusion.refs_3_), channel_id=1, source_target_pairs={{0,24},{8,16},{16,8},{24,0},{1,25},{9,17},{17,9},{25,1},{2,26},{10... | collective-permute-start | bytes 147464 | tf_op jit(solution)/shard_map/ppermute | solution.py:20
  61.3 1.3 %collective-permute-start.25 = (bf16[96,256]{1,0:T(8,128)(2,1)S(1)}, bf16[96,256]{1,0:T(8,128)(2,1)S(1)}, u32[]{:S(2)}, u32[]{:S(2)}) collective-permute-start(bf16[96,256]{1,0:T(8,128)(2,1)S(1)} %add_convert_fusion.refs_3_), channel_id=1, source_target_pairs={{0,16},{8,24},{16,0},{24,8},{1,17},{9,25},{17,1},{25,9},{2,18},{10... | collective-permute-start | bytes 147464 | tf_op jit(solution)/shard_map/ppermute | solution.py:20
  62.5 1.0 %collective-permute-start.24 = (bf16[96,256]{1,0:T(8,128)(2,1)S(1)}, bf16[96,256]{1,0:T(8,128)(2,1)S(1)}, u32[]{:S(2)}, u32[]{:S(2)}) collective-permute-start(bf16[96,256]{1,0:T(8,128)(2,1)S(1)} %add_convert_fusion.refs_3_), channel_id=1, source_target_pairs={{0,8},{8,0},{16,24},{24,16},{1,9},{9,1},{17,25},{25,17},{2,10},{10... | collective-permute-start | bytes 147464 | tf_op jit(solution)/shard_map/ppermute | solution.py:20
  63.5 1.6 %collective-permute-done.19.refs_1_ = bf16[176,256]{1,0:T(8,128)(2,1)S(1)} collective-permute-done((bf16[176,256]{1,0:T(8,128)(2,1)S(1)}, bf16[176,256]{1,0:T(8,128)(2,1)S(1)}, u32[]{:S(2)}, u32[]{:S(2)}) %collective-permute-start.19) | collective-permute-done | bytes 90144 | tf_op jit(solution)/shard_map/ppermute | solution.py:20
  65.6 1.1 %collective-permute-done.24.refs_4_ = bf16[96,256]{1,0:T(8,128)(2,1)S(1)} collective-permute-done((bf16[96,256]{1,0:T(8,128)(2,1)S(1)}, bf16[96,256]{1,0:T(8,128)(2,1)S(1)}, u32[]{:S(2)}, u32[]{:S(2)}) %collective-permute-start.24) | collective-permute-done | bytes 49184 | tf_op jit(solution)/shard_map/ppermute | solution.py:20
  66.6 1.5 %results.1 = (bf16[172,256]{1,0:T(8,128)(2,1)}, f32[128,256]{1,0:T(8,128)}, f32[1,256]{1,0:T(1,128)}, f32[172,256]{1,0:T(8,128)}, f32[1,172]{1,0:T(1,128)}) custom-call(s32[2]{0:T(128)S(1)} %pad_add_fusion.refs_0_.place_ref, f32[176,256]{1,0:T(8,128)S(1)} %get-tuple-element.53.total_ref, f32[16,128]{1,0:T(8,128)S(1)} %get-tuple-element.44.refs_2_.degree_ref, ...), custom_call_target="tpu_custom_call" | custom-call | tf_op jit(solution)/shard_map/results/pallas_call | solution.py:27
  (48 shorter events, 8.7 us)
Async XLA Ops:
  0.6 36.6 %copy-start.5 = (f32[256]{0:T(256)S(1)}, f32[256]{0:T(256)}, u32[]{:S(2)}) copy-start(f32[256]{0:T(256)} %param.16) | copy-start | bytes 3076
  0.6 13.1 %collective-permute-start.1 = (bf16[172,256]{1,0:T(8,128)(2,1)}, bf16[172,256]{1,0:T(8,128)(2,1)S(1)}, u32[]{:S(2)}, u32[]{:S(2)}) collective-permute-start(bf16[172,256]{1,0:T(8,128)(2,1)} %bitcast.18), channel_id=1, source_target_pairs={{0,4},{1,5},{2,6},{3,7},{4,0},{5,1},{6,2},{7,3},{8,12},{9,13},{10,... | collective-permute-start | bytes 264200 | tf_op jit(solution)/shard_map/ppermute | solution.py:20
  4.7 4.9 %collective-permute-start = (bf16[256,128]{1,0:T(8,128)(2,1)}, bf16[256,128]{1,0:T(8,128)(2,1)S(1)}, u32[]{:S(2)}, u32[]{:S(2)}) collective-permute-start(bf16[256,128]{1,0:T(8,128)(2,1)} %features_ref.1), channel_id=1, source_target_pairs={{0,8},{8,0},{16,24},{24,16},{1,9},{9,1},{17,25},{25,17},{2,10},{10... | collective-permute-start | bytes 196616 | tf_op jit(solution)/shard_map/ppermute | solution.py:20
  6.2 7.5 %collective-permute-start.3 = (bf16[256,128]{1,0:T(8,128)(2,1)}, bf16[256,128]{1,0:T(8,128)(2,1)S(1)}, u32[]{:S(2)}, u32[]{:S(2)}) collective-permute-start(bf16[256,128]{1,0:T(8,128)(2,1)} %features_ref.1), channel_id=1, source_target_pairs={{0,24},{8,16},{16,8},{24,0},{1,25},{9,17},{17,9},{25,1},{2,26},{10... | collective-permute-start | bytes 196616 | tf_op jit(solution)/shard_map/ppermute | solution.py:20
  7.7 6.0 %collective-permute-start.2 = (bf16[256,128]{1,0:T(8,128)(2,1)}, bf16[256,128]{1,0:T(8,128)(2,1)S(1)}, u32[]{:S(2)}, u32[]{:S(2)}) collective-permute-start(bf16[256,128]{1,0:T(8,128)(2,1)} %features_ref.1), channel_id=1, source_target_pairs={{0,16},{8,24},{16,0},{24,8},{1,17},{9,25},{17,1},{25,9},{2,18},{10... | collective-permute-start | bytes 196616 | tf_op jit(solution)/shard_map/ppermute | solution.py:20
  9.6 1.4 %copy-start = (bf16[1,1,48,128,128]{4,3,2,1,0:T(8,128)(2,1)S(1)}, bf16[1,1,48,128,128]{4,3,2,1,0:T(8,128)(2,1)}, u32[]{:S(2)}) copy-start(bf16[1,1,48,128,128]{4,3,2,1,0:T(8,128)(2,1)} %param.11) | copy-start | bytes 4718596
  11.0 26.2 %copy-start.1 = (bf16[256,172]{0,1:T(8,128)(2,1)S(1)}, bf16[256,172]{0,1:T(8,128)(2,1)}, u32[]{:S(2)}) copy-start(bf16[256,172]{0,1:T(8,128)(2,1)} %param.17) | copy-start | bytes 264196
  11.1 26.2 %copy-start.2 = (bf16[128,256]{1,0:T(8,128)(2,1)S(1)}, bf16[128,256]{1,0:T(8,128)(2,1)}, u32[]{:S(2)}) copy-start(bf16[128,256]{1,0:T(8,128)(2,1)} %refs_4_.1) | copy-start | bytes 196612
  17.3 1.6 %collective-permute-start.4 = (bf16[1056,128]{1,0:T(8,128)(2,1)S(1)}, bf16[1056,128]{1,0:T(8,128)(2,1)S(1)}, u32[]{:S(2)}, u32[]{:S(2)}) collective-permute-start(bf16[1056,128]{1,0:T(8,128)(2,1)S(1)} %get-tuple-element.37), channel_id=1, source_target_pairs={{0,1},{1,0},{2,3},{3,2},{4,5},{5,4},{6,7},{7,6},{8,9},{9,8},{10,11... | collective-permute-start | bytes 811016 | tf_op jit(solution)/shard_map/ppermute | solution.py:20
  17.3 9.0 %collective-permute-start.5 = (bf16[2,172,256]{2,1,0:T(8,128)(2,1)S(1)}, bf16[2,172,256]{2,1,0:T(8,128)(2,1)S(1)}, u32[]{:S(2)}, u32[]{:S(2)}) collective-permute-start(bf16[2,172,256]{2,1,0:T(8,128)(2,1)S(1)} %get-tuple-element.40.left_ref), channel_id=1, source_target_pairs={{0,2},{1,3},{2,0},{3,1},{4,6},{5,7},{6,4},{7,5},{8,10},{9,11},{10,... | collective-permute-start | bytes 528392 | tf_op jit(solution)/shard_map/ppermute | solution.py:20
  18.9 8.8 %collective-permute-start.6 = (bf16[288,128]{1,0:T(8,128)(2,1)S(1)}, bf16[288,128]{1,0:T(8,128)(2,1)S(1)}, u32[]{:S(2)}, u32[]{:S(2)}) collective-permute-start(bf16[288,128]{1,0:T(8,128)(2,1)S(1)} %get-tuple-element.41), channel_id=1, source_target_pairs={{0,2},{1,3},{2,0},{3,1},{4,6},{5,7},{6,4},{7,5},{8,10},{9,11},{10,... | collective-permute-start | bytes 221192 | tf_op jit(solution)/shard_map/ppermute | solution.py:20
  19.9 7.8 %collective-permute-start.7 = (bf16[288,128]{1,0:T(8,128)(2,1)S(1)}, bf16[288,128]{1,0:T(8,128)(2,1)S(1)}, u32[]{:S(2)}, u32[]{:S(2)}) collective-permute-start(bf16[288,128]{1,0:T(8,128)(2,1)S(1)} %get-tuple-element.42), channel_id=1, source_target_pairs={{0,4},{1,5},{2,6},{3,7},{4,0},{5,1},{6,2},{7,3},{8,12},{9,13},{10,... | collective-permute-start | bytes 221192 | tf_op jit(solution)/shard_map/ppermute | solution.py:20
  21.2 7.8 %collective-permute-start.8 = (bf16[288,128]{1,0:T(8,128)(2,1)S(1)}, bf16[288,128]{1,0:T(8,128)(2,1)S(1)}, u32[]{:S(2)}, u32[]{:S(2)}) collective-permute-start(bf16[288,128]{1,0:T(8,128)(2,1)S(1)} %get-tuple-element.43), channel_id=1, source_target_pairs={{0,6},{1,7},{2,4},{3,5},{4,2},{5,3},{6,0},{7,1},{8,14},{9,15},{10,... | collective-permute-start | bytes 221192 | tf_op jit(solution)/shard_map/ppermute | solution.py:20
  29.3 8.0 %collective-permute-start.12 = (bf16[4,172,256]{2,1,0:T(8,128)(2,1)S(1)}, bf16[4,172,256]{2,1,0:T(8,128)(2,1)S(1)}, u32[]{:S(2)}, u32[]{:S(2)}) collective-permute-start(bf16[4,172,256]{2,1,0:T(8,128)(2,1)S(1)} %get-tuple-element.46.refs_7_), channel_id=1, source_target_pairs={{0,1},{1,0},{2,3},{3,2},{4,5},{5,4},{6,7},{7,6},{8,9},{9,8},{10,11... | collective-permute-start | bytes 1056776 | tf_op jit(solution)/shard_map/ppermute | solution.py:20
  29.4 5.4 %collective-permute-start.11 = (bf16[256,128]{1,0:T(8,128)(2,1)S(1)}, bf16[256,128]{1,0:T(8,128)(2,1)S(1)}, u32[]{:S(2)}, u32[]{:S(2)}) collective-permute-start(bf16[256,128]{1,0:T(8,128)(2,1)S(1)} %get-tuple-element.45.refs_3_.refs_0_), channel_id=1, source_target_pairs={{0,24},{8,16},{16,8},{24,0},{1,25},{9,17},{17,9},{25,1},{2,26},{10... | collective-permute-start | bytes 196616 | tf_op jit(solution)/shard_map/ppermute | solution.py:20
  32.0 4.3 %collective-permute-start.10 = (bf16[256,128]{1,0:T(8,128)(2,1)S(1)}, bf16[256,128]{1,0:T(8,128)(2,1)S(1)}, u32[]{:S(2)}, u32[]{:S(2)}) collective-permute-start(bf16[256,128]{1,0:T(8,128)(2,1)S(1)} %get-tuple-element.45.refs_3_.refs_0_), channel_id=1, source_target_pairs={{0,16},{8,24},{16,0},{24,8},{1,17},{9,25},{17,1},{25,9},{2,18},{10... | collective-permute-start | bytes 196616 | tf_op jit(solution)/shard_map/ppermute | solution.py:20
  33.0 4.3 %collective-permute-start.9 = (bf16[256,128]{1,0:T(8,128)(2,1)S(1)}, bf16[256,128]{1,0:T(8,128)(2,1)S(1)}, u32[]{:S(2)}, u32[]{:S(2)}) collective-permute-start(bf16[256,128]{1,0:T(8,128)(2,1)S(1)} %get-tuple-element.45.refs_3_.refs_0_), channel_id=1, source_target_pairs={{0,8},{8,0},{16,24},{24,16},{1,9},{9,1},{17,25},{25,17},{2,10},{10... | collective-permute-start | bytes 196616 | tf_op jit(solution)/shard_map/ppermute | solution.py:20
  41.4 25.2 %copy-start.6 = (f32[172]{0:T(256)S(1)}, f32[172]{0:T(256)}, u32[]{:S(2)}) copy-start(f32[172]{0:T(256)} %param.18) | copy-start | bytes 2068
  41.5 6.4 %collective-permute-start.14 = (bf16[96,256]{1,0:T(8,128)(2,1)S(1)}, bf16[96,256]{1,0:T(8,128)(2,1)S(1)}, u32[]{:S(2)}, u32[]{:S(2)}) collective-permute-start(bf16[96,256]{1,0:T(8,128)(2,1)S(1)} %get-tuple-element.50), channel_id=1, source_target_pairs={{0,8},{8,0},{16,24},{24,16},{1,9},{9,1},{17,25},{25,17},{2,10},{10... | collective-permute-start | bytes 147464 | tf_op jit(solution)/shard_map/ppermute | solution.py:20
  42.6 5.3 %collective-permute-start.15 = (bf16[96,256]{1,0:T(8,128)(2,1)S(1)}, bf16[96,256]{1,0:T(8,128)(2,1)S(1)}, u32[]{:S(2)}, u32[]{:S(2)}) collective-permute-start(bf16[96,256]{1,0:T(8,128)(2,1)S(1)} %get-tuple-element.51), channel_id=1, source_target_pairs={{0,16},{8,24},{16,0},{24,8},{1,17},{9,25},{17,1},{25,9},{2,18},{10... | collective-permute-start | bytes 147464 | tf_op jit(solution)/shard_map/ppermute | solution.py:20
  43.8 5.0 %collective-permute-start.16 = (bf16[96,256]{1,0:T(8,128)(2,1)S(1)}, bf16[96,256]{1,0:T(8,128)(2,1)S(1)}, u32[]{:S(2)}, u32[]{:S(2)}) collective-permute-start(bf16[96,256]{1,0:T(8,128)(2,1)S(1)} %get-tuple-element.52), channel_id=1, source_target_pairs={{0,24},{8,16},{16,8},{24,0},{1,25},{9,17},{17,9},{25,1},{2,26},{10... | collective-permute-start | bytes 147464 | tf_op jit(solution)/shard_map/ppermute | solution.py:20
  47.7 2.4 %collective-permute-start.13 = (bf16[4,176,256]{2,1,0:T(8,128)(2,1)S(1)}, bf16[4,176,256]{2,1,0:T(8,128)(2,1)S(1)}, u32[]{:S(2)}, u32[]{:S(2)}) collective-permute-start(bf16[4,176,256]{2,1,0:T(8,128)(2,1)S(1)} %get-tuple-element.49), channel_id=1, source_target_pairs={{0,1},{1,0},{2,3},{3,2},{4,5},{5,4},{6,7},{7,6},{8,9},{9,8},{10,11... | collective-permute-start | bytes 1081352 | tf_op jit(solution)/shard_map/ppermute | solution.py:20
  48.8 1.4 %collective-permute-start.17 = (f32[96,256]{1,0:T(8,128)S(1)}, f32[96,256]{1,0:T(8,128)S(1)}, u32[]{:S(2)}, u32[]{:S(2)}) collective-permute-start(f32[96,256]{1,0:T(8,128)S(1)} %convert_add_fusion.mine_ref), channel_id=1, source_target_pairs={{0,1},{1,0},{2,3},{3,2},{4,5},{5,4},{6,7},{7,6},{8,9},{9,8},{10,11... | collective-permute-start | bytes 294920 | tf_op jit(solution)/shard_map/ppermute | solution.py:20
  50.3 8.0 %collective-permute-start.23 = (bf16[96,256]{1,0:T(8,128)(2,1)S(1)}, bf16[96,256]{1,0:T(8,128)(2,1)S(1)}, u32[]{:S(2)}, u32[]{:S(2)}) collective-permute-start(bf16[96,256]{1,0:T(8,128)(2,1)S(1)} %get-tuple-element.57), channel_id=1, source_target_pairs={{0,6},{1,7},{2,4},{3,5},{4,2},{5,3},{6,0},{7,1},{8,14},{9,15},{10,... | collective-permute-start | bytes 147464 | tf_op jit(solution)/shard_map/ppermute | solution.py:20
  53.3 6.5 %collective-permute-start.22 = (bf16[96,256]{1,0:T(8,128)(2,1)S(1)}, bf16[96,256]{1,0:T(8,128)(2,1)S(1)}, u32[]{:S(2)}, u32[]{:S(2)}) collective-permute-start(bf16[96,256]{1,0:T(8,128)(2,1)S(1)} %get-tuple-element.57), channel_id=1, source_target_pairs={{0,4},{1,5},{2,6},{3,7},{4,0},{5,1},{6,2},{7,3},{8,12},{9,13},{10,... | collective-permute-start | bytes 147464 | tf_op jit(solution)/shard_map/ppermute | solution.py:20
  53.3 6.7 %collective-permute-start.21 = (bf16[96,256]{1,0:T(8,128)(2,1)S(1)}, bf16[96,256]{1,0:T(8,128)(2,1)S(1)}, u32[]{:S(2)}, u32[]{:S(2)}) collective-permute-start(bf16[96,256]{1,0:T(8,128)(2,1)S(1)} %get-tuple-element.57), channel_id=1, source_target_pairs={{0,2},{1,3},{2,0},{3,1},{4,6},{5,7},{6,4},{7,5},{8,10},{9,11},{10,... | collective-permute-start | bytes 147464 | tf_op jit(solution)/shard_map/ppermute | solution.py:20
  54.7 7.8 %collective-permute-start.18 = (bf16[176,256]{1,0:T(8,128)(2,1)S(1)}, bf16[176,256]{1,0:T(8,128)(2,1)S(1)}, u32[]{:S(2)}, u32[]{:S(2)}) collective-permute-start(bf16[176,256]{1,0:T(8,128)(2,1)S(1)} %get-tuple-element.54), channel_id=1, source_target_pairs={{0,2},{1,3},{2,0},{3,1},{4,6},{5,7},{6,4},{7,5},{8,10},{9,11},{10,... | collective-permute-start | bytes 270344 | tf_op jit(solution)/shard_map/ppermute | solution.py:20
  55.3 9.8 %collective-permute-start.19 = (bf16[176,256]{1,0:T(8,128)(2,1)S(1)}, bf16[176,256]{1,0:T(8,128)(2,1)S(1)}, u32[]{:S(2)}, u32[]{:S(2)}) collective-permute-start(bf16[176,256]{1,0:T(8,128)(2,1)S(1)} %get-tuple-element.55), channel_id=1, source_target_pairs={{0,4},{1,5},{2,6},{3,7},{4,0},{5,1},{6,2},{7,3},{8,12},{9,13},{10,... | collective-permute-start | bytes 270344 | tf_op jit(solution)/shard_map/ppermute | solution.py:20
  58.3 6.9 %collective-permute-start.20 = (bf16[176,256]{1,0:T(8,128)(2,1)S(1)}, bf16[176,256]{1,0:T(8,128)(2,1)S(1)}, u32[]{:S(2)}, u32[]{:S(2)}) collective-permute-start(bf16[176,256]{1,0:T(8,128)(2,1)S(1)} %get-tuple-element.56), channel_id=1, source_target_pairs={{0,6},{1,7},{2,4},{3,5},{4,2},{5,3},{6,0},{7,1},{8,14},{9,15},{10,... | collective-permute-start | bytes 270344 | tf_op jit(solution)/shard_map/ppermute | solution.py:20
  60.0 5.2 %collective-permute-start.26 = (bf16[96,256]{1,0:T(8,128)(2,1)S(1)}, bf16[96,256]{1,0:T(8,128)(2,1)S(1)}, u32[]{:S(2)}, u32[]{:S(2)}) collective-permute-start(bf16[96,256]{1,0:T(8,128)(2,1)S(1)} %add_convert_fusion.refs_3_), channel_id=1, source_target_pairs={{0,24},{8,16},{16,8},{24,0},{1,25},{9,17},{17,9},{25,1},{2,26},{10... | collective-permute-start | bytes 147464 | tf_op jit(solution)/shard_map/ppermute | solution.py:20
  61.3 4.3 %collective-permute-start.25 = (bf16[96,256]{1,0:T(8,128)(2,1)S(1)}, bf16[96,256]{1,0:T(8,128)(2,1)S(1)}, u32[]{:S(2)}, u32[]{:S(2)}) collective-permute-start(bf16[96,256]{1,0:T(8,128)(2,1)S(1)} %add_convert_fusion.refs_3_), channel_id=1, source_target_pairs={{0,16},{8,24},{16,0},{24,8},{1,17},{9,25},{17,1},{25,9},{2,18},{10... | collective-permute-start | bytes 147464 | tf_op jit(solution)/shard_map/ppermute | solution.py:20
  62.5 4.1 %collective-permute-start.24 = (bf16[96,256]{1,0:T(8,128)(2,1)S(1)}, bf16[96,256]{1,0:T(8,128)(2,1)S(1)}, u32[]{:S(2)}, u32[]{:S(2)}) collective-permute-start(bf16[96,256]{1,0:T(8,128)(2,1)S(1)} %add_convert_fusion.refs_3_), channel_id=1, source_target_pairs={{0,8},{8,0},{16,24},{24,16},{1,9},{9,1},{17,25},{25,17},{2,10},{10... | collective-permute-start | bytes 147464 | tf_op jit(solution)/shard_map/ppermute | solution.py:20
  (2 other events, 1.7 us)

commit v4 on v3

--- a/solution.py
+++ b/solution.py
@@ -1,4 +1,5 @@
 import functools
+import math
 
 import jax
 import jax.numpy as jnp
@@ -10,9 +11,10 @@
 BF16 = jnp.bfloat16
 F32 = jnp.float32
 LANES = 128
-SMEM = pl.BlockSpec(memory_space=pltpu.SMEM)
+GRANT = 820 << 16
 VMEM = pl.BlockSpec(memory_space=pltpu.VMEM)
 ANY = pl.BlockSpec(memory_space=pl.ANY)
+HBM = pl.BlockSpec(memory_space=pltpu.HBM)
 
 
 def exchange(value, axis, mask):
@@ -20,17 +22,16 @@
     return lax.ppermute(value, axis, [(i, i ^ mask) for i in range(count)])
 
 
-def call(kernel, name, outs, in_specs, args, scratch=()):
-    size = sum(a.size * a.dtype.itemsize for a in args)
-    size += sum(o.size * o.dtype.itemsize for o in outs)
-    grant = size + (6 << 20)
+def call(kernel, name, outs, in_specs, args, scratch=(), grant=None):
+    size = sum(math.prod(a.shape) * a.dtype.itemsize for a in [*args, *outs])
+    grant = min(size + (6 << 20), 60 << 20) if grant is None else grant
     return pl.pallas_call(
         kernel,
         out_shape=tuple(outs),
         in_specs=in_specs,
         out_specs=tuple(VMEM for _ in outs),
         scratch_shapes=scratch,
-        compiler_params=pltpu.CompilerParams(vmem_limit_bytes=min(grant, 60 << 20)),
+        compiler_params=pltpu.CompilerParams(vmem_limit_bytes=grant),
         name=name,
     )(*args)
 
@@ -48,39 +49,58 @@
     return high, (value - high.astype(F32)).astype(BF16)
 
 
-def dense_kernel(own, index_ref, tiles_ref, after_ref, dense_ref, degree_ref):
-    slots, block, _ = tiles_ref.shape
+def dense_kernel(own, row_hbm, col_hbm, live_hbm, tiles_hbm, features_hbm, g_hbm, next_hbm, *refs):
+    dense_ref, degree_ref, held_ref, g_ref, row_ref, col_ref, live_ref, tiles_ref, done = refs
+    pairs = (
+        (row_hbm, row_ref),
+        (col_hbm, col_ref),
+        (live_hbm, live_ref),
+        (tiles_hbm, tiles_ref),
+        (features_hbm, held_ref.at[0]),
+        (next_hbm, held_ref.at[1]),
+        (g_hbm, g_ref),
+    )
+    copies = [pltpu.make_async_copy(a, b, done.at[n]) for n, (a, b) in enumerate(pairs)]
+    for copy in copies:
+        copy.start()
+    block = tiles_ref.shape[-1]
     rows, columns = dense_ref.shape
     half = rows // (block * own * 2)
-    r, c = index_ref[2 * slots + 1], index_ref[2 * slots + 2]
+    r, c = lax.axis_index("row"), lax.axis_index("col")
     dense_ref[...] = jnp.zeros_like(dense_ref)
-
-    @pl.loop(0, index_ref[2 * slots])
+    for copy in copies[:4]:
+        copy.wait()
+
+    @pl.loop(0, live_ref[0, 0])
     def _(slot):
-        k = index_ref[slot]
-        j = index_ref[slots + slot]
+        k = row_ref[0, 0, slot]
+        j = col_ref[0, 0, slot]
         p = (k // own) ^ c
         at_row = ((p & 1) * half + (p >> 1)) * own + k % own
         at_col = ((j // own) ^ r) * own + j % own
         dense_ref[
             pl.ds(pl.multiple_of(at_row * block, block), block),
             pl.ds(pl.multiple_of(at_col * block, block), block),
-        ] = tiles_ref[slot]
+        ] = tiles_ref[0, 0, slot]
 
     ones = jnp.ones((8, columns), BF16)
     for start in range(0, rows, 2 * block):
         sums = product(ones, dense_ref[pl.ds(start, 2 * block), :], ((1,), (1,)))
         for part in range(2):
             degree_ref[pl.ds(start // block + part, 1), :] = sums[:1, part * block : (part + 1) * block]
-
-
-def first_kernel(spans, dense_ref, degree_ref, g_ref, far_ref, *refs):
-    pieces, (send_ref, keep_ref, pair_ref, held) = refs[:spans], refs[spans:]
+    for copy in copies[4:]:
+        copy.wait()
+
+
+def first_kernel(spans, dense_ref, degree_ref, g_ref, far_ref, pair_in_ref, *refs):
+    pieces, (send_ref, keep_ref, pair_ref, held) = refs[: spans - 2], refs[spans - 2 :]
     pair_ref[0] = g_ref[...]
     pair_ref[1] = far_ref[...]
-    nodes = pieces[0].shape[0]
-    for s in range(spans):
-        held[pl.ds(s * nodes, nodes), :] = pieces[s][...]
+    nodes = g_ref.shape[1]
+    held[pl.ds(0, nodes), :] = pair_in_ref[0]
+    held[pl.ds(nodes, nodes), :] = pair_in_ref[1]
+    for s in range(2, spans):
+        held[pl.ds(s * nodes, nodes), :] = pieces[s - 2][...]
     half = keep_ref.shape[0] // nodes
     blocks = degree_ref.shape[0]
     high, low = split(degree_ref[...])
@@ -118,11 +138,11 @@
     return jnp.concatenate([value[q * own : (q + 1) * own] for q in order], axis=0)
 
 
-def agg_kernel(half, near_ref, part_ref, features_ref, left_ref, right_ref, *refs):
+def agg_kernel(half, near_ref, part_ref, held_ref, left_ref, right_ref, *refs):
     got, (agg_ref, degree_ref, joined_ref) = refs[: half - 1], refs[half - 1 :]
     joined_ref[: half // 2] = left_ref[...]
     joined_ref[half // 2 :] = right_ref[...]
-    nodes = features_ref.shape[0]
+    nodes = held_ref.shape[1]
     block = LANES
     blocks = degree_ref.shape[0]
     total = near_ref[...]
@@ -134,7 +154,7 @@
     degree = 1.0 + degree
     degree_ref[...] = degree
     upright = degree.T
-    total = total + features_ref[...].astype(F32)
+    total = total + held_ref[0].astype(F32)
     for b in range(nodes // block):
         at = slice(b * block, (b + 1) * block)
         agg_ref[at, :] = (total[at] / upright[:, b : b + 1]).astype(BF16)
@@ -154,49 +174,46 @@
     return value, slope
 
 
-def second_kernel(spans, dense_ref, after_ref, *refs):
-    pieces, refs = refs[:spans], refs[spans:]
-    w1_ref, b1_ref, w2_ref, send_ref, keep_ref, held = refs
-    nodes = pieces[0].shape[0]
-    half, tall, _ = keep_ref.shape
-    classes = w2_ref.shape[0]
-    for s in range(spans):
-        value, _ = gelu_parts(product(pieces[s][...], w1_ref[...]) + b1_ref[...])
-        hidden = product(w2_ref[...], value.astype(BF16), ((1,), (1,)))
-        if tall > classes:
-            hidden = jnp.concatenate([hidden, jnp.zeros((tall - classes, nodes), F32)], axis=0)
-        held[:, s * nodes : (s + 1) * nodes] = hidden.astype(BF16)
-        if s == 0:
-            first = hidden
+def second_kernel(dense_ref, hidden_ref, first_ref, after_ref, send_ref, keep_ref):
+    half, _, nodes = keep_ref.shape
 
     @pl.loop(0, half)
     def _(s):
         at = pl.multiple_of((half + s) * nodes, nodes)
-        send_ref[s] = product(held[...], dense_ref[pl.ds(at, nodes), :], ((1,), (1,))).astype(BF16)
+        send_ref[s] = product(hidden_ref[...], dense_ref[pl.ds(at, nodes), :], ((1,), (1,))).astype(BF16)
         at = pl.multiple_of(s * nodes, nodes)
-        keep_ref[s] = product(held[...], dense_ref[pl.ds(at, nodes), :], ((1,), (1,)))
-
-    keep_ref[0] += first
-
-
-def grad_kernel(spans, count, place_ref, dense_ref, degree_ref, *refs):
-    pieces, refs = refs[:spans], refs[spans:]
-    cots, refs = refs[:count], refs[count:]
-    w1_ref, b1_ref, w2_ref, mine_ref, refs = refs[0], refs[1], refs[2], refs[3], refs[4:]
-    sends, turned, total = refs[: spans - 1], refs[-2], refs[-1]
-    fin, hidden = w1_ref.shape
-    block = LANES
+        keep_ref[s] = product(hidden_ref[...], dense_ref[pl.ds(at, nodes), :], ((1,), (1,)))
+
+    keep_ref[0] += first_ref[...]
+
+
+def back_kernel(spans, order, dense_ref, degree_ref, near_ref, other_ref, back_ref, turned):
+    _, classes, nodes = near_ref.shape
     tall = turned.shape[0]
-    rank = place_ref[0]
-    nodes = pieces[0].shape[0]
-    classes = w2_ref.shape[0]
-    for q in range(count):
-        ref, at = cots[q]
+    for q in range(2 * len(order)):
+        source = near_ref if q < len(order) else other_ref
         degree = jnp.concatenate([degree_ref[2 * q : 2 * q + 1, :], degree_ref[2 * q + 1 : 2 * q + 2, :]], axis=1)
-        scaled = (ref[...] if at is None else ref[at]).astype(F32) / degree
+        scaled = source[order.index(q % len(order))].astype(F32) / degree
         if tall > classes:
             scaled = jnp.concatenate([scaled, jnp.zeros((tall - classes, nodes), F32)], axis=0)
         turned[:, q * nodes : (q + 1) * nodes] = scaled.astype(BF16)
+    for s in range(spans):
+        part = product(turned[...], dense_ref[:, s * nodes : (s + 1) * nodes])
+        if s == 0:
+            part = part + turned[:, :nodes].astype(F32)
+        back_ref[s] = part
+
+
+def grad_kernel(spans, back_ref, g_ref, *refs):
+    pieces, refs = refs[:spans], refs[spans:]
+    w1_ref, b1_ref, w2_ref, mine_ref, hidden_ref, first_ref, refs = refs[0], refs[1], refs[2], refs[3], refs[4], refs[5], refs[6:]
+    sends, total = refs[: spans - 1], refs[-1]
+    fin, hidden = w1_ref.shape
+    block = LANES
+    tall = back_ref.shape[1]
+    rank = lax.axis_index("row")
+    nodes = pieces[0].shape[0]
+    classes = w2_ref.shape[0]
     w2 = jnp.concatenate([w2_ref[...].astype(F32), jnp.zeros((2 * block - classes, hidden), F32)], axis=0).astype(BF16)
     grad_w1 = jnp.zeros((fin, hidden), F32)
     grad_w2 = jnp.zeros((tall, hidden), F32)
@@ -204,18 +221,19 @@
     for s in range(spans):
         agg = pieces[s][...]
         value, slope = gelu_parts(product(agg, w1_ref[...]) + b1_ref[...])
-        q = product(turned[...], dense_ref[:, s * nodes : (s + 1) * nodes])
+        h = value.astype(BF16)
+        projected = product(w2, h, ((1,), (1,)))[:tall]
+        hidden_ref[:, s * nodes : (s + 1) * nodes] = projected.astype(BF16)
         if s == 0:
-            q = q + turned[:, :nodes].astype(F32)
+            first_ref[...] = projected
+        q = back_ref[s]
         high, low = split(q)
-        h = value.astype(BF16)
         grad_w2 = grad_w2 + product(high, h) + product(low, h)
         high, low = split(jnp.concatenate([q, jnp.zeros((2 * block - tall, nodes), F32)], axis=0).T)
         d_first = (product(high, w2) + product(low, w2)) * slope
         grad_w1 = grad_w1 + product(agg.astype(F32).T.astype(BF16), d_first.astype(BF16))
         grad_b1 = grad_b1 + jnp.sum(d_first, axis=0, keepdims=True)
-    own = cots[0][0][...] if cots[0][1] is None else cots[0][0][cots[0][1]]
-    grad_b2 = product(jnp.ones((8, nodes), BF16), own, ((1,), (1,)))[:1]
+    grad_b2 = product(jnp.ones((8, nodes), BF16), g_ref[...], ((1,), (1,)))[:1]
     a = fin // spans
     b = total.shape[1] - a - 16
     total[...] = jnp.zeros_like(total)
@@ -238,7 +256,7 @@
         sends[s - 1][...] = (keep_ref[s] + other_ref[s].astype(F32)).astype(BF16)
 
 
-def last_kernel(spans, half, place_ref, total_ref, degree_ref, bias_ref, *refs):
+def last_kernel(spans, half, total_ref, degree_ref, bias_ref, *refs):
     parts, refs = refs[: half - 1], refs[half - 1 :]
     got, (logits_ref, w1_ref, b1_ref, w2_ref, b2_ref, tall_ref) = refs[:spans], refs[spans:]
     total = total_ref[...]
@@ -255,7 +273,7 @@
     a = fin // spans
     b = got[0].shape[0] - a - 16
     for s in range(spans):
-        t = place_ref[0] ^ s
+        t = lax.axis_index("row") ^ s
         share = got[s][...].astype(F32)
         w1_ref[pl.ds(pl.multiple_of(t * a, a), a), :] = share[:a]
         tall_ref[pl.ds(pl.multiple_of(t * b, b), b), :] = share[a : a + b]
@@ -291,8 +309,6 @@
     tall = -(-classes // 16) * 16
     rows, columns = col_count * nodes, row_count * nodes
     blocks = rows // block
-    place = jnp.stack([lax.axis_index("row"), lax.axis_index("col")]).astype(jnp.int32)
-    index = jnp.concatenate([tile_row[0, 0], tile_col[0, 0], tile_live[0], place])
     bias = b_first[None, :]
     w2 = w_second.T
     g_own = grad_logits.T
@@ -305,12 +321,27 @@
         order = order + [s ^ (mask // 2) for s in order]
         mask //= 2
 
-    dense, degree = call(
+    whole = rows * columns * 2 <= 4 << 20
+    keep_in = pltpu.VMEM if whole else shaped
+    dense, degree, held, own_g = call(
         functools.partial(dense_kernel, own),
         "dense_adjacency",
-        [shaped((rows, columns), BF16), shaped((blocks, block), F32)],
-        [SMEM, VMEM, ANY],
-        [index, tiles[0, 0], inputs[1]],
+        [
+            keep_in((rows, columns), BF16),
+            keep_in((blocks, block), F32),
+            keep_in((2, nodes, fin), BF16),
+            keep_in(g_own.shape, BF16),
+        ],
+        [HBM] * 7,
+        [tile_row, tile_col, tile_live, tiles, features, g_own, inputs[1]],
+        scratch=[
+            pltpu.SMEM(tile_row.shape, jnp.int32),
+            pltpu.SMEM(tile_col.shape, jnp.int32),
+            pltpu.SMEM(tile_live.shape, jnp.int32),
+            pltpu.VMEM(tiles.shape, BF16),
+            pltpu.SemaphoreType.DMA((7,)),
+        ],
+        grant=GRANT if whole else 60 << 20,
     )
     send, keep, left = call(
         functools.partial(first_kernel, row_count),
@@ -320,8 +351,8 @@
             shaped((rows // 2, fin), F32),
             shaped((2, classes, nodes), BF16),
         ],
-        [VMEM] * (4 + row_count),
-        [dense, degree, g_own, far_g] + inputs,
+        [VMEM] * (5 + row_count - 2),
+        [dense, degree, own_g, far_g, held] + inputs[2:],
         scratch=[pltpu.VMEM((columns, fin), BF16)],
     )
     other = exchange(send, "col", 1)
@@ -344,37 +375,39 @@
         "first_aggregate",
         [shaped((nodes, fin), BF16), shaped((blocks, block), F32), shaped((half, classes, nodes), BF16)],
         [VMEM] * (5 + half - 1),
-        [out[0], out[1], features, left, right] + got,
+        [out[0], out[1], held, left, right] + got,
     )
     pieces = [agg] + [exchange(agg, "row", s) for s in range(1, row_count)]
     other_g = exchange(near_g, "col", 1)
 
     size = fin // row_count + -(-classes // (16 * row_count)) * 16 + 16
+    back = call(
+        functools.partial(back_kernel, row_count, order),
+        "back_product",
+        [shaped((row_count, tall, nodes), F32)],
+        [VMEM] * 4,
+        [dense, degree, near_g, other_g],
+        scratch=[pltpu.VMEM((tall, rows), BF16)],
+    )[0]
     out = call(
-        lambda *refs: grad_kernel(
-            row_count,
-            col_count,
-            *refs[: 3 + row_count],
-            *((refs[3 + row_count + h], order.index(s)) for h in range(2) for s in range(half)),
-            *refs[5 + row_count :],
-        ),
+        functools.partial(grad_kernel, row_count),
         "gradients",
-        [shaped((size, hidden), F32)] + [shaped((size, hidden), BF16)] * (row_count - 1),
-        [SMEM] + [VMEM] * (2 + row_count + 2 + 3),
-        [place, dense, degree] + pieces + [near_g, other_g, w_first, bias, w2],
-        scratch=[pltpu.VMEM((tall, rows), BF16), pltpu.VMEM((row_count, size, hidden), F32)],
+        [shaped((size, hidden), F32), shaped((tall, columns), BF16), shaped((tall, nodes), F32)]
+        + [shaped((size, hidden), BF16)] * (row_count - 1),
+        [VMEM] * (2 + row_count + 3),
+        [back, own_g] + pieces + [w_first, bias, w2],
+        scratch=[pltpu.VMEM((row_count, size, hidden), F32)],
     )
     mine = out[0]
     for s in range(1, row_count):
-        mine = mine + exchange(out[s], "row", s).astype(F32)
+        mine = mine + exchange(out[2 + s], "row", s).astype(F32)
 
     send, keep = call(
-        functools.partial(second_kernel, row_count),
+        second_kernel,
         "second_product",
         [shaped((half, tall, nodes), BF16), shaped((half, tall, nodes), F32)],
-        [VMEM, ANY] + [VMEM] * (row_count + 3),
-        [dense, out[0]] + pieces + [w_first, bias, w2],
-        scratch=[pltpu.VMEM((tall, columns), BF16)],
+        [VMEM, VMEM, VMEM, ANY],
+        [dense, out[1], out[2], out[0]],
     )
     out = call(
         functools.partial(core_kernel, half),
@@ -397,8 +430,8 @@
             shaped((classes, hidden), F32),
             shaped((1, classes), F32),
         ],
-        [SMEM] + [VMEM] * (3 + half - 1 + row_count),
-        [place, out[0], degree, b_second[None, :]] + parts + shares,
+        [VMEM] * (3 + half - 1 + row_count),
+        [out[0], degree, b_second[None, :]] + parts + shares,
         scratch=[pltpu.VMEM(((size - fin // row_count - 16) * row_count, hidden), F32)],
     )
     return logits.T, grad_w1, grad_b1[0], grad_w2.T, grad_b2[0]

time: 68.1 us -> 63.8 us (0.937)
  local copies, waits for them, and re-layouts: 3.9 us -> 0.65 us
  Pallas kernels: 13.2 us -> 11 us
  starting transfers between devices: 33.8 us -> 35.1 us
    unnamed x14 -> x10, local copies, waits for them, and re-layouts: 3.15 us -> 0.65 us
    pallas_call x8 -> x9, Pallas kernels: 13.2 us -> 11 us  [call(): pl.pallas_call(kernel, out_shape=tuple(outs), in_specs=in_specs, out_spec...]
    ppermute x27, starting transfers between devices: 33.8 us -> 35.1 us  [exchange(): return lax.ppermute(value, axis, [(i, i ^ mask) for i in range(count)])]
    concatenate x1 -> x0, local copies, waits for them, and re-layouts: 0.75 us -> none  [local(): jnp.concatenate([tile_row[0, 0], tile_col[0, 0], tile_live[0], place])]
  transfers between devices with their start and end apart: 27 -> 27, of which waited for: 13 -> 13; matrix products, arithmetic and copies ran while one was open for 1% -> 0% of each run, Pallas kernels for 8% -> 9%
where the time goes in v4:
time: 63.8 us; the launch traced here: 63.4 us
  starting transfers between devices  35.1 us (55%)
  waiting for transfers between devices  15.1 us (24%)
  Pallas kernels  11 us (17%)
  between operations  1.47 us (2%)
  local copies, waits for them, and re-layouts  0.65 us (1%)
    ppermute x27, starting transfers between devices, exchange(): return lax.ppermute(value, axis, [(i, i ^ mask) for i in range(count)])  35.1 us
    ppermute x27, waiting for transfers between devices, exchange(): return lax.ppermute(value, axis, [(i, i ^ mask) for i in range(count)])  15.1 us
    pallas_call x9, Pallas kernels, call(): pl.pallas_call(kernel, out_shape=tuple(outs), in_specs=in_specs, out_spec...  11 us
  transfers between devices with their start and end apart: 27, of which 13 were waited for; matrix products, arithmetic and copies ran while one was open for 0% of the time, Pallas kernels for 9%

profile of v4, /device:TPU:0, one launch (start us, length us, event | category | flops | bytes accessed | tf_op | source)
XLA Modules:
  0.0 63.4 jit_solution(3436440984701568989)
XLA Ops:
  0.6 4.1 %collective-permute-start.1 = (bf16[172,256]{1,0:T(8,128)(2,1)}, bf16[172,256]{1,0:T(8,128)(2,1)S(1)}, u32[]{:S(2)}, u32[]{:S(2)}) collective-permute-start(bf16[172,256]{1,0:T(8,128)(2,1)} %bitcast.11), channel_id=1, source_target_pairs={{0,4},{1,5},{2,6},{3,7},{4,0},{5,1},{6,2},{7,3},{8,12},{9,13},{10,... | collective-permute-start | bytes 264200 | tf_op jit(solution)/shard_map/ppermute | solution.py:22
  4.7 1.5 %collective-permute-start = (bf16[256,128]{1,0:T(8,128)(2,1)}, bf16[256,128]{1,0:T(8,128)(2,1)S(1)}, u32[]{:S(2)}, u32[]{:S(2)}) collective-permute-start(bf16[256,128]{1,0:T(8,128)(2,1)} %features_hbm.1), channel_id=1, source_target_pairs={{0,8},{8,0},{16,24},{24,16},{1,9},{9,1},{17,25},{25,17},{2,10},{10... | collective-permute-start | bytes 196616 | tf_op jit(solution)/shard_map/ppermute | solution.py:22
  6.2 1.5 %collective-permute-start.3 = (bf16[256,128]{1,0:T(8,128)(2,1)}, bf16[256,128]{1,0:T(8,128)(2,1)S(1)}, u32[]{:S(2)}, u32[]{:S(2)}) collective-permute-start(bf16[256,128]{1,0:T(8,128)(2,1)} %features_hbm.1), channel_id=1, source_target_pairs={{0,24},{8,16},{16,8},{24,0},{1,25},{9,17},{17,9},{25,1},{2,26},{10... | collective-permute-start | bytes 196616 | tf_op jit(solution)/shard_map/ppermute | solution.py:22
  9.8 3.0 %dense_adjacency.1 = (bf16[2048,1024]{1,0:T(8,128)(2,1)S(1)}, f32[16,128]{1,0:T(8,128)S(1)}, bf16[2,256,128]{2,1,0:T(8,128)(2,1)S(1)}, bf16[172,256]{1,0:T(8,128)(2,1)S(1)}) custom-call(s32[1,1,48]{2,1,0:T(1,128)} %row_hbm.1, s32[1,1,48]{2,1,0:T(1,128)} %col_hbm.1, s32[1,1]{1,0:T(1,128)S(6)} %copy.15.live_hbm, bf16[1,1,48,128,128]{4,3,2,1,0:T(8,128)(2,1)} %tiles_hbm.1, ...), custom_call_target="tpu_custom_call" | custom-call | tf_op jit(solution)/shard_map/dense_adjacency/pallas_call | solution.py:28
  12.8 1.7 %first_product.1 = (bf16[1056,128]{1,0:T(8,128)(2,1)S(1)}, f32[1024,128]{1,0:T(8,128)S(1)}, bf16[2,172,256]{2,1,0:T(8,128)(2,1)S(1)}) custom-call(bf16[2048,1024]{1,0:T(8,128)(2,1)S(1)} %get-tuple-element.38.dense_ref, f32[16,128]{1,0:T(8,128)S(1)} %get-tuple-element.39.degree_ref.part_ref, bf16[172,256]{1,0:T(8,128)(2,1)S(1)} %get-tuple-element.40.g_ref, ...), custom_call_target="tpu_custom_call" | custom-call | tf_op jit(solution)/shard_map/first_product/pallas_call | solution.py:28
  14.7 2.2 %collective-permute-start.5 = (bf16[2,172,256]{2,1,0:T(8,128)(2,1)S(1)}, bf16[2,172,256]{2,1,0:T(8,128)(2,1)S(1)}, u32[]{:S(2)}, u32[]{:S(2)}) collective-permute-start(bf16[2,172,256]{2,1,0:T(8,128)(2,1)S(1)} %get-tuple-element.46.left_ref), channel_id=1, source_target_pairs={{0,2},{1,3},{2,0},{3,1},{4,6},{5,7},{6,4},{7,5},{8,10},{9,11},{10,... | collective-permute-start | bytes 528392 | tf_op jit(solution)/shard_map/ppermute | solution.py:22
  16.9 1.5 %collective-permute-start.6 = (bf16[288,128]{1,0:T(8,128)(2,1)S(1)}, bf16[288,128]{1,0:T(8,128)(2,1)S(1)}, u32[]{:S(2)}, u32[]{:S(2)}) collective-permute-start(bf16[288,128]{1,0:T(8,128)(2,1)S(1)} %get-tuple-element.47), channel_id=1, source_target_pairs={{0,2},{1,3},{2,0},{3,1},{4,6},{5,7},{6,4},{7,5},{8,10},{9,11},{10,... | collective-permute-start | bytes 221192 | tf_op jit(solution)/shard_map/ppermute | solution.py:22
  18.5 0.9 %collective-permute-start.7 = (bf16[288,128]{1,0:T(8,128)(2,1)S(1)}, bf16[288,128]{1,0:T(8,128)(2,1)S(1)}, u32[]{:S(2)}, u32[]{:S(2)}) collective-permute-start(bf16[288,128]{1,0:T(8,128)(2,1)S(1)} %get-tuple-element.48), channel_id=1, source_target_pairs={{0,4},{1,5},{2,6},{3,7},{4,0},{5,1},{6,2},{7,3},{8,12},{9,13},{10,... | collective-permute-start | bytes 221192 | tf_op jit(solution)/shard_map/ppermute | solution.py:22
  19.4 2.0 %collective-permute-start.8 = (bf16[288,128]{1,0:T(8,128)(2,1)S(1)}, bf16[288,128]{1,0:T(8,128)(2,1)S(1)}, u32[]{:S(2)}, u32[]{:S(2)}) collective-permute-start(bf16[288,128]{1,0:T(8,128)(2,1)S(1)} %get-tuple-element.49), channel_id=1, source_target_pairs={{0,6},{1,7},{2,4},{3,5},{4,2},{5,3},{6,0},{7,1},{8,14},{9,15},{10,... | collective-permute-start | bytes 221192 | tf_op jit(solution)/shard_map/ppermute | solution.py:22
  21.4 1.8 %collective-permute-done.5.right_ref = bf16[2,172,256]{2,1,0:T(8,128)(2,1)S(1)} collective-permute-done((bf16[2,172,256]{2,1,0:T(8,128)(2,1)S(1)}, bf16[2,172,256]{2,1,0:T(8,128)(2,1)S(1)}, u32[]{:S(2)}, u32[]{:S(2)}) %collective-permute-start.5) | collective-permute-done | bytes 176160 | tf_op jit(solution)/shard_map/ppermute | solution.py:22
  23.2 1.9 %collective-permute-done.6.refs_0_ = bf16[288,128]{1,0:T(8,128)(2,1)S(1)} collective-permute-done((bf16[288,128]{1,0:T(8,128)(2,1)S(1)}, bf16[288,128]{1,0:T(8,128)(2,1)S(1)}, u32[]{:S(2)}, u32[]{:S(2)}) %collective-permute-start.6) | collective-permute-done | bytes 73760 | tf_op jit(solution)/shard_map/ppermute | solution.py:22
  25.0 2.3 %collective-permute-done.7.refs_1_ = bf16[288,128]{1,0:T(8,128)(2,1)S(1)} collective-permute-done((bf16[288,128]{1,0:T(8,128)(2,1)S(1)}, bf16[288,128]{1,0:T(8,128)(2,1)S(1)}, u32[]{:S(2)}, u32[]{:S(2)}) %collective-permute-start.7) | collective-permute-done | bytes 73760 | tf_op jit(solution)/shard_map/ppermute | solution.py:22
  27.6 2.5 %collective-permute-start.12 = (bf16[256,128]{1,0:T(8,128)(2,1)S(1)}, bf16[256,128]{1,0:T(8,128)(2,1)S(1)}, u32[]{:S(2)}, u32[]{:S(2)}) collective-permute-start(bf16[256,128]{1,0:T(8,128)(2,1)S(1)} %get-tuple-element.52.refs_0_), channel_id=1, source_target_pairs={{0,24},{8,16},{16,8},{24,0},{1,25},{9,17},{17,9},{25,1},{2,26},{10... | collective-permute-start | bytes 196616 | tf_op jit(solution)/shard_map/ppermute | solution.py:22
  30.2 1.5 %collective-permute-start.11 = (bf16[256,128]{1,0:T(8,128)(2,1)S(1)}, bf16[256,128]{1,0:T(8,128)(2,1)S(1)}, u32[]{:S(2)}, u32[]{:S(2)}) collective-permute-start(bf16[256,128]{1,0:T(8,128)(2,1)S(1)} %get-tuple-element.52.refs_0_), channel_id=1, source_target_pairs={{0,16},{8,24},{16,0},{24,8},{1,17},{9,25},{17,1},{25,9},{2,18},{10... | collective-permute-start | bytes 196616 | tf_op jit(solution)/shard_map/ppermute | solution.py:22
  31.7 0.9 %back_product.1.back_ref = f32[4,176,256]{2,1,0:T(8,128)S(1)} custom-call(bf16[2048,1024]{1,0:T(8,128)(2,1)S(1)} %get-tuple-element.38.dense_ref, f32[16,128]{1,0:T(8,128)S(1)} %get-tuple-element.50.degree_ref, bf16[4,172,256]{2,1,0:T(8,128)(2,1)S(1)} %get-tuple-element.51.near_ref, bf16[4,172,256]{2,1,0:T(8,128)(2,1)S(1)} %collective-permute-done.9.other_ref), custom_call_target="tpu_custom_call" | custom-call | tf_op jit(solution)/shard_map/back_product/pallas_call | solution.py:28
  33.1 1.4 %collective-permute-done.11.refs_2_ = bf16[256,128]{1,0:T(8,128)(2,1)S(1)} collective-permute-done((bf16[256,128]{1,0:T(8,128)(2,1)S(1)}, bf16[256,128]{1,0:T(8,128)(2,1)S(1)}, u32[]{:S(2)}, u32[]{:S(2)}) %collective-permute-start.11) | collective-permute-done | bytes 65568 | tf_op jit(solution)/shard_map/ppermute | solution.py:22
  34.5 1.5 %collective-permute-done.10.refs_1_ = bf16[256,128]{1,0:T(8,128)(2,1)S(1)} collective-permute-done((bf16[256,128]{1,0:T(8,128)(2,1)S(1)}, bf16[256,128]{1,0:T(8,128)(2,1)S(1)}, u32[]{:S(2)}, u32[]{:S(2)}) %collective-permute-start.10) | collective-permute-done | bytes 65568 | tf_op jit(solution)/shard_map/ppermute | solution.py:22
  36.0 2.0 %gradients.1 = (f32[96,256]{1,0:T(8,128)S(1)}, bf16[176,1024]{1,0:T(8,128)(2,1)S(1)}, f32[176,256]{1,0:T(8,128)S(1)}, bf16[96,256]{1,0:T(8,128)(2,1)S(1)}, bf16[...) custom-call(f32[4,176,256]{2,1,0:T(8,128)S(1)} %back_product.1.back_ref, ...), custom_call_target="tpu_custom_call" | custom-call | tf_op jit(solution)/shard_map/gradients/pallas_call | solution.py:28
  38.7 1.0 %collective-permute-start.15 = (bf16[96,256]{1,0:T(8,128)(2,1)S(1)}, bf16[96,256]{1,0:T(8,128)(2,1)S(1)}, u32[]{:S(2)}, u32[]{:S(2)}) collective-permute-start(bf16[96,256]{1,0:T(8,128)(2,1)S(1)} %get-tuple-element.59), channel_id=1, source_target_pairs={{0,16},{8,24},{16,0},{24,8},{1,17},{9,25},{17,1},{25,9},{2,18},{10... | collective-permute-start | bytes 147464 | tf_op jit(solution)/shard_map/ppermute | solution.py:22
  39.6 1.9 %collective-permute-start.16 = (bf16[96,256]{1,0:T(8,128)(2,1)S(1)}, bf16[96,256]{1,0:T(8,128)(2,1)S(1)}, u32[]{:S(2)}, u32[]{:S(2)}) collective-permute-start(bf16[96,256]{1,0:T(8,128)(2,1)S(1)} %get-tuple-element.60), channel_id=1, source_target_pairs={{0,24},{8,16},{16,8},{24,0},{1,25},{9,17},{17,9},{25,1},{2,26},{10... | collective-permute-start | bytes 147464 | tf_op jit(solution)/shard_map/ppermute | solution.py:22
  41.5 2.0 %second_product.1 = (bf16[4,176,256]{2,1,0:T(8,128)(2,1)S(1)}, f32[4,176,256]{2,1,0:T(8,128)S(1)}) custom-call(bf16[2048,1024]{1,0:T(8,128)(2,1)S(1)} %get-tuple-element.38.dense_ref, bf16[176,1024]{1,0:T(8,128)(2,1)S(1)} %get-tuple-element.53.hidden_ref, f32[176,256]{1,0:T(8,128)S(1)} %get-tuple-element.54.first_ref, f32[96,256]{1,0:T(8,128)S(1)} %get-tuple-element.55.after_ref), custom_call_target="tpu_custom_call" | custom-call | tf_op jit(solution)/shard_map/second_product/pallas_call | solution.py:28
  43.7 1.0 %collective-permute-done.16 = bf16[96,256]{1,0:T(8,128)(2,1)S(1)} collective-permute-done((bf16[96,256]{1,0:T(8,128)(2,1)S(1)}, bf16[96,256]{1,0:T(8,128)(2,1)S(1)}, u32[]{:S(2)}, u32[]{:S(2)}) %collective-permute-start.16) | collective-permute-done | bytes 49184 | tf_op jit(solution)/shard_map/ppermute | solution.py:22
  44.7 1.3 %collective-permute-done.17.far_ref = f32[96,256]{1,0:T(8,128)S(1)} collective-permute-done((f32[96,256]{1,0:T(8,128)S(1)}, f32[96,256]{1,0:T(8,128)S(1)}, u32[]{:S(2)}, u32[]{:S(2)}) %collective-permute-start.17) | collective-permute-done | bytes 98336 | tf_op jit(solution)/shard_map/ppermute | solution.py:22
  46.1 3.0 %collective-permute-start.23 = (bf16[96,256]{1,0:T(8,128)(2,1)S(1)}, bf16[96,256]{1,0:T(8,128)(2,1)S(1)}, u32[]{:S(2)}, u32[]{:S(2)}) collective-permute-start(bf16[96,256]{1,0:T(8,128)(2,1)S(1)} %get-tuple-element.65), channel_id=1, source_target_pairs={{0,6},{1,7},{2,4},{3,5},{4,2},{5,3},{6,0},{7,1},{8,14},{9,15},{10,... | collective-permute-start | bytes 147464 | tf_op jit(solution)/shard_map/ppermute | solution.py:22
  49.2 1.4 %collective-permute-start.21 = (bf16[96,256]{1,0:T(8,128)(2,1)S(1)}, bf16[96,256]{1,0:T(8,128)(2,1)S(1)}, u32[]{:S(2)}, u32[]{:S(2)}) collective-permute-start(bf16[96,256]{1,0:T(8,128)(2,1)S(1)} %get-tuple-element.65), channel_id=1, source_target_pairs={{0,2},{1,3},{2,0},{3,1},{4,6},{5,7},{6,4},{7,5},{8,10},{9,11},{10,... | collective-permute-start | bytes 147464 | tf_op jit(solution)/shard_map/ppermute | solution.py:22
  51.2 2.9 %collective-permute-start.19 = (bf16[176,256]{1,0:T(8,128)(2,1)S(1)}, bf16[176,256]{1,0:T(8,128)(2,1)S(1)}, u32[]{:S(2)}, u32[]{:S(2)}) collective-permute-start(bf16[176,256]{1,0:T(8,128)(2,1)S(1)} %get-tuple-element.63), channel_id=1, source_target_pairs={{0,4},{1,5},{2,6},{3,7},{4,0},{5,1},{6,2},{7,3},{8,12},{9,13},{10,... | collective-permute-start | bytes 270344 | tf_op jit(solution)/shard_map/ppermute | solution.py:22
  54.1 1.5 %collective-permute-start.20 = (bf16[176,256]{1,0:T(8,128)(2,1)S(1)}, bf16[176,256]{1,0:T(8,128)(2,1)S(1)}, u32[]{:S(2)}, u32[]{:S(2)}) collective-permute-start(bf16[176,256]{1,0:T(8,128)(2,1)S(1)} %get-tuple-element.64), channel_id=1, source_target_pairs={{0,6},{1,7},{2,4},{3,5},{4,2},{5,3},{6,0},{7,1},{8,14},{9,15},{10,... | collective-permute-start | bytes 270344 | tf_op jit(solution)/shard_map/ppermute | solution.py:22
  55.8 2.0 %collective-permute-start.26 = (bf16[96,256]{1,0:T(8,128)(2,1)S(1)}, bf16[96,256]{1,0:T(8,128)(2,1)S(1)}, u32[]{:S(2)}, u32[]{:S(2)}) collective-permute-start(bf16[96,256]{1,0:T(8,128)(2,1)S(1)} %add_convert_fusion.refs_3_), channel_id=1, source_target_pairs={{0,24},{8,16},{16,8},{24,0},{1,25},{9,17},{17,9},{25,1},{2,26},{10... | collective-permute-start | bytes 147464 | tf_op jit(solution)/shard_map/ppermute | solution.py:22
  58.3 1.1 %collective-permute-start.24 = (bf16[96,256]{1,0:T(8,128)(2,1)S(1)}, bf16[96,256]{1,0:T(8,128)(2,1)S(1)}, u32[]{:S(2)}, u32[]{:S(2)}) collective-permute-start(bf16[96,256]{1,0:T(8,128)(2,1)S(1)} %add_convert_fusion.refs_3_), channel_id=1, source_target_pairs={{0,8},{8,0},{16,24},{24,16},{1,9},{9,1},{17,25},{25,17},{2,10},{10... | collective-permute-start | bytes 147464 | tf_op jit(solution)/shard_map/ppermute | solution.py:22
  59.4 1.6 %collective-permute-done.19.refs_1_ = bf16[176,256]{1,0:T(8,128)(2,1)S(1)} collective-permute-done((bf16[176,256]{1,0:T(8,128)(2,1)S(1)}, bf16[176,256]{1,0:T(8,128)(2,1)S(1)}, u32[]{:S(2)}, u32[]{:S(2)}) %collective-permute-start.19) | collective-permute-done | bytes 90144 | tf_op jit(solution)/shard_map/ppermute | solution.py:22
  61.0 0.9 %collective-permute-done.25.refs_5_ = bf16[96,256]{1,0:T(8,128)(2,1)S(1)} collective-permute-done((bf16[96,256]{1,0:T(8,128)(2,1)S(1)}, bf16[96,256]{1,0:T(8,128)(2,1)S(1)}, u32[]{:S(2)}, u32[]{:S(2)}) %collective-permute-start.25) | collective-permute-done | bytes 49184 | tf_op jit(solution)/shard_map/ppermute | solution.py:22
  62.4 1.0 %results.1 = (bf16[172,256]{1,0:T(8,128)(2,1)}, f32[128,256]{1,0:T(8,128)}, f32[1,256]{1,0:T(1,128)}, f32[172,256]{1,0:T(8,128)}, f32[1,172]{1,0:T(1,128)}) custom-call(f32[176,256]{1,0:T(8,128)S(1)} %get-tuple-element.61.total_ref, f32[16,128]{1,0:T(8,128)S(1)} %get-tuple-element.50.degree_ref, f32[1,172]{1,0:T(1,128)S(1)} %bitcast.9, ...), custom_call_target="tpu_custom_call" | custom-call | tf_op jit(solution)/shard_map/results/pallas_call | solution.py:28
  (43 shorter events, 5.2 us)
Async XLA Ops:
  0.6 12.2 %collective-permute-start.1 = (bf16[172,256]{1,0:T(8,128)(2,1)}, bf16[172,256]{1,0:T(8,128)(2,1)S(1)}, u32[]{:S(2)}, u32[]{:S(2)}) collective-permute-start(bf16[172,256]{1,0:T(8,128)(2,1)} %bitcast.11), channel_id=1, source_target_pairs={{0,4},{1,5},{2,6},{3,7},{4,0},{5,1},{6,2},{7,3},{8,12},{9,13},{10,... | collective-permute-start | bytes 264200 | tf_op jit(solution)/shard_map/ppermute | solution.py:22
  4.7 4.5 %collective-permute-start = (bf16[256,128]{1,0:T(8,128)(2,1)}, bf16[256,128]{1,0:T(8,128)(2,1)S(1)}, u32[]{:S(2)}, u32[]{:S(2)}) collective-permute-start(bf16[256,128]{1,0:T(8,128)(2,1)} %features_hbm.1), channel_id=1, source_target_pairs={{0,8},{8,0},{16,24},{24,16},{1,9},{9,1},{17,25},{25,17},{2,10},{10... | collective-permute-start | bytes 196616 | tf_op jit(solution)/shard_map/ppermute | solution.py:22
  6.2 6.6 %collective-permute-start.3 = (bf16[256,128]{1,0:T(8,128)(2,1)}, bf16[256,128]{1,0:T(8,128)(2,1)S(1)}, u32[]{:S(2)}, u32[]{:S(2)}) collective-permute-start(bf16[256,128]{1,0:T(8,128)(2,1)} %features_hbm.1), channel_id=1, source_target_pairs={{0,24},{8,16},{16,8},{24,0},{1,25},{9,17},{17,9},{25,1},{2,26},{10... | collective-permute-start | bytes 196616 | tf_op jit(solution)/shard_map/ppermute | solution.py:22
  7.7 5.1 %collective-permute-start.2 = (bf16[256,128]{1,0:T(8,128)(2,1)}, bf16[256,128]{1,0:T(8,128)(2,1)S(1)}, u32[]{:S(2)}, u32[]{:S(2)}) collective-permute-start(bf16[256,128]{1,0:T(8,128)(2,1)} %features_hbm.1), channel_id=1, source_target_pairs={{0,16},{8,24},{16,0},{24,8},{1,17},{9,25},{17,1},{25,9},{2,18},{10... | collective-permute-start | bytes 196616 | tf_op jit(solution)/shard_map/ppermute | solution.py:22
  9.2 0.6 copy-start.4
  14.6 21.4 %copy-start = (bf16[256,172]{0,1:T(8,128)(2,1)S(1)}, bf16[256,172]{0,1:T(8,128)(2,1)}, u32[]{:S(2)}) copy-start(bf16[256,172]{0,1:T(8,128)(2,1)} %param.17) | copy-start | bytes 264196
  14.6 21.4 %copy-start.1 = (bf16[128,256]{1,0:T(8,128)(2,1)S(1)}, bf16[128,256]{1,0:T(8,128)(2,1)}, u32[]{:S(2)}) copy-start(bf16[128,256]{1,0:T(8,128)(2,1)} %refs_4_.1) | copy-start | bytes 196612
  14.6 21.4 %copy-start.3 = (f32[256]{0:T(256)S(1)}, f32[256]{0:T(256)}, u32[]{:S(2)}) copy-start(f32[256]{0:T(256)} %param.16) | copy-start | bytes 3076
  14.6 2.2 %collective-permute-start.4 = (bf16[1056,128]{1,0:T(8,128)(2,1)S(1)}, bf16[1056,128]{1,0:T(8,128)(2,1)S(1)}, u32[]{:S(2)}, u32[]{:S(2)}) collective-permute-start(bf16[1056,128]{1,0:T(8,128)(2,1)S(1)} %get-tuple-element.43), channel_id=1, source_target_pairs={{0,1},{1,0},{2,3},{3,2},{4,5},{5,4},{6,7},{7,6},{8,9},{9,8},{10,11... | collective-permute-start | bytes 811016 | tf_op jit(solution)/shard_map/ppermute | solution.py:22
  14.7 8.5 %collective-permute-start.5 = (bf16[2,172,256]{2,1,0:T(8,128)(2,1)S(1)}, bf16[2,172,256]{2,1,0:T(8,128)(2,1)S(1)}, u32[]{:S(2)}, u32[]{:S(2)}) collective-permute-start(bf16[2,172,256]{2,1,0:T(8,128)(2,1)S(1)} %get-tuple-element.46.left_ref), channel_id=1, source_target_pairs={{0,2},{1,3},{2,0},{3,1},{4,6},{5,7},{6,4},{7,5},{8,10},{9,11},{10,... | collective-permute-start | bytes 528392 | tf_op jit(solution)/shard_map/ppermute | solution.py:22
  16.9 8.1 %collective-permute-start.6 = (bf16[288,128]{1,0:T(8,128)(2,1)S(1)}, bf16[288,128]{1,0:T(8,128)(2,1)S(1)}, u32[]{:S(2)}, u32[]{:S(2)}) collective-permute-start(bf16[288,128]{1,0:T(8,128)(2,1)S(1)} %get-tuple-element.47), channel_id=1, source_target_pairs={{0,2},{1,3},{2,0},{3,1},{4,6},{5,7},{6,4},{7,5},{8,10},{9,11},{10,... | collective-permute-start | bytes 221192 | tf_op jit(solution)/shard_map/ppermute | solution.py:22
  18.5 8.9 %collective-permute-start.7 = (bf16[288,128]{1,0:T(8,128)(2,1)S(1)}, bf16[288,128]{1,0:T(8,128)(2,1)S(1)}, u32[]{:S(2)}, u32[]{:S(2)}) collective-permute-start(bf16[288,128]{1,0:T(8,128)(2,1)S(1)} %get-tuple-element.48), channel_id=1, source_target_pairs={{0,4},{1,5},{2,6},{3,7},{4,0},{5,1},{6,2},{7,3},{8,12},{9,13},{10,... | collective-permute-start | bytes 221192 | tf_op jit(solution)/shard_map/ppermute | solution.py:22
  19.4 8.0 %collective-permute-start.8 = (bf16[288,128]{1,0:T(8,128)(2,1)S(1)}, bf16[288,128]{1,0:T(8,128)(2,1)S(1)}, u32[]{:S(2)}, u32[]{:S(2)}) collective-permute-start(bf16[288,128]{1,0:T(8,128)(2,1)S(1)} %get-tuple-element.49), channel_id=1, source_target_pairs={{0,6},{1,7},{2,4},{3,5},{4,2},{5,3},{6,0},{7,1},{8,14},{9,15},{10,... | collective-permute-start | bytes 221192 | tf_op jit(solution)/shard_map/ppermute | solution.py:22
  27.6 4.1 %collective-permute-start.9 = (bf16[4,172,256]{2,1,0:T(8,128)(2,1)S(1)}, bf16[4,172,256]{2,1,0:T(8,128)(2,1)S(1)}, u32[]{:S(2)}, u32[]{:S(2)}) collective-permute-start(bf16[4,172,256]{2,1,0:T(8,128)(2,1)S(1)} %get-tuple-element.51.near_ref), channel_id=1, source_target_pairs={{0,1},{1,0},{2,3},{3,2},{4,5},{5,4},{6,7},{7,6},{8,9},{9,8},{10,11... | collective-permute-start | bytes 1056776 | tf_op jit(solution)/shard_map/ppermute | solution.py:22
  27.6 5.4 %collective-permute-start.12 = (bf16[256,128]{1,0:T(8,128)(2,1)S(1)}, bf16[256,128]{1,0:T(8,128)(2,1)S(1)}, u32[]{:S(2)}, u32[]{:S(2)}) collective-permute-start(bf16[256,128]{1,0:T(8,128)(2,1)S(1)} %get-tuple-element.52.refs_0_), channel_id=1, source_target_pairs={{0,24},{8,16},{16,8},{24,0},{1,25},{9,17},{17,9},{25,1},{2,26},{10... | collective-permute-start | bytes 196616 | tf_op jit(solution)/shard_map/ppermute | solution.py:22
  30.2 4.3 %collective-permute-start.11 = (bf16[256,128]{1,0:T(8,128)(2,1)S(1)}, bf16[256,128]{1,0:T(8,128)(2,1)S(1)}, u32[]{:S(2)}, u32[]{:S(2)}) collective-permute-start(bf16[256,128]{1,0:T(8,128)(2,1)S(1)} %get-tuple-element.52.refs_0_), channel_id=1, source_target_pairs={{0,16},{8,24},{16,0},{24,8},{1,17},{9,25},{17,1},{25,9},{2,18},{10... | collective-permute-start | bytes 196616 | tf_op jit(solution)/shard_map/ppermute | solution.py:22
  31.7 4.3 %collective-permute-start.10 = (bf16[256,128]{1,0:T(8,128)(2,1)S(1)}, bf16[256,128]{1,0:T(8,128)(2,1)S(1)}, u32[]{:S(2)}, u32[]{:S(2)}) collective-permute-start(bf16[256,128]{1,0:T(8,128)(2,1)S(1)} %get-tuple-element.52.refs_0_), channel_id=1, source_target_pairs={{0,8},{8,0},{16,24},{24,16},{1,9},{9,1},{17,25},{25,17},{2,10},{10... | collective-permute-start | bytes 196616 | tf_op jit(solution)/shard_map/ppermute | solution.py:22
  32.6 29.8 %copy-start.2 = (f32[172]{0:T(256)S(1)}, f32[172]{0:T(256)}, u32[]{:S(2)}) copy-start(f32[172]{0:T(256)} %param.18) | copy-start | bytes 2068
  38.0 5.7 %collective-permute-start.14 = (bf16[96,256]{1,0:T(8,128)(2,1)S(1)}, bf16[96,256]{1,0:T(8,128)(2,1)S(1)}, u32[]{:S(2)}, u32[]{:S(2)}) collective-permute-start(bf16[96,256]{1,0:T(8,128)(2,1)S(1)} %get-tuple-element.58), channel_id=1, source_target_pairs={{0,8},{8,0},{16,24},{24,16},{1,9},{9,1},{17,25},{25,17},{2,10},{10... | collective-permute-start | bytes 147464 | tf_op jit(solution)/shard_map/ppermute | solution.py:22
  38.7 5.0 %collective-permute-start.15 = (bf16[96,256]{1,0:T(8,128)(2,1)S(1)}, bf16[96,256]{1,0:T(8,128)(2,1)S(1)}, u32[]{:S(2)}, u32[]{:S(2)}) collective-permute-start(bf16[96,256]{1,0:T(8,128)(2,1)S(1)} %get-tuple-element.59), channel_id=1, source_target_pairs={{0,16},{8,24},{16,0},{24,8},{1,17},{9,25},{17,1},{25,9},{2,18},{10... | collective-permute-start | bytes 147464 | tf_op jit(solution)/shard_map/ppermute | solution.py:22
  39.6 5.0 %collective-permute-start.16 = (bf16[96,256]{1,0:T(8,128)(2,1)S(1)}, bf16[96,256]{1,0:T(8,128)(2,1)S(1)}, u32[]{:S(2)}, u32[]{:S(2)}) collective-permute-start(bf16[96,256]{1,0:T(8,128)(2,1)S(1)} %get-tuple-element.60), channel_id=1, source_target_pairs={{0,24},{8,16},{16,8},{24,0},{1,25},{9,17},{17,9},{25,1},{2,26},{10... | collective-permute-start | bytes 147464 | tf_op jit(solution)/shard_map/ppermute | solution.py:22
  43.6 2.5 %collective-permute-start.13 = (bf16[4,176,256]{2,1,0:T(8,128)(2,1)S(1)}, bf16[4,176,256]{2,1,0:T(8,128)(2,1)S(1)}, u32[]{:S(2)}, u32[]{:S(2)}) collective-permute-start(bf16[4,176,256]{2,1,0:T(8,128)(2,1)S(1)} %get-tuple-element.57), channel_id=1, source_target_pairs={{0,1},{1,0},{2,3},{3,2},{4,5},{5,4},{6,7},{7,6},{8,9},{9,8},{10,11... | collective-permute-start | bytes 1081352 | tf_op jit(solution)/shard_map/ppermute | solution.py:22
  44.7 1.4 %collective-permute-start.17 = (f32[96,256]{1,0:T(8,128)S(1)}, f32[96,256]{1,0:T(8,128)S(1)}, u32[]{:S(2)}, u32[]{:S(2)}) collective-permute-start(f32[96,256]{1,0:T(8,128)S(1)} %convert_add_fusion.mine_ref), channel_id=1, source_target_pairs={{0,1},{1,0},{2,3},{3,2},{4,5},{5,4},{6,7},{7,6},{8,9},{9,8},{10,11... | collective-permute-start | bytes 294920 | tf_op jit(solution)/shard_map/ppermute | solution.py:22
  46.1 8.0 %collective-permute-start.23 = (bf16[96,256]{1,0:T(8,128)(2,1)S(1)}, bf16[96,256]{1,0:T(8,128)(2,1)S(1)}, u32[]{:S(2)}, u32[]{:S(2)}) collective-permute-start(bf16[96,256]{1,0:T(8,128)(2,1)S(1)} %get-tuple-element.65), channel_id=1, source_target_pairs={{0,6},{1,7},{2,4},{3,5},{4,2},{5,3},{6,0},{7,1},{8,14},{9,15},{10,... | collective-permute-start | bytes 147464 | tf_op jit(solution)/shard_map/ppermute | solution.py:22
  49.1 6.5 %collective-permute-start.22 = (bf16[96,256]{1,0:T(8,128)(2,1)S(1)}, bf16[96,256]{1,0:T(8,128)(2,1)S(1)}, u32[]{:S(2)}, u32[]{:S(2)}) collective-permute-start(bf16[96,256]{1,0:T(8,128)(2,1)S(1)} %get-tuple-element.65), channel_id=1, source_target_pairs={{0,4},{1,5},{2,6},{3,7},{4,0},{5,1},{6,2},{7,3},{8,12},{9,13},{10,... | collective-permute-start | bytes 147464 | tf_op jit(solution)/shard_map/ppermute | solution.py:22
  49.2 6.7 %collective-permute-start.21 = (bf16[96,256]{1,0:T(8,128)(2,1)S(1)}, bf16[96,256]{1,0:T(8,128)(2,1)S(1)}, u32[]{:S(2)}, u32[]{:S(2)}) collective-permute-start(bf16[96,256]{1,0:T(8,128)(2,1)S(1)} %get-tuple-element.65), channel_id=1, source_target_pairs={{0,2},{1,3},{2,0},{3,1},{4,6},{5,7},{6,4},{7,5},{8,10},{9,11},{10,... | collective-permute-start | bytes 147464 | tf_op jit(solution)/shard_map/ppermute | solution.py:22
  50.6 7.7 %collective-permute-start.18 = (bf16[176,256]{1,0:T(8,128)(2,1)S(1)}, bf16[176,256]{1,0:T(8,128)(2,1)S(1)}, u32[]{:S(2)}, u32[]{:S(2)}) collective-permute-start(bf16[176,256]{1,0:T(8,128)(2,1)S(1)} %get-tuple-element.62), channel_id=1, source_target_pairs={{0,2},{1,3},{2,0},{3,1},{4,6},{5,7},{6,4},{7,5},{8,10},{9,11},{10,... | collective-permute-start | bytes 270344 | tf_op jit(solution)/shard_map/ppermute | solution.py:22
  51.2 9.8 %collective-permute-start.19 = (bf16[176,256]{1,0:T(8,128)(2,1)S(1)}, bf16[176,256]{1,0:T(8,128)(2,1)S(1)}, u32[]{:S(2)}, u32[]{:S(2)}) collective-permute-start(bf16[176,256]{1,0:T(8,128)(2,1)S(1)} %get-tuple-element.63), channel_id=1, source_target_pairs={{0,4},{1,5},{2,6},{3,7},{4,0},{5,1},{6,2},{7,3},{8,12},{9,13},{10,... | collective-permute-start | bytes 270344 | tf_op jit(solution)/shard_map/ppermute | solution.py:22
  54.1 6.9 %collective-permute-start.20 = (bf16[176,256]{1,0:T(8,128)(2,1)S(1)}, bf16[176,256]{1,0:T(8,128)(2,1)S(1)}, u32[]{:S(2)}, u32[]{:S(2)}) collective-permute-start(bf16[176,256]{1,0:T(8,128)(2,1)S(1)} %get-tuple-element.64), channel_id=1, source_target_pairs={{0,6},{1,7},{2,4},{3,5},{4,2},{5,3},{6,0},{7,1},{8,14},{9,15},{10,... | collective-permute-start | bytes 270344 | tf_op jit(solution)/shard_map/ppermute | solution.py:22
  55.8 5.2 %collective-permute-start.26 = (bf16[96,256]{1,0:T(8,128)(2,1)S(1)}, bf16[96,256]{1,0:T(8,128)(2,1)S(1)}, u32[]{:S(2)}, u32[]{:S(2)}) collective-permute-start(bf16[96,256]{1,0:T(8,128)(2,1)S(1)} %add_convert_fusion.refs_3_), channel_id=1, source_target_pairs={{0,24},{8,16},{16,8},{24,0},{1,25},{9,17},{17,9},{25,1},{2,26},{10... | collective-permute-start | bytes 147464 | tf_op jit(solution)/shard_map/ppermute | solution.py:22
  57.8 4.1 %collective-permute-start.25 = (bf16[96,256]{1,0:T(8,128)(2,1)S(1)}, bf16[96,256]{1,0:T(8,128)(2,1)S(1)}, u32[]{:S(2)}, u32[]{:S(2)}) collective-permute-start(bf16[96,256]{1,0:T(8,128)(2,1)S(1)} %add_convert_fusion.refs_3_), channel_id=1, source_target_pairs={{0,16},{8,24},{16,0},{24,8},{1,17},{9,25},{17,1},{25,9},{2,18},{10... | collective-permute-start | bytes 147464 | tf_op jit(solution)/shard_map/ppermute | solution.py:22
  58.3 4.1 %collective-permute-start.24 = (bf16[96,256]{1,0:T(8,128)(2,1)S(1)}, bf16[96,256]{1,0:T(8,128)(2,1)S(1)}, u32[]{:S(2)}, u32[]{:S(2)}) collective-permute-start(bf16[96,256]{1,0:T(8,128)(2,1)S(1)} %add_convert_fusion.refs_3_), channel_id=1, source_target_pairs={{0,8},{8,0},{16,24},{24,16},{1,9},{9,1},{17,25},{25,17},{2,10},{10... | collective-permute-start | bytes 147464 | tf_op jit(solution)/shard_map/ppermute | solution.py:22

commit v5 on v4

--- a/solution.py
+++ b/solution.py
@@ -50,7 +50,7 @@
 
 
 def dense_kernel(own, row_hbm, col_hbm, live_hbm, tiles_hbm, features_hbm, g_hbm, next_hbm, *refs):
-    dense_ref, degree_ref, held_ref, g_ref, row_ref, col_ref, live_ref, tiles_ref, done = refs
+    dense_ref, held_ref, g_ref, row_ref, col_ref, live_ref, tiles_ref, done = refs
     pairs = (
         (row_hbm, row_ref),
         (col_hbm, col_ref),
@@ -83,37 +83,37 @@
             pl.ds(pl.multiple_of(at_col * block, block), block),
         ] = tiles_ref[0, 0, slot]
 
-    ones = jnp.ones((8, columns), BF16)
-    for start in range(0, rows, 2 * block):
-        sums = product(ones, dense_ref[pl.ds(start, 2 * block), :], ((1,), (1,)))
-        for part in range(2):
-            degree_ref[pl.ds(start // block + part, 1), :] = sums[:1, part * block : (part + 1) * block]
     for copy in copies[4:]:
         copy.wait()
 
 
-def first_kernel(spans, dense_ref, degree_ref, g_ref, far_ref, pair_in_ref, *refs):
-    pieces, (send_ref, keep_ref, pair_ref, held) = refs[: spans - 2], refs[spans - 2 :]
+def first_kernel(spans, dense_ref, g_ref, far_ref, pair_in_ref, *refs):
+    pieces, (send_ref, keep_ref, degree_ref, pair_ref, held) = refs[: spans - 2], refs[spans - 2 :]
     pair_ref[0] = g_ref[...]
     pair_ref[1] = far_ref[...]
     nodes = g_ref.shape[1]
-    held[pl.ds(0, nodes), :] = pair_in_ref[0]
-    held[pl.ds(nodes, nodes), :] = pair_in_ref[1]
-    for s in range(2, spans):
-        held[pl.ds(s * nodes, nodes), :] = pieces[s - 2][...]
+    fin = pair_in_ref.shape[2]
+    block = LANES
+    for s in range(spans):
+        held[pl.ds(s * nodes, nodes), :fin] = pair_in_ref[s] if s < 2 else pieces[s - 2][...]
+    held[:, fin:] = jnp.ones((held.shape[0], block), BF16)
     half = keep_ref.shape[0] // nodes
     blocks = degree_ref.shape[0]
+    line = lax.broadcasted_iota(jnp.int32, (block, block), 0) == lax.broadcasted_iota(jnp.int32, (block, block), 1)
+
+    for s in range(2 * half):
+        out = product(dense_ref[pl.ds(s * nodes, nodes), :], held[...])
+        if s < half:
+            keep_ref[pl.ds(s * nodes, nodes), :] = out[:, :fin]
+        else:
+            send_ref[pl.ds((s - half) * nodes, nodes), :] = out[:, :fin].astype(BF16)
+        for b in range(nodes // block):
+            sums = jnp.where(line, out[b * block : (b + 1) * block, fin:], 0.0)
+            at = s * (nodes // block) + b
+            degree_ref[at : at + 1, :] = jnp.sum(sums, axis=0, keepdims=True)
     high, low = split(degree_ref[...])
     send_ref[pl.ds(half * nodes, blocks), :] = high
     send_ref[pl.ds(half * nodes + blocks, blocks), :] = low
-
-    @pl.loop(0, half)
-    def _(s):
-        at = pl.multiple_of(s * nodes, nodes)
-        send_ref[pl.ds(at, nodes), :] = product(
-            dense_ref[pl.ds(pl.multiple_of((half + s) * nodes, nodes), nodes), :], held[...]
-        ).astype(BF16)
-        keep_ref[pl.ds(at, nodes), :] = product(dense_ref[pl.ds(at, nodes), :], held[...])
 
 
 def near_kernel(half, keep_ref, other_ref, part_ref, own_ref, degree_ref, *sends):
@@ -323,12 +323,11 @@
 
     whole = rows * columns * 2 <= 4 << 20
     keep_in = pltpu.VMEM if whole else shaped
-    dense, degree, held, own_g = call(
+    dense, held, own_g = call(
         functools.partial(dense_kernel, own),
         "dense_adjacency",
         [
             keep_in((rows, columns), BF16),
-            keep_in((blocks, block), F32),
             keep_in((2, nodes, fin), BF16),
             keep_in(g_own.shape, BF16),
         ],
@@ -343,17 +342,18 @@
         ],
         grant=GRANT if whole else 60 << 20,
     )
-    send, keep, left = call(
+    send, keep, degree, left = call(
         functools.partial(first_kernel, row_count),
         "first_product",
         [
             shaped((rows // 2 + 2 * blocks, fin), BF16),
             shaped((rows // 2, fin), F32),
+            shaped((blocks, block), F32),
             shaped((2, classes, nodes), BF16),
         ],
-        [VMEM] * (5 + row_count - 2),
-        [dense, degree, own_g, far_g, held] + inputs[2:],
-        scratch=[pltpu.VMEM((columns, fin), BF16)],
+        [VMEM] * (2 + row_count),
+        [dense, own_g, far_g, held] + inputs[2:],
+        scratch=[pltpu.VMEM((columns, fin + LANES), BF16)],
     )
     other = exchange(send, "col", 1)
     mask = half // 2

time: 63.8 us -> 62.1 us (0.973)
  starting transfers between devices: 35.1 us -> 33.8 us
    ppermute x27, starting transfers between devices: 35.1 us -> 33.8 us  [exchange(): return lax.ppermute(value, axis, [(i, i ^ mask) for i in range(count)])]
  transfers between devices with their start and end apart: 27 -> 27, of which waited for: 13 -> 14; matrix products, arithmetic and copies ran while one was open for 0% -> 0% of each run, Pallas kernels for 9% -> 10%
where the time goes in v5:
time: 62.1 us; the launch traced here: 62 us
  starting transfers between devices  33.8 us (54%)
  waiting for transfers between devices  15.5 us (25%)
  Pallas kernels  10.5 us (17%)
  between operations  1.47 us (2%)
  local copies, waits for them, and re-layouts  0.65 us (1%)
    ppermute x27, starting transfers between devices, exchange(): return lax.ppermute(value, axis, [(i, i ^ mask) for i in range(count)])  33.8 us
    ppermute x27, waiting for transfers between devices, exchange(): return lax.ppermute(value, axis, [(i, i ^ mask) for i in range(count)])  15.5 us
    pallas_call x9, Pallas kernels, call(): pl.pallas_call(kernel, out_shape=tuple(outs), in_specs=in_specs, out_spec...  10.5 us
  transfers between devices with their start and end apart: 27, of which 14 were waited for; matrix products, arithmetic and copies ran while one was open for 0% of the time, Pallas kernels for 10%

profile of v5, /device:TPU:0, one launch (start us, length us, event | category | flops | bytes accessed | tf_op | source)
XLA Modules:
  0.0 62.0 jit_solution(14371932188712280812)
XLA Ops:
  0.6 4.1 %collective-permute-start.1 = (bf16[172,256]{1,0:T(8,128)(2,1)}, bf16[172,256]{1,0:T(8,128)(2,1)S(1)}, u32[]{:S(2)}, u32[]{:S(2)}) collective-permute-start(bf16[172,256]{1,0:T(8,128)(2,1)} %bitcast.11), channel_id=1, source_target_pairs={{0,4},{1,5},{2,6},{3,7},{4,0},{5,1},{6,2},{7,3},{8,12},{9,13},{10,... | collective-permute-start | bytes 264200 | tf_op jit(solution)/shard_map/ppermute | solution.py:22
  4.7 1.5 %collective-permute-start = (bf16[256,128]{1,0:T(8,128)(2,1)}, bf16[256,128]{1,0:T(8,128)(2,1)S(1)}, u32[]{:S(2)}, u32[]{:S(2)}) collective-permute-start(bf16[256,128]{1,0:T(8,128)(2,1)} %features_hbm.1), channel_id=1, source_target_pairs={{0,8},{8,0},{16,24},{24,16},{1,9},{9,1},{17,25},{25,17},{2,10},{10... | collective-permute-start | bytes 196616 | tf_op jit(solution)/shard_map/ppermute | solution.py:22
  6.2 1.5 %collective-permute-start.3 = (bf16[256,128]{1,0:T(8,128)(2,1)}, bf16[256,128]{1,0:T(8,128)(2,1)S(1)}, u32[]{:S(2)}, u32[]{:S(2)}) collective-permute-start(bf16[256,128]{1,0:T(8,128)(2,1)} %features_hbm.1), channel_id=1, source_target_pairs={{0,24},{8,16},{16,8},{24,0},{1,25},{9,17},{17,9},{25,1},{2,26},{10... | collective-permute-start | bytes 196616 | tf_op jit(solution)/shard_map/ppermute | solution.py:22
  9.8 2.9 %dense_adjacency.1 = (bf16[2048,1024]{1,0:T(8,128)(2,1)S(1)}, bf16[2,256,128]{2,1,0:T(8,128)(2,1)S(1)}, bf16[172,256]{1,0:T(8,128)(2,1)S(1)}) custom-call(s32[1,1,48]{2,1,0:T(1,128)} %row_hbm.1, s32[1,1,48]{2,1,0:T(1,128)} %col_hbm.1, s32[1,1]{1,0:T(1,128)S(6)} %copy.15.live_hbm, bf16[1,1,48,128,128]{4,3,2,1,0:T(8,128)(2,1)} %tiles_hbm.1, ...), custom_call_target="tpu_custom_call" | custom-call | tf_op jit(solution)/shard_map/dense_adjacency/pallas_call | solution.py:28
  12.8 1.3 %first_product.1 = (bf16[1056,128]{1,0:T(8,128)(2,1)S(1)}, f32[1024,128]{1,0:T(8,128)S(1)}, f32[16,128]{1,0:T(8,128)S(1)}, bf16[2,172,256]{2,1,0:T(8,128)(2,1)S(1)}) custom-call(bf16[2048,1024]{1,0:T(8,128)(2,1)S(1)} %get-tuple-element.38.dense_ref, bf16[172,256]{1,0:T(8,128)(2,1)S(1)} %get-tuple-element.39.g_ref, ...), custom_call_target="tpu_custom_call" | custom-call | tf_op jit(solution)/shard_map/first_product/pallas_call | solution.py:28
  14.2 1.2 %collective-permute-start.5 = (bf16[2,172,256]{2,1,0:T(8,128)(2,1)S(1)}, bf16[2,172,256]{2,1,0:T(8,128)(2,1)S(1)}, u32[]{:S(2)}, u32[]{:S(2)}) collective-permute-start(bf16[2,172,256]{2,1,0:T(8,128)(2,1)S(1)} %get-tuple-element.46.left_ref), channel_id=1, source_target_pairs={{0,2},{1,3},{2,0},{3,1},{4,6},{5,7},{6,4},{7,5},{8,10},{9,11},{10,... | collective-permute-start | bytes 528392 | tf_op jit(solution)/shard_map/ppermute | solution.py:22
  15.8 1.2 %collective-permute-start.6 = (bf16[288,128]{1,0:T(8,128)(2,1)S(1)}, bf16[288,128]{1,0:T(8,128)(2,1)S(1)}, u32[]{:S(2)}, u32[]{:S(2)}) collective-permute-start(bf16[288,128]{1,0:T(8,128)(2,1)S(1)} %get-tuple-element.47), channel_id=1, source_target_pairs={{0,2},{1,3},{2,0},{3,1},{4,6},{5,7},{6,4},{7,5},{8,10},{9,11},{10,... | collective-permute-start | bytes 221192 | tf_op jit(solution)/shard_map/ppermute | solution.py:22
  17.3 2.9 %collective-permute-start.8 = (bf16[288,128]{1,0:T(8,128)(2,1)S(1)}, bf16[288,128]{1,0:T(8,128)(2,1)S(1)}, u32[]{:S(2)}, u32[]{:S(2)}) collective-permute-start(bf16[288,128]{1,0:T(8,128)(2,1)S(1)} %get-tuple-element.49), channel_id=1, source_target_pairs={{0,6},{1,7},{2,4},{3,5},{4,2},{5,3},{6,0},{7,1},{8,14},{9,15},{10,... | collective-permute-start | bytes 221192 | tf_op jit(solution)/shard_map/ppermute | solution.py:22
  20.2 2.6 %collective-permute-done.5.right_ref = bf16[2,172,256]{2,1,0:T(8,128)(2,1)S(1)} collective-permute-done((bf16[2,172,256]{2,1,0:T(8,128)(2,1)S(1)}, bf16[2,172,256]{2,1,0:T(8,128)(2,1)S(1)}, u32[]{:S(2)}, u32[]{:S(2)}) %collective-permute-start.5) | collective-permute-done | bytes 176160 | tf_op jit(solution)/shard_map/ppermute | solution.py:22
  22.9 1.6 %collective-permute-done.6.refs_0_ = bf16[288,128]{1,0:T(8,128)(2,1)S(1)} collective-permute-done((bf16[288,128]{1,0:T(8,128)(2,1)S(1)}, bf16[288,128]{1,0:T(8,128)(2,1)S(1)}, u32[]{:S(2)}, u32[]{:S(2)}) %collective-permute-start.6) | collective-permute-done | bytes 73760 | tf_op jit(solution)/shard_map/ppermute | solution.py:22
  24.5 1.5 %collective-permute-done.7.refs_1_ = bf16[288,128]{1,0:T(8,128)(2,1)S(1)} collective-permute-done((bf16[288,128]{1,0:T(8,128)(2,1)S(1)}, bf16[288,128]{1,0:T(8,128)(2,1)S(1)}, u32[]{:S(2)}, u32[]{:S(2)}) %collective-permute-start.7) | collective-permute-done | bytes 73760 | tf_op jit(solution)/shard_map/ppermute | solution.py:22
  26.2 2.5 %collective-permute-start.12 = (bf16[256,128]{1,0:T(8,128)(2,1)S(1)}, bf16[256,128]{1,0:T(8,128)(2,1)S(1)}, u32[]{:S(2)}, u32[]{:S(2)}) collective-permute-start(bf16[256,128]{1,0:T(8,128)(2,1)S(1)} %get-tuple-element.52.refs_0_), channel_id=1, source_target_pairs={{0,24},{8,16},{16,8},{24,0},{1,25},{9,17},{17,9},{25,1},{2,26},{10... | collective-permute-start | bytes 196616 | tf_op jit(solution)/shard_map/ppermute | solution.py:22
  29.9 0.9 %back_product.1.back_ref = f32[4,176,256]{2,1,0:T(8,128)S(1)} custom-call(bf16[2048,1024]{1,0:T(8,128)(2,1)S(1)} %get-tuple-element.38.dense_ref, f32[16,128]{1,0:T(8,128)S(1)} %get-tuple-element.50.degree_ref, bf16[4,172,256]{2,1,0:T(8,128)(2,1)S(1)} %get-tuple-element.51.near_ref, bf16[4,172,256]{2,1,0:T(8,128)(2,1)S(1)} %collective-permute-done.9.other_ref), custom_call_target="tpu_custom_call" | custom-call | tf_op jit(solution)/shard_map/back_product/pallas_call | solution.py:28
  30.8 0.8 %collective-permute-done.12.refs_3_ = bf16[256,128]{1,0:T(8,128)(2,1)S(1)} collective-permute-done((bf16[256,128]{1,0:T(8,128)(2,1)S(1)}, bf16[256,128]{1,0:T(8,128)(2,1)S(1)}, u32[]{:S(2)}, u32[]{:S(2)}) %collective-permute-start.12) | collective-permute-done | bytes 65568 | tf_op jit(solution)/shard_map/ppermute | solution.py:22
  31.6 1.4 %collective-permute-done.11.refs_2_ = bf16[256,128]{1,0:T(8,128)(2,1)S(1)} collective-permute-done((bf16[256,128]{1,0:T(8,128)(2,1)S(1)}, bf16[256,128]{1,0:T(8,128)(2,1)S(1)}, u32[]{:S(2)}, u32[]{:S(2)}) %collective-permute-start.11) | collective-permute-done | bytes 65568 | tf_op jit(solution)/shard_map/ppermute | solution.py:22
  33.8 2.0 %gradients.1 = (f32[96,256]{1,0:T(8,128)S(1)}, bf16[176,1024]{1,0:T(8,128)(2,1)S(1)}, f32[176,256]{1,0:T(8,128)S(1)}, bf16[96,256]{1,0:T(8,128)(2,1)S(1)}, bf16[...) custom-call(f32[4,176,256]{2,1,0:T(8,128)S(1)} %back_product.1.back_ref, ...), custom_call_target="tpu_custom_call" | custom-call | tf_op jit(solution)/shard_map/gradients/pallas_call | solution.py:28
  35.8 1.1 %collective-permute-start.14 = (bf16[96,256]{1,0:T(8,128)(2,1)S(1)}, bf16[96,256]{1,0:T(8,128)(2,1)S(1)}, u32[]{:S(2)}, u32[]{:S(2)}) collective-permute-start(bf16[96,256]{1,0:T(8,128)(2,1)S(1)} %get-tuple-element.58), channel_id=1, source_target_pairs={{0,8},{8,0},{16,24},{24,16},{1,9},{9,1},{17,25},{25,17},{2,10},{10... | collective-permute-start | bytes 147464 | tf_op jit(solution)/shard_map/ppermute | solution.py:22
  36.9 1.4 %collective-permute-start.15 = (bf16[96,256]{1,0:T(8,128)(2,1)S(1)}, bf16[96,256]{1,0:T(8,128)(2,1)S(1)}, u32[]{:S(2)}, u32[]{:S(2)}) collective-permute-start(bf16[96,256]{1,0:T(8,128)(2,1)S(1)} %get-tuple-element.59), channel_id=1, source_target_pairs={{0,16},{8,24},{16,0},{24,8},{1,17},{9,25},{17,1},{25,9},{2,18},{10... | collective-permute-start | bytes 147464 | tf_op jit(solution)/shard_map/ppermute | solution.py:22
  38.2 1.1 %collective-permute-start.16 = (bf16[96,256]{1,0:T(8,128)(2,1)S(1)}, bf16[96,256]{1,0:T(8,128)(2,1)S(1)}, u32[]{:S(2)}, u32[]{:S(2)}) collective-permute-start(bf16[96,256]{1,0:T(8,128)(2,1)S(1)} %get-tuple-element.60), channel_id=1, source_target_pairs={{0,24},{8,16},{16,8},{24,0},{1,25},{9,17},{17,9},{25,1},{2,26},{10... | collective-permute-start | bytes 147464 | tf_op jit(solution)/shard_map/ppermute | solution.py:22
  39.3 2.0 %second_product.1 = (bf16[4,176,256]{2,1,0:T(8,128)(2,1)S(1)}, f32[4,176,256]{2,1,0:T(8,128)S(1)}) custom-call(bf16[2048,1024]{1,0:T(8,128)(2,1)S(1)} %get-tuple-element.38.dense_ref, bf16[176,1024]{1,0:T(8,128)(2,1)S(1)} %get-tuple-element.53.hidden_ref, f32[176,256]{1,0:T(8,128)S(1)} %get-tuple-element.54.first_ref, f32[96,256]{1,0:T(8,128)S(1)} %get-tuple-element.55.after_ref), custom_call_target="tpu_custom_call" | custom-call | tf_op jit(solution)/shard_map/second_product/pallas_call | solution.py:28
  41.5 1.8 %collective-permute-done.16 = bf16[96,256]{1,0:T(8,128)(2,1)S(1)} collective-permute-done((bf16[96,256]{1,0:T(8,128)(2,1)S(1)}, bf16[96,256]{1,0:T(8,128)(2,1)S(1)}, u32[]{:S(2)}, u32[]{:S(2)}) %collective-permute-start.16) | collective-permute-done | bytes 49184 | tf_op jit(solution)/shard_map/ppermute | solution.py:22
  43.3 1.3 %collective-permute-done.17.far_ref = f32[96,256]{1,0:T(8,128)S(1)} collective-permute-done((f32[96,256]{1,0:T(8,128)S(1)}, f32[96,256]{1,0:T(8,128)S(1)}, u32[]{:S(2)}, u32[]{:S(2)}) %collective-permute-start.17) | collective-permute-done | bytes 98336 | tf_op jit(solution)/shard_map/ppermute | solution.py:22
  44.7 3.0 %collective-permute-start.23 = (bf16[96,256]{1,0:T(8,128)(2,1)S(1)}, bf16[96,256]{1,0:T(8,128)(2,1)S(1)}, u32[]{:S(2)}, u32[]{:S(2)}) collective-permute-start(bf16[96,256]{1,0:T(8,128)(2,1)S(1)} %get-tuple-element.65), channel_id=1, source_target_pairs={{0,6},{1,7},{2,4},{3,5},{4,2},{5,3},{6,0},{7,1},{8,14},{9,15},{10,... | collective-permute-start | bytes 147464 | tf_op jit(solution)/shard_map/ppermute | solution.py:22
  47.8 1.4 %collective-permute-start.21 = (bf16[96,256]{1,0:T(8,128)(2,1)S(1)}, bf16[96,256]{1,0:T(8,128)(2,1)S(1)}, u32[]{:S(2)}, u32[]{:S(2)}) collective-permute-start(bf16[96,256]{1,0:T(8,128)(2,1)S(1)} %get-tuple-element.65), channel_id=1, source_target_pairs={{0,2},{1,3},{2,0},{3,1},{4,6},{5,7},{6,4},{7,5},{8,10},{9,11},{10,... | collective-permute-start | bytes 147464 | tf_op jit(solution)/shard_map/ppermute | solution.py:22
  49.8 2.9 %collective-permute-start.19 = (bf16[176,256]{1,0:T(8,128)(2,1)S(1)}, bf16[176,256]{1,0:T(8,128)(2,1)S(1)}, u32[]{:S(2)}, u32[]{:S(2)}) collective-permute-start(bf16[176,256]{1,0:T(8,128)(2,1)S(1)} %get-tuple-element.63), channel_id=1, source_target_pairs={{0,4},{1,5},{2,6},{3,7},{4,0},{5,1},{6,2},{7,3},{8,12},{9,13},{10,... | collective-permute-start | bytes 270344 | tf_op jit(solution)/shard_map/ppermute | solution.py:22
  52.7 1.5 %collective-permute-start.20 = (bf16[176,256]{1,0:T(8,128)(2,1)S(1)}, bf16[176,256]{1,0:T(8,128)(2,1)S(1)}, u32[]{:S(2)}, u32[]{:S(2)}) collective-permute-start(bf16[176,256]{1,0:T(8,128)(2,1)S(1)} %get-tuple-element.64), channel_id=1, source_target_pairs={{0,6},{1,7},{2,4},{3,5},{4,2},{5,3},{6,0},{7,1},{8,14},{9,15},{10,... | collective-permute-start | bytes 270344 | tf_op jit(solution)/shard_map/ppermute | solution.py:22
  54.5 1.1 %collective-permute-start.26 = (bf16[96,256]{1,0:T(8,128)(2,1)S(1)}, bf16[96,256]{1,0:T(8,128)(2,1)S(1)}, u32[]{:S(2)}, u32[]{:S(2)}) collective-permute-start(bf16[96,256]{1,0:T(8,128)(2,1)S(1)} %add_convert_fusion.refs_3_), channel_id=1, source_target_pairs={{0,24},{8,16},{16,8},{24,0},{1,25},{9,17},{17,9},{25,1},{2,26},{10... | collective-permute-start | bytes 147464 | tf_op jit(solution)/shard_map/ppermute | solution.py:22
  55.6 1.3 %collective-permute-start.25 = (bf16[96,256]{1,0:T(8,128)(2,1)S(1)}, bf16[96,256]{1,0:T(8,128)(2,1)S(1)}, u32[]{:S(2)}, u32[]{:S(2)}) collective-permute-start(bf16[96,256]{1,0:T(8,128)(2,1)S(1)} %add_convert_fusion.refs_3_), channel_id=1, source_target_pairs={{0,16},{8,24},{16,0},{24,8},{1,17},{9,25},{17,1},{25,9},{2,18},{10... | collective-permute-start | bytes 147464 | tf_op jit(solution)/shard_map/ppermute | solution.py:22
  56.9 1.1 %collective-permute-start.24 = (bf16[96,256]{1,0:T(8,128)(2,1)S(1)}, bf16[96,256]{1,0:T(8,128)(2,1)S(1)}, u32[]{:S(2)}, u32[]{:S(2)}) collective-permute-start(bf16[96,256]{1,0:T(8,128)(2,1)S(1)} %add_convert_fusion.refs_3_), channel_id=1, source_target_pairs={{0,8},{8,0},{16,24},{24,16},{1,9},{9,1},{17,25},{25,17},{2,10},{10... | collective-permute-start | bytes 147464 | tf_op jit(solution)/shard_map/ppermute | solution.py:22
  58.0 1.6 %collective-permute-done.19.refs_1_ = bf16[176,256]{1,0:T(8,128)(2,1)S(1)} collective-permute-done((bf16[176,256]{1,0:T(8,128)(2,1)S(1)}, bf16[176,256]{1,0:T(8,128)(2,1)S(1)}, u32[]{:S(2)}, u32[]{:S(2)}) %collective-permute-start.19) | collective-permute-done | bytes 90144 | tf_op jit(solution)/shard_map/ppermute | solution.py:22
  60.1 1.0 %collective-permute-done.24.refs_4_ = bf16[96,256]{1,0:T(8,128)(2,1)S(1)} collective-permute-done((bf16[96,256]{1,0:T(8,128)(2,1)S(1)}, bf16[96,256]{1,0:T(8,128)(2,1)S(1)}, u32[]{:S(2)}, u32[]{:S(2)}) %collective-permute-start.24) | collective-permute-done | bytes 49184 | tf_op jit(solution)/shard_map/ppermute | solution.py:22
  61.0 1.0 %results.1 = (bf16[172,256]{1,0:T(8,128)(2,1)}, f32[128,256]{1,0:T(8,128)}, f32[1,256]{1,0:T(1,128)}, f32[172,256]{1,0:T(8,128)}, f32[1,172]{1,0:T(1,128)}) custom-call(f32[176,256]{1,0:T(8,128)S(1)} %get-tuple-element.61.total_ref, f32[16,128]{1,0:T(8,128)S(1)} %get-tuple-element.50.degree_ref, f32[1,172]{1,0:T(1,128)S(1)} %bitcast.9, ...), custom_call_target="tpu_custom_call" | custom-call | tf_op jit(solution)/shard_map/results/pallas_call | solution.py:28
  (43 shorter events, 6.0 us)
Async XLA Ops:
  0.6 12.1 %collective-permute-start.1 = (bf16[172,256]{1,0:T(8,128)(2,1)}, bf16[172,256]{1,0:T(8,128)(2,1)S(1)}, u32[]{:S(2)}, u32[]{:S(2)}) collective-permute-start(bf16[172,256]{1,0:T(8,128)(2,1)} %bitcast.11), channel_id=1, source_target_pairs={{0,4},{1,5},{2,6},{3,7},{4,0},{5,1},{6,2},{7,3},{8,12},{9,13},{10,... | collective-permute-start | bytes 264200 | tf_op jit(solution)/shard_map/ppermute | solution.py:22
  4.7 4.5 %collective-permute-start = (bf16[256,128]{1,0:T(8,128)(2,1)}, bf16[256,128]{1,0:T(8,128)(2,1)S(1)}, u32[]{:S(2)}, u32[]{:S(2)}) collective-permute-start(bf16[256,128]{1,0:T(8,128)(2,1)} %features_hbm.1), channel_id=1, source_target_pairs={{0,8},{8,0},{16,24},{24,16},{1,9},{9,1},{17,25},{25,17},{2,10},{10... | collective-permute-start | bytes 196616 | tf_op jit(solution)/shard_map/ppermute | solution.py:22
  6.2 6.5 %collective-permute-start.3 = (bf16[256,128]{1,0:T(8,128)(2,1)}, bf16[256,128]{1,0:T(8,128)(2,1)S(1)}, u32[]{:S(2)}, u32[]{:S(2)}) collective-permute-start(bf16[256,128]{1,0:T(8,128)(2,1)} %features_hbm.1), channel_id=1, source_target_pairs={{0,24},{8,16},{16,8},{24,0},{1,25},{9,17},{17,9},{25,1},{2,26},{10... | collective-permute-start | bytes 196616 | tf_op jit(solution)/shard_map/ppermute | solution.py:22
  7.7 5.0 %collective-permute-start.2 = (bf16[256,128]{1,0:T(8,128)(2,1)}, bf16[256,128]{1,0:T(8,128)(2,1)S(1)}, u32[]{:S(2)}, u32[]{:S(2)}) collective-permute-start(bf16[256,128]{1,0:T(8,128)(2,1)} %features_hbm.1), channel_id=1, source_target_pairs={{0,16},{8,24},{16,0},{24,8},{1,17},{9,25},{17,1},{25,9},{2,18},{10... | collective-permute-start | bytes 196616 | tf_op jit(solution)/shard_map/ppermute | solution.py:22
  9.2 0.6 %copy-start.4 = (bf16[256,128]{1,0:T(8,128)(2,1)}, bf16[256,128]{1,0:T(8,128)(2,1)S(1)}, u32[]{:S(2)}) copy-start(bf16[256,128]{1,0:T(8,128)(2,1)S(1)} %collective-permute-done.next_hbm) | copy-start | bytes 196612
  14.1 19.7 %copy-start = (bf16[256,172]{0,1:T(8,128)(2,1)S(1)}, bf16[256,172]{0,1:T(8,128)(2,1)}, u32[]{:S(2)}) copy-start(bf16[256,172]{0,1:T(8,128)(2,1)} %param.17) | copy-start | bytes 264196
  14.1 19.7 %copy-start.1 = (bf16[128,256]{1,0:T(8,128)(2,1)S(1)}, bf16[128,256]{1,0:T(8,128)(2,1)}, u32[]{:S(2)}) copy-start(bf16[128,256]{1,0:T(8,128)(2,1)} %refs_4_.1) | copy-start | bytes 196612
  14.1 19.7 %copy-start.3 = (f32[256]{0:T(256)S(1)}, f32[256]{0:T(256)}, u32[]{:S(2)}) copy-start(f32[256]{0:T(256)} %param.16) | copy-start | bytes 3076
  14.1 1.6 %collective-permute-start.4 = (bf16[1056,128]{1,0:T(8,128)(2,1)S(1)}, bf16[1056,128]{1,0:T(8,128)(2,1)S(1)}, u32[]{:S(2)}, u32[]{:S(2)}) collective-permute-start(bf16[1056,128]{1,0:T(8,128)(2,1)S(1)} %get-tuple-element.42), channel_id=1, source_target_pairs={{0,1},{1,0},{2,3},{3,2},{4,5},{5,4},{6,7},{7,6},{8,9},{9,8},{10,11... | collective-permute-start | bytes 811016 | tf_op jit(solution)/shard_map/ppermute | solution.py:22
  14.2 8.7 %collective-permute-start.5 = (bf16[2,172,256]{2,1,0:T(8,128)(2,1)S(1)}, bf16[2,172,256]{2,1,0:T(8,128)(2,1)S(1)}, u32[]{:S(2)}, u32[]{:S(2)}) collective-permute-start(bf16[2,172,256]{2,1,0:T(8,128)(2,1)S(1)} %get-tuple-element.46.left_ref), channel_id=1, source_target_pairs={{0,2},{1,3},{2,0},{3,1},{4,6},{5,7},{6,4},{7,5},{8,10},{9,11},{10,... | collective-permute-start | bytes 528392 | tf_op jit(solution)/shard_map/ppermute | solution.py:22
  15.8 8.7 %collective-permute-start.6 = (bf16[288,128]{1,0:T(8,128)(2,1)S(1)}, bf16[288,128]{1,0:T(8,128)(2,1)S(1)}, u32[]{:S(2)}, u32[]{:S(2)}) collective-permute-start(bf16[288,128]{1,0:T(8,128)(2,1)S(1)} %get-tuple-element.47), channel_id=1, source_target_pairs={{0,2},{1,3},{2,0},{3,1},{4,6},{5,7},{6,4},{7,5},{8,10},{9,11},{10,... | collective-permute-start | bytes 221192 | tf_op jit(solution)/shard_map/ppermute | solution.py:22
  17.0 8.9 %collective-permute-start.7 = (bf16[288,128]{1,0:T(8,128)(2,1)S(1)}, bf16[288,128]{1,0:T(8,128)(2,1)S(1)}, u32[]{:S(2)}, u32[]{:S(2)}) collective-permute-start(bf16[288,128]{1,0:T(8,128)(2,1)S(1)} %get-tuple-element.48), channel_id=1, source_target_pairs={{0,4},{1,5},{2,6},{3,7},{4,0},{5,1},{6,2},{7,3},{8,12},{9,13},{10,... | collective-permute-start | bytes 221192 | tf_op jit(solution)/shard_map/ppermute | solution.py:22
  17.3 8.6 %collective-permute-start.8 = (bf16[288,128]{1,0:T(8,128)(2,1)S(1)}, bf16[288,128]{1,0:T(8,128)(2,1)S(1)}, u32[]{:S(2)}, u32[]{:S(2)}) collective-permute-start(bf16[288,128]{1,0:T(8,128)(2,1)S(1)} %get-tuple-element.49), channel_id=1, source_target_pairs={{0,6},{1,7},{2,4},{3,5},{4,2},{5,3},{6,0},{7,1},{8,14},{9,15},{10,... | collective-permute-start | bytes 221192 | tf_op jit(solution)/shard_map/ppermute | solution.py:22
  26.1 3.7 %collective-permute-start.9 = (bf16[4,172,256]{2,1,0:T(8,128)(2,1)S(1)}, bf16[4,172,256]{2,1,0:T(8,128)(2,1)S(1)}, u32[]{:S(2)}, u32[]{:S(2)}) collective-permute-start(bf16[4,172,256]{2,1,0:T(8,128)(2,1)S(1)} %get-tuple-element.51.near_ref), channel_id=1, source_target_pairs={{0,1},{1,0},{2,3},{3,2},{4,5},{5,4},{6,7},{7,6},{8,9},{9,8},{10,11... | collective-permute-start | bytes 1056776 | tf_op jit(solution)/shard_map/ppermute | solution.py:22
  26.2 5.4 %collective-permute-start.12 = (bf16[256,128]{1,0:T(8,128)(2,1)S(1)}, bf16[256,128]{1,0:T(8,128)(2,1)S(1)}, u32[]{:S(2)}, u32[]{:S(2)}) collective-permute-start(bf16[256,128]{1,0:T(8,128)(2,1)S(1)} %get-tuple-element.52.refs_0_), channel_id=1, source_target_pairs={{0,24},{8,16},{16,8},{24,0},{1,25},{9,17},{17,9},{25,1},{2,26},{10... | collective-permute-start | bytes 196616 | tf_op jit(solution)/shard_map/ppermute | solution.py:22
  28.7 4.3 %collective-permute-start.11 = (bf16[256,128]{1,0:T(8,128)(2,1)S(1)}, bf16[256,128]{1,0:T(8,128)(2,1)S(1)}, u32[]{:S(2)}, u32[]{:S(2)}) collective-permute-start(bf16[256,128]{1,0:T(8,128)(2,1)S(1)} %get-tuple-element.52.refs_0_), channel_id=1, source_target_pairs={{0,16},{8,24},{16,0},{24,8},{1,17},{9,25},{17,1},{25,9},{2,18},{10... | collective-permute-start | bytes 196616 | tf_op jit(solution)/shard_map/ppermute | solution.py:22
  29.5 4.3 %collective-permute-start.10 = (bf16[256,128]{1,0:T(8,128)(2,1)S(1)}, bf16[256,128]{1,0:T(8,128)(2,1)S(1)}, u32[]{:S(2)}, u32[]{:S(2)}) collective-permute-start(bf16[256,128]{1,0:T(8,128)(2,1)S(1)} %get-tuple-element.52.refs_0_), channel_id=1, source_target_pairs={{0,8},{8,0},{16,24},{24,16},{1,9},{9,1},{17,25},{25,17},{2,10},{10... | collective-permute-start | bytes 196616 | tf_op jit(solution)/shard_map/ppermute | solution.py:22
  30.8 30.2 %copy-start.2 = (f32[172]{0:T(256)S(1)}, f32[172]{0:T(256)}, u32[]{:S(2)}) copy-start(f32[172]{0:T(256)} %param.18) | copy-start | bytes 2068
  35.8 5.7 %collective-permute-start.14 = (bf16[96,256]{1,0:T(8,128)(2,1)S(1)}, bf16[96,256]{1,0:T(8,128)(2,1)S(1)}, u32[]{:S(2)}, u32[]{:S(2)}) collective-permute-start(bf16[96,256]{1,0:T(8,128)(2,1)S(1)} %get-tuple-element.58), channel_id=1, source_target_pairs={{0,8},{8,0},{16,24},{24,16},{1,9},{9,1},{17,25},{25,17},{2,10},{10... | collective-permute-start | bytes 147464 | tf_op jit(solution)/shard_map/ppermute | solution.py:22
  36.9 4.6 %collective-permute-start.15 = (bf16[96,256]{1,0:T(8,128)(2,1)S(1)}, bf16[96,256]{1,0:T(8,128)(2,1)S(1)}, u32[]{:S(2)}, u32[]{:S(2)}) collective-permute-start(bf16[96,256]{1,0:T(8,128)(2,1)S(1)} %get-tuple-element.59), channel_id=1, source_target_pairs={{0,16},{8,24},{16,0},{24,8},{1,17},{9,25},{17,1},{25,9},{2,18},{10... | collective-permute-start | bytes 147464 | tf_op jit(solution)/shard_map/ppermute | solution.py:22
  38.2 5.0 %collective-permute-start.16 = (bf16[96,256]{1,0:T(8,128)(2,1)S(1)}, bf16[96,256]{1,0:T(8,128)(2,1)S(1)}, u32[]{:S(2)}, u32[]{:S(2)}) collective-permute-start(bf16[96,256]{1,0:T(8,128)(2,1)S(1)} %get-tuple-element.60), channel_id=1, source_target_pairs={{0,24},{8,16},{16,8},{24,0},{1,25},{9,17},{17,9},{25,1},{2,26},{10... | collective-permute-start | bytes 147464 | tf_op jit(solution)/shard_map/ppermute | solution.py:22
  41.4 3.2 %collective-permute-start.13 = (bf16[4,176,256]{2,1,0:T(8,128)(2,1)S(1)}, bf16[4,176,256]{2,1,0:T(8,128)(2,1)S(1)}, u32[]{:S(2)}, u32[]{:S(2)}) collective-permute-start(bf16[4,176,256]{2,1,0:T(8,128)(2,1)S(1)} %get-tuple-element.57), channel_id=1, source_target_pairs={{0,1},{1,0},{2,3},{3,2},{4,5},{5,4},{6,7},{7,6},{8,9},{9,8},{10,11... | collective-permute-start | bytes 1081352 | tf_op jit(solution)/shard_map/ppermute | solution.py:22
  43.3 1.4 %collective-permute-start.17 = (f32[96,256]{1,0:T(8,128)S(1)}, f32[96,256]{1,0:T(8,128)S(1)}, u32[]{:S(2)}, u32[]{:S(2)}) collective-permute-start(f32[96,256]{1,0:T(8,128)S(1)} %convert_add_fusion.mine_ref), channel_id=1, source_target_pairs={{0,1},{1,0},{2,3},{3,2},{4,5},{5,4},{6,7},{7,6},{8,9},{9,8},{10,11... | collective-permute-start | bytes 294920 | tf_op jit(solution)/shard_map/ppermute | solution.py:22
  44.7 8.0 %collective-permute-start.23 = (bf16[96,256]{1,0:T(8,128)(2,1)S(1)}, bf16[96,256]{1,0:T(8,128)(2,1)S(1)}, u32[]{:S(2)}, u32[]{:S(2)}) collective-permute-start(bf16[96,256]{1,0:T(8,128)(2,1)S(1)} %get-tuple-element.65), channel_id=1, source_target_pairs={{0,6},{1,7},{2,4},{3,5},{4,2},{5,3},{6,0},{7,1},{8,14},{9,15},{10,... | collective-permute-start | bytes 147464 | tf_op jit(solution)/shard_map/ppermute | solution.py:22
  47.8 6.5 %collective-permute-start.22 = (bf16[96,256]{1,0:T(8,128)(2,1)S(1)}, bf16[96,256]{1,0:T(8,128)(2,1)S(1)}, u32[]{:S(2)}, u32[]{:S(2)}) collective-permute-start(bf16[96,256]{1,0:T(8,128)(2,1)S(1)} %get-tuple-element.65), channel_id=1, source_target_pairs={{0,4},{1,5},{2,6},{3,7},{4,0},{5,1},{6,2},{7,3},{8,12},{9,13},{10,... | collective-permute-start | bytes 147464 | tf_op jit(solution)/shard_map/ppermute | solution.py:22
  47.8 6.7 %collective-permute-start.21 = (bf16[96,256]{1,0:T(8,128)(2,1)S(1)}, bf16[96,256]{1,0:T(8,128)(2,1)S(1)}, u32[]{:S(2)}, u32[]{:S(2)}) collective-permute-start(bf16[96,256]{1,0:T(8,128)(2,1)S(1)} %get-tuple-element.65), channel_id=1, source_target_pairs={{0,2},{1,3},{2,0},{3,1},{4,6},{5,7},{6,4},{7,5},{8,10},{9,11},{10,... | collective-permute-start | bytes 147464 | tf_op jit(solution)/shard_map/ppermute | solution.py:22
  49.2 7.7 %collective-permute-start.18 = (bf16[176,256]{1,0:T(8,128)(2,1)S(1)}, bf16[176,256]{1,0:T(8,128)(2,1)S(1)}, u32[]{:S(2)}, u32[]{:S(2)}) collective-permute-start(bf16[176,256]{1,0:T(8,128)(2,1)S(1)} %get-tuple-element.62), channel_id=1, source_target_pairs={{0,2},{1,3},{2,0},{3,1},{4,6},{5,7},{6,4},{7,5},{8,10},{9,11},{10,... | collective-permute-start | bytes 270344 | tf_op jit(solution)/shard_map/ppermute | solution.py:22
  49.8 9.8 %collective-permute-start.19 = (bf16[176,256]{1,0:T(8,128)(2,1)S(1)}, bf16[176,256]{1,0:T(8,128)(2,1)S(1)}, u32[]{:S(2)}, u32[]{:S(2)}) collective-permute-start(bf16[176,256]{1,0:T(8,128)(2,1)S(1)} %get-tuple-element.63), channel_id=1, source_target_pairs={{0,4},{1,5},{2,6},{3,7},{4,0},{5,1},{6,2},{7,3},{8,12},{9,13},{10,... | collective-permute-start | bytes 270344 | tf_op jit(solution)/shard_map/ppermute | solution.py:22
  52.7 6.9 %collective-permute-start.20 = (bf16[176,256]{1,0:T(8,128)(2,1)S(1)}, bf16[176,256]{1,0:T(8,128)(2,1)S(1)}, u32[]{:S(2)}, u32[]{:S(2)}) collective-permute-start(bf16[176,256]{1,0:T(8,128)(2,1)S(1)} %get-tuple-element.64), channel_id=1, source_target_pairs={{0,6},{1,7},{2,4},{3,5},{4,2},{5,3},{6,0},{7,1},{8,14},{9,15},{10,... | collective-permute-start | bytes 270344 | tf_op jit(solution)/shard_map/ppermute | solution.py:22
  54.5 5.2 %collective-permute-start.26 = (bf16[96,256]{1,0:T(8,128)(2,1)S(1)}, bf16[96,256]{1,0:T(8,128)(2,1)S(1)}, u32[]{:S(2)}, u32[]{:S(2)}) collective-permute-start(bf16[96,256]{1,0:T(8,128)(2,1)S(1)} %add_convert_fusion.refs_3_), channel_id=1, source_target_pairs={{0,24},{8,16},{16,8},{24,0},{1,25},{9,17},{17,9},{25,1},{2,26},{10... | collective-permute-start | bytes 147464 | tf_op jit(solution)/shard_map/ppermute | solution.py:22
  55.6 4.4 %collective-permute-start.25 = (bf16[96,256]{1,0:T(8,128)(2,1)S(1)}, bf16[96,256]{1,0:T(8,128)(2,1)S(1)}, u32[]{:S(2)}, u32[]{:S(2)}) collective-permute-start(bf16[96,256]{1,0:T(8,128)(2,1)S(1)} %add_convert_fusion.refs_3_), channel_id=1, source_target_pairs={{0,16},{8,24},{16,0},{24,8},{1,17},{9,25},{17,1},{25,9},{2,18},{10... | collective-permute-start | bytes 147464 | tf_op jit(solution)/shard_map/ppermute | solution.py:22
  56.9 4.1 %collective-permute-start.24 = (bf16[96,256]{1,0:T(8,128)(2,1)S(1)}, bf16[96,256]{1,0:T(8,128)(2,1)S(1)}, u32[]{:S(2)}, u32[]{:S(2)}) collective-permute-start(bf16[96,256]{1,0:T(8,128)(2,1)S(1)} %add_convert_fusion.refs_3_), channel_id=1, source_target_pairs={{0,8},{8,0},{16,24},{24,16},{1,9},{9,1},{17,25},{25,17},{2,10},{10... | collective-permute-start | bytes 147464 | tf_op jit(solution)/shard_map/ppermute | solution.py:22

commit v6 on v5

--- a/solution.py
+++ b/solution.py
@@ -174,15 +174,18 @@
     return value, slope
 
 
-def second_kernel(dense_ref, hidden_ref, first_ref, after_ref, send_ref, keep_ref):
+def second_kernel(spans, dense_ref, outer_ref, inner_ref, first_ref, after_ref, send_ref, keep_ref, held):
     half, _, nodes = keep_ref.shape
+    held[:, :nodes] = outer_ref[:, :nodes]
+    held[:, nodes : (spans - 1) * nodes] = inner_ref[...]
+    held[:, (spans - 1) * nodes :] = outer_ref[:, nodes:]
 
     @pl.loop(0, half)
     def _(s):
         at = pl.multiple_of((half + s) * nodes, nodes)
-        send_ref[s] = product(hidden_ref[...], dense_ref[pl.ds(at, nodes), :], ((1,), (1,))).astype(BF16)
+        send_ref[s] = product(held[...], dense_ref[pl.ds(at, nodes), :], ((1,), (1,))).astype(BF16)
         at = pl.multiple_of(s * nodes, nodes)
-        keep_ref[s] = product(hidden_ref[...], dense_ref[pl.ds(at, nodes), :], ((1,), (1,)))
+        keep_ref[s] = product(held[...], dense_ref[pl.ds(at, nodes), :], ((1,), (1,)))
 
     keep_ref[0] += first_ref[...]
 
@@ -204,26 +207,22 @@
         back_ref[s] = part
 
 
-def grad_kernel(spans, back_ref, g_ref, *refs):
-    pieces, refs = refs[:spans], refs[spans:]
-    w1_ref, b1_ref, w2_ref, mine_ref, hidden_ref, first_ref, refs = refs[0], refs[1], refs[2], refs[3], refs[4], refs[5], refs[6:]
-    sends, total = refs[: spans - 1], refs[-1]
+def grad_parts(places, back_ref, pieces, w1_ref, b1_ref, w2_ref, hidden_ref, first_ref):
     fin, hidden = w1_ref.shape
     block = LANES
     tall = back_ref.shape[1]
-    rank = lax.axis_index("row")
     nodes = pieces[0].shape[0]
     classes = w2_ref.shape[0]
     w2 = jnp.concatenate([w2_ref[...].astype(F32), jnp.zeros((2 * block - classes, hidden), F32)], axis=0).astype(BF16)
     grad_w1 = jnp.zeros((fin, hidden), F32)
     grad_w2 = jnp.zeros((tall, hidden), F32)
     grad_b1 = jnp.zeros((1, hidden), F32)
-    for s in range(spans):
-        agg = pieces[s][...]
+    for n, s in enumerate(places):
+        agg = pieces[n][...]
         value, slope = gelu_parts(product(agg, w1_ref[...]) + b1_ref[...])
         h = value.astype(BF16)
         projected = product(w2, h, ((1,), (1,)))[:tall]
-        hidden_ref[:, s * nodes : (s + 1) * nodes] = projected.astype(BF16)
+        hidden_ref[:, n * nodes : (n + 1) * nodes] = projected.astype(BF16)
         if s == 0:
             first_ref[...] = projected
         q = back_ref[s]
@@ -233,6 +232,26 @@
         d_first = (product(high, w2) + product(low, w2)) * slope
         grad_w1 = grad_w1 + product(agg.astype(F32).T.astype(BF16), d_first.astype(BF16))
         grad_b1 = grad_b1 + jnp.sum(d_first, axis=0, keepdims=True)
+    return grad_w1, grad_w2, grad_b1
+
+
+def early_kernel(places, back_ref, own_ref, last_ref, w1_ref, b1_ref, w2_ref, *refs):
+    out1_ref, out2_ref, bias_ref, hidden_ref, first_ref = refs
+    out1_ref[...], out2_ref[...], bias_ref[...] = grad_parts(
+        places, back_ref, (own_ref, last_ref), w1_ref, b1_ref, w2_ref, hidden_ref, first_ref
+    )
+
+
+def grad_kernel(spans, places, back_ref, g_ref, in1_ref, in2_ref, inb_ref, *refs):
+    pieces, refs = refs[: len(places)], refs[len(places) :]
+    w1_ref, b1_ref, w2_ref, mine_ref, hidden_ref, refs = refs[0], refs[1], refs[2], refs[3], refs[4], refs[5:]
+    sends, total = refs[: spans - 1], refs[-1]
+    fin = w1_ref.shape[0]
+    classes, nodes = g_ref.shape
+    tall = back_ref.shape[1]
+    rank = lax.axis_index("row")
+    parts = grad_parts(places, back_ref, pieces, w1_ref, b1_ref, w2_ref, hidden_ref, None)
+    grad_w1, grad_w2, grad_b1 = in1_ref[...] + parts[0], in2_ref[...] + parts[1], inb_ref[...] + parts[2]
     grad_b2 = product(jnp.ones((8, nodes), BF16), g_ref[...], ((1,), (1,)))[:1]
     a = fin // spans
     b = total.shape[1] - a - 16
@@ -389,25 +408,41 @@
         [dense, degree, near_g, other_g],
         scratch=[pltpu.VMEM((tall, rows), BF16)],
     )[0]
+    outer = [0, row_count - 1]
+    inner = list(range(1, row_count - 1))
+    early = call(
+        functools.partial(early_kernel, outer),
+        "gradients_early",
+        [
+            shaped((fin, hidden), F32),
+            shaped((tall, hidden), F32),
+            shaped((1, hidden), F32),
+            shaped((tall, 2 * nodes), BF16),
+            shaped((tall, nodes), F32),
+        ],
+        [VMEM] * 6,
+        [back, pieces[0], pieces[-1], w_first, bias, w2],
+    )
     out = call(
-        functools.partial(grad_kernel, row_count),
+        functools.partial(grad_kernel, row_count, inner),
         "gradients",
-        [shaped((size, hidden), F32), shaped((tall, columns), BF16), shaped((tall, nodes), F32)]
+        [shaped((size, hidden), F32), shaped((tall, columns - 2 * nodes), BF16)]
         + [shaped((size, hidden), BF16)] * (row_count - 1),
-        [VMEM] * (2 + row_count + 3),
-        [back, own_g] + pieces + [w_first, bias, w2],
+        [VMEM] * (5 + row_count - 2 + 3),
+        [back, own_g, *early[:3]] + pieces[1:-1] + [w_first, bias, w2],
         scratch=[pltpu.VMEM((row_count, size, hidden), F32)],
     )
     mine = out[0]
     for s in range(1, row_count):
-        mine = mine + exchange(out[2 + s], "row", s).astype(F32)
+        mine = mine + exchange(out[1 + s], "row", s).astype(F32)
 
     send, keep = call(
-        second_kernel,
+        functools.partial(second_kernel, row_count),
         "second_product",
         [shaped((half, tall, nodes), BF16), shaped((half, tall, nodes), F32)],
-        [VMEM, VMEM, VMEM, ANY],
-        [dense, out[1], out[2], out[0]],
+        [VMEM, VMEM, VMEM, VMEM, ANY],
+        [dense, early[3], out[1], early[4], out[0]],
+        scratch=[pltpu.VMEM((tall, columns), BF16)],
     )
     out = call(
         functools.partial(core_kernel, half),

time: 62.1 us -> 61.1 us (0.984)
  waiting for transfers between devices: 15.5 us -> 14.8 us
    ppermute x27, waiting for transfers between devices: 15.5 us -> 14.8 us  [exchange(): return lax.ppermute(value, axis, [(i, i ^ mask) for i in range(count)])]
    pallas_call x9 -> x10, Pallas kernels: 10.5 us -> 10.1 us  [call(): pl.pallas_call(kernel, out_shape=tuple(outs), in_specs=in_specs, out_spec...]
where the time goes in v6:
time: 61.1 us; the launch traced here: 61.3 us
  starting transfers between devices  34.2 us (56%)
  waiting for transfers between devices  14.8 us (24%)
  Pallas kernels  10.1 us (17%)
  between operations  1.45 us (2%)
  local copies, waits for them, and re-layouts  0.65 us (1%)
    ppermute x27, starting transfers between devices, exchange(): return lax.ppermute(value, axis, [(i, i ^ mask) for i in range(count)])  34.2 us
    ppermute x27, waiting for transfers between devices, exchange(): return lax.ppermute(value, axis, [(i, i ^ mask) for i in range(count)])  14.8 us
    pallas_call x10, Pallas kernels, call(): pl.pallas_call(kernel, out_shape=tuple(outs), in_specs=in_specs, out_spec...  10.1 us
  transfers between devices with their start and end apart: 27, of which 14 were waited for; matrix products, arithmetic and copies ran while one was open for 0% of the time, Pallas kernels for 10%

profile of v6, /device:TPU:0, one launch (start us, length us, event | category | flops | bytes accessed | tf_op | source)
XLA Modules:
  0.0 61.3 jit_solution(10244608592447511407)
XLA Ops:
  0.6 4.1 %collective-permute-start.1 = (bf16[172,256]{1,0:T(8,128)(2,1)}, bf16[172,256]{1,0:T(8,128)(2,1)S(1)}, u32[]{:S(2)}, u32[]{:S(2)}) collective-permute-start(bf16[172,256]{1,0:T(8,128)(2,1)} %bitcast.13), channel_id=1, source_target_pairs={{0,4},{1,5},{2,6},{3,7},{4,0},{5,1},{6,2},{7,3},{8,12},{9,13},{10,... | collective-permute-start | bytes 264200 | tf_op jit(solution)/shard_map/ppermute | solution.py:22
  4.7 1.5 %collective-permute-start = (bf16[256,128]{1,0:T(8,128)(2,1)}, bf16[256,128]{1,0:T(8,128)(2,1)S(1)}, u32[]{:S(2)}, u32[]{:S(2)}) collective-permute-start(bf16[256,128]{1,0:T(8,128)(2,1)} %features_hbm.1), channel_id=1, source_target_pairs={{0,8},{8,0},{16,24},{24,16},{1,9},{9,1},{17,25},{25,17},{2,10},{10... | collective-permute-start | bytes 196616 | tf_op jit(solution)/shard_map/ppermute | solution.py:22
  6.2 1.5 %collective-permute-start.3 = (bf16[256,128]{1,0:T(8,128)(2,1)}, bf16[256,128]{1,0:T(8,128)(2,1)S(1)}, u32[]{:S(2)}, u32[]{:S(2)}) collective-permute-start(bf16[256,128]{1,0:T(8,128)(2,1)} %features_hbm.1), channel_id=1, source_target_pairs={{0,24},{8,16},{16,8},{24,0},{1,25},{9,17},{17,9},{25,1},{2,26},{10... | collective-permute-start | bytes 196616 | tf_op jit(solution)/shard_map/ppermute | solution.py:22
  9.8 2.4 %dense_adjacency.1 = (bf16[2048,1024]{1,0:T(8,128)(2,1)S(1)}, bf16[2,256,128]{2,1,0:T(8,128)(2,1)S(1)}, bf16[172,256]{1,0:T(8,128)(2,1)S(1)}) custom-call(s32[1,1,48]{2,1,0:T(1,128)} %row_hbm.1, s32[1,1,48]{2,1,0:T(1,128)} %col_hbm.1, s32[1,1]{1,0:T(1,128)S(6)} %copy.15.live_hbm, bf16[1,1,48,128,128]{4,3,2,1,0:T(8,128)(2,1)} %tiles_hbm.1, ...), custom_call_target="tpu_custom_call" | custom-call | tf_op jit(solution)/shard_map/dense_adjacency/pallas_call | solution.py:28
  12.3 1.3 %first_product.1 = (bf16[1056,128]{1,0:T(8,128)(2,1)S(1)}, f32[1024,128]{1,0:T(8,128)S(1)}, f32[16,128]{1,0:T(8,128)S(1)}, bf16[2,172,256]{2,1,0:T(8,128)(2,1)S(1)}) custom-call(bf16[2048,1024]{1,0:T(8,128)(2,1)S(1)} %get-tuple-element.42.dense_ref, bf16[172,256]{1,0:T(8,128)(2,1)S(1)} %get-tuple-element.43.g_ref, ...), custom_call_target="tpu_custom_call" | custom-call | tf_op jit(solution)/shard_map/first_product/pallas_call | solution.py:28
  13.8 1.6 %collective-permute-start.5 = (bf16[2,172,256]{2,1,0:T(8,128)(2,1)S(1)}, bf16[2,172,256]{2,1,0:T(8,128)(2,1)S(1)}, u32[]{:S(2)}, u32[]{:S(2)}) collective-permute-start(bf16[2,172,256]{2,1,0:T(8,128)(2,1)S(1)} %get-tuple-element.50.left_ref), channel_id=1, source_target_pairs={{0,2},{1,3},{2,0},{3,1},{4,6},{5,7},{6,4},{7,5},{8,10},{9,11},{10,... | collective-permute-start | bytes 528392 | tf_op jit(solution)/shard_map/ppermute | solution.py:22
  15.4 1.5 %collective-permute-start.6 = (bf16[288,128]{1,0:T(8,128)(2,1)S(1)}, bf16[288,128]{1,0:T(8,128)(2,1)S(1)}, u32[]{:S(2)}, u32[]{:S(2)}) collective-permute-start(bf16[288,128]{1,0:T(8,128)(2,1)S(1)} %get-tuple-element.51), channel_id=1, source_target_pairs={{0,2},{1,3},{2,0},{3,1},{4,6},{5,7},{6,4},{7,5},{8,10},{9,11},{10,... | collective-permute-start | bytes 221192 | tf_op jit(solution)/shard_map/ppermute | solution.py:22
  17.4 2.5 %collective-permute-start.8 = (bf16[288,128]{1,0:T(8,128)(2,1)S(1)}, bf16[288,128]{1,0:T(8,128)(2,1)S(1)}, u32[]{:S(2)}, u32[]{:S(2)}) collective-permute-start(bf16[288,128]{1,0:T(8,128)(2,1)S(1)} %get-tuple-element.53), channel_id=1, source_target_pairs={{0,6},{1,7},{2,4},{3,5},{4,2},{5,3},{6,0},{7,1},{8,14},{9,15},{10,... | collective-permute-start | bytes 221192 | tf_op jit(solution)/shard_map/ppermute | solution.py:22
  19.9 2.3 %collective-permute-done.5.right_ref = bf16[2,172,256]{2,1,0:T(8,128)(2,1)S(1)} collective-permute-done((bf16[2,172,256]{2,1,0:T(8,128)(2,1)S(1)}, bf16[2,172,256]{2,1,0:T(8,128)(2,1)S(1)}, u32[]{:S(2)}, u32[]{:S(2)}) %collective-permute-start.5) | collective-permute-done | bytes 176160 | tf_op jit(solution)/shard_map/ppermute | solution.py:22
  22.2 1.4 %collective-permute-done.6.refs_0_ = bf16[288,128]{1,0:T(8,128)(2,1)S(1)} collective-permute-done((bf16[288,128]{1,0:T(8,128)(2,1)S(1)}, bf16[288,128]{1,0:T(8,128)(2,1)S(1)}, u32[]{:S(2)}, u32[]{:S(2)}) %collective-permute-start.6) | collective-permute-done | bytes 73760 | tf_op jit(solution)/shard_map/ppermute | solution.py:22
  23.6 2.3 %collective-permute-done.7.refs_1_ = bf16[288,128]{1,0:T(8,128)(2,1)S(1)} collective-permute-done((bf16[288,128]{1,0:T(8,128)(2,1)S(1)}, bf16[288,128]{1,0:T(8,128)(2,1)S(1)}, u32[]{:S(2)}, u32[]{:S(2)}) %collective-permute-start.7) | collective-permute-done | bytes 73760 | tf_op jit(solution)/shard_map/ppermute | solution.py:22
  26.2 2.9 %collective-permute-start.10 = (bf16[256,128]{1,0:T(8,128)(2,1)S(1)}, bf16[256,128]{1,0:T(8,128)(2,1)S(1)}, u32[]{:S(2)}, u32[]{:S(2)}) collective-permute-start(bf16[256,128]{1,0:T(8,128)(2,1)S(1)} %get-tuple-element.56.own_ref), channel_id=1, source_target_pairs={{0,24},{8,16},{16,8},{24,0},{1,25},{9,17},{17,9},{25,1},{2,26},{10... | collective-permute-start | bytes 196616 | tf_op jit(solution)/shard_map/ppermute | solution.py:22
  29.8 0.9 %back_product.1.back_ref = f32[4,176,256]{2,1,0:T(8,128)S(1)} custom-call(bf16[2048,1024]{1,0:T(8,128)(2,1)S(1)} %get-tuple-element.42.dense_ref, f32[16,128]{1,0:T(8,128)S(1)} %get-tuple-element.54.degree_ref, bf16[4,172,256]{2,1,0:T(8,128)(2,1)S(1)} %get-tuple-element.55.near_ref, bf16[4,172,256]{2,1,0:T(8,128)(2,1)S(1)} %collective-permute-done.9.other_ref), custom_call_target="tpu_custom_call" | custom-call | tf_op jit(solution)/shard_map/back_product/pallas_call | solution.py:28
  30.8 1.0 %collective-permute-done.10.last_ref = bf16[256,128]{1,0:T(8,128)(2,1)S(1)} collective-permute-done((bf16[256,128]{1,0:T(8,128)(2,1)S(1)}, bf16[256,128]{1,0:T(8,128)(2,1)S(1)}, u32[]{:S(2)}, u32[]{:S(2)}) %collective-permute-start.10) | collective-permute-done | bytes 65568 | tf_op jit(solution)/shard_map/ppermute | solution.py:22
  31.8 1.0 %gradients_early.1 = (f32[128,256]{1,0:T(8,128)S(1)}, f32[176,256]{1,0:T(8,128)S(1)}, f32[1,256]{1,0:T(1,128)S(1)}, bf16[176,512]{1,0:T(8,128)(2,1)S(1)}, f32[176,256]{1,0:T(8,128)S(1)}) custom-call(f32[4,176,256]{2,1,0:T(8,128)S(1)} %back_product.1.back_ref, bf16[256,128]{1,0:T(8,128)(2,1)S(1)} %get-tuple-element.56.own_ref, ...), custom_call_target="tpu_custom_call" | custom-call | tf_op jit(solution)/shard_map/gradients_early/pallas_call | solution.py:28
  33.8 1.0 %gradients.1 = (f32[96,256]{1,0:T(8,128)S(1)}, bf16[176,512]{1,0:T(8,128)(2,1)S(1)}, bf16[96,256]{1,0:T(8,128)(2,1)S(1)}, bf16[96,256]{1,0:T(8,128)(2,1)S(1)}, bf16[96,256]{1,0:T(8,128)(2,1)S(1)}) custom-call(f32[4,176,256]{2,1,0:T(8,128)S(1)} %back_product.1.back_ref, bf16[172,256]{1,0:T(8,128)(2,1)S(1)} %get-tuple-element.43.g_ref, ...), custom_call_target="tpu_custom_call" | custom-call | tf_op jit(solution)/shard_map/gradients/pallas_call | solution.py:28
  34.9 1.2 %collective-permute-start.14 = (bf16[96,256]{1,0:T(8,128)(2,1)S(1)}, bf16[96,256]{1,0:T(8,128)(2,1)S(1)}, u32[]{:S(2)}, u32[]{:S(2)}) collective-permute-start(bf16[96,256]{1,0:T(8,128)(2,1)S(1)} %get-tuple-element.66), channel_id=1, source_target_pairs={{0,8},{8,0},{16,24},{24,16},{1,9},{9,1},{17,25},{25,17},{2,10},{10... | collective-permute-start | bytes 147464 | tf_op jit(solution)/shard_map/ppermute | solution.py:22
  36.0 1.5 %collective-permute-start.15 = (bf16[96,256]{1,0:T(8,128)(2,1)S(1)}, bf16[96,256]{1,0:T(8,128)(2,1)S(1)}, u32[]{:S(2)}, u32[]{:S(2)}) collective-permute-start(bf16[96,256]{1,0:T(8,128)(2,1)S(1)} %get-tuple-element.67), channel_id=1, source_target_pairs={{0,16},{8,24},{16,0},{24,8},{1,17},{9,25},{17,1},{25,9},{2,18},{10... | collective-permute-start | bytes 147464 | tf_op jit(solution)/shard_map/ppermute | solution.py:22
  37.6 0.8 %collective-permute-start.16 = (bf16[96,256]{1,0:T(8,128)(2,1)S(1)}, bf16[96,256]{1,0:T(8,128)(2,1)S(1)}, u32[]{:S(2)}, u32[]{:S(2)}) collective-permute-start(bf16[96,256]{1,0:T(8,128)(2,1)S(1)} %get-tuple-element.68), channel_id=1, source_target_pairs={{0,24},{8,16},{16,8},{24,0},{1,25},{9,17},{17,9},{25,1},{2,26},{10... | collective-permute-start | bytes 147464 | tf_op jit(solution)/shard_map/ppermute | solution.py:22
  38.4 2.1 %second_product.1 = (bf16[4,176,256]{2,1,0:T(8,128)(2,1)S(1)}, f32[4,176,256]{2,1,0:T(8,128)S(1)}) custom-call(bf16[2048,1024]{1,0:T(8,128)(2,1)S(1)} %get-tuple-element.42.dense_ref, bf16[176,512]{1,0:T(8,128)(2,1)S(1)} %get-tuple-element.57.outer_ref, bf16[176,512]{1,0:T(8,128)(2,1)S(1)} %get-tuple-element.61.inner_ref, ...), custom_call_target="tpu_custom_call" | custom-call | tf_op jit(solution)/shard_map/second_product/pallas_call | solution.py:28
  40.7 1.9 %collective-permute-done.16 = bf16[96,256]{1,0:T(8,128)(2,1)S(1)} collective-permute-done((bf16[96,256]{1,0:T(8,128)(2,1)S(1)}, bf16[96,256]{1,0:T(8,128)(2,1)S(1)}, u32[]{:S(2)}, u32[]{:S(2)}) %collective-permute-start.16) | collective-permute-done | bytes 49184 | tf_op jit(solution)/shard_map/ppermute | solution.py:22
  42.7 1.3 %collective-permute-done.17.far_ref = f32[96,256]{1,0:T(8,128)S(1)} collective-permute-done((f32[96,256]{1,0:T(8,128)S(1)}, f32[96,256]{1,0:T(8,128)S(1)}, u32[]{:S(2)}, u32[]{:S(2)}) %collective-permute-start.17) | collective-permute-done | bytes 98336 | tf_op jit(solution)/shard_map/ppermute | solution.py:22
  44.1 3.0 %collective-permute-start.23 = (bf16[96,256]{1,0:T(8,128)(2,1)S(1)}, bf16[96,256]{1,0:T(8,128)(2,1)S(1)}, u32[]{:S(2)}, u32[]{:S(2)}) collective-permute-start(bf16[96,256]{1,0:T(8,128)(2,1)S(1)} %get-tuple-element.73), channel_id=1, source_target_pairs={{0,6},{1,7},{2,4},{3,5},{4,2},{5,3},{6,0},{7,1},{8,14},{9,15},{10,... | collective-permute-start | bytes 147464 | tf_op jit(solution)/shard_map/ppermute | solution.py:22
  47.1 1.4 %collective-permute-start.21 = (bf16[96,256]{1,0:T(8,128)(2,1)S(1)}, bf16[96,256]{1,0:T(8,128)(2,1)S(1)}, u32[]{:S(2)}, u32[]{:S(2)}) collective-permute-start(bf16[96,256]{1,0:T(8,128)(2,1)S(1)} %get-tuple-element.73), channel_id=1, source_target_pairs={{0,2},{1,3},{2,0},{3,1},{4,6},{5,7},{6,4},{7,5},{8,10},{9,11},{10,... | collective-permute-start | bytes 147464 | tf_op jit(solution)/shard_map/ppermute | solution.py:22
  49.1 2.9 %collective-permute-start.19 = (bf16[176,256]{1,0:T(8,128)(2,1)S(1)}, bf16[176,256]{1,0:T(8,128)(2,1)S(1)}, u32[]{:S(2)}, u32[]{:S(2)}) collective-permute-start(bf16[176,256]{1,0:T(8,128)(2,1)S(1)} %get-tuple-element.71), channel_id=1, source_target_pairs={{0,4},{1,5},{2,6},{3,7},{4,0},{5,1},{6,2},{7,3},{8,12},{9,13},{10,... | collective-permute-start | bytes 270344 | tf_op jit(solution)/shard_map/ppermute | solution.py:22
  52.1 1.5 %collective-permute-start.20 = (bf16[176,256]{1,0:T(8,128)(2,1)S(1)}, bf16[176,256]{1,0:T(8,128)(2,1)S(1)}, u32[]{:S(2)}, u32[]{:S(2)}) collective-permute-start(bf16[176,256]{1,0:T(8,128)(2,1)S(1)} %get-tuple-element.72), channel_id=1, source_target_pairs={{0,6},{1,7},{2,4},{3,5},{4,2},{5,3},{6,0},{7,1},{8,14},{9,15},{10,... | collective-permute-start | bytes 270344 | tf_op jit(solution)/shard_map/ppermute | solution.py:22
  53.8 0.9 %collective-permute-start.26 = (bf16[96,256]{1,0:T(8,128)(2,1)S(1)}, bf16[96,256]{1,0:T(8,128)(2,1)S(1)}, u32[]{:S(2)}, u32[]{:S(2)}) collective-permute-start(bf16[96,256]{1,0:T(8,128)(2,1)S(1)} %add_convert_fusion.refs_3_), channel_id=1, source_target_pairs={{0,24},{8,16},{16,8},{24,0},{1,25},{9,17},{17,9},{25,1},{2,26},{10... | collective-permute-start | bytes 147464 | tf_op jit(solution)/shard_map/ppermute | solution.py:22
  54.7 1.5 %collective-permute-start.25 = (bf16[96,256]{1,0:T(8,128)(2,1)S(1)}, bf16[96,256]{1,0:T(8,128)(2,1)S(1)}, u32[]{:S(2)}, u32[]{:S(2)}) collective-permute-start(bf16[96,256]{1,0:T(8,128)(2,1)S(1)} %add_convert_fusion.refs_3_), channel_id=1, source_target_pairs={{0,16},{8,24},{16,0},{24,8},{1,17},{9,25},{17,1},{25,9},{2,18},{10... | collective-permute-start | bytes 147464 | tf_op jit(solution)/shard_map/ppermute | solution.py:22
  56.2 1.1 %collective-permute-start.24 = (bf16[96,256]{1,0:T(8,128)(2,1)S(1)}, bf16[96,256]{1,0:T(8,128)(2,1)S(1)}, u32[]{:S(2)}, u32[]{:S(2)}) collective-permute-start(bf16[96,256]{1,0:T(8,128)(2,1)S(1)} %add_convert_fusion.refs_3_), channel_id=1, source_target_pairs={{0,8},{8,0},{16,24},{24,16},{1,9},{9,1},{17,25},{25,17},{2,10},{10... | collective-permute-start | bytes 147464 | tf_op jit(solution)/shard_map/ppermute | solution.py:22
  57.4 1.6 %collective-permute-done.19.refs_1_ = bf16[176,256]{1,0:T(8,128)(2,1)S(1)} collective-permute-done((bf16[176,256]{1,0:T(8,128)(2,1)S(1)}, bf16[176,256]{1,0:T(8,128)(2,1)S(1)}, u32[]{:S(2)}, u32[]{:S(2)}) %collective-permute-start.19) | collective-permute-done | bytes 90144 | tf_op jit(solution)/shard_map/ppermute | solution.py:22
  59.3 1.0 %collective-permute-done.24.refs_4_ = bf16[96,256]{1,0:T(8,128)(2,1)S(1)} collective-permute-done((bf16[96,256]{1,0:T(8,128)(2,1)S(1)}, bf16[96,256]{1,0:T(8,128)(2,1)S(1)}, u32[]{:S(2)}, u32[]{:S(2)}) %collective-permute-start.24) | collective-permute-done | bytes 49184 | tf_op jit(solution)/shard_map/ppermute | solution.py:22
  60.3 1.0 %results.1 = (bf16[172,256]{1,0:T(8,128)(2,1)}, f32[128,256]{1,0:T(8,128)}, f32[1,256]{1,0:T(1,128)}, f32[172,256]{1,0:T(8,128)}, f32[1,172]{1,0:T(1,128)}) custom-call(f32[176,256]{1,0:T(8,128)S(1)} %get-tuple-element.69.total_ref, f32[16,128]{1,0:T(8,128)S(1)} %get-tuple-element.54.degree_ref, f32[1,172]{1,0:T(1,128)S(1)} %bitcast.12, ...), custom_call_target="tpu_custom_call" | custom-call | tf_op jit(solution)/shard_map/results/pallas_call | solution.py:28
  (44 shorter events, 5.7 us)
Async XLA Ops:
  0.6 11.7 %collective-permute-start.1 = (bf16[172,256]{1,0:T(8,128)(2,1)}, bf16[172,256]{1,0:T(8,128)(2,1)S(1)}, u32[]{:S(2)}, u32[]{:S(2)}) collective-permute-start(bf16[172,256]{1,0:T(8,128)(2,1)} %bitcast.13), channel_id=1, source_target_pairs={{0,4},{1,5},{2,6},{3,7},{4,0},{5,1},{6,2},{7,3},{8,12},{9,13},{10,... | collective-permute-start | bytes 264200 | tf_op jit(solution)/shard_map/ppermute | solution.py:22
  4.7 4.5 %collective-permute-start = (bf16[256,128]{1,0:T(8,128)(2,1)}, bf16[256,128]{1,0:T(8,128)(2,1)S(1)}, u32[]{:S(2)}, u32[]{:S(2)}) collective-permute-start(bf16[256,128]{1,0:T(8,128)(2,1)} %features_hbm.1), channel_id=1, source_target_pairs={{0,8},{8,0},{16,24},{24,16},{1,9},{9,1},{17,25},{25,17},{2,10},{10... | collective-permute-start | bytes 196616 | tf_op jit(solution)/shard_map/ppermute | solution.py:22
  6.2 6.0 %collective-permute-start.3 = (bf16[256,128]{1,0:T(8,128)(2,1)}, bf16[256,128]{1,0:T(8,128)(2,1)S(1)}, u32[]{:S(2)}, u32[]{:S(2)}) collective-permute-start(bf16[256,128]{1,0:T(8,128)(2,1)} %features_hbm.1), channel_id=1, source_target_pairs={{0,24},{8,16},{16,8},{24,0},{1,25},{9,17},{17,9},{25,1},{2,26},{10... | collective-permute-start | bytes 196616 | tf_op jit(solution)/shard_map/ppermute | solution.py:22
  7.7 4.6 %collective-permute-start.2 = (bf16[256,128]{1,0:T(8,128)(2,1)}, bf16[256,128]{1,0:T(8,128)(2,1)S(1)}, u32[]{:S(2)}, u32[]{:S(2)}) collective-permute-start(bf16[256,128]{1,0:T(8,128)(2,1)} %features_hbm.1), channel_id=1, source_target_pairs={{0,16},{8,24},{16,0},{24,8},{1,17},{9,25},{17,1},{25,9},{2,18},{10... | collective-permute-start | bytes 196616 | tf_op jit(solution)/shard_map/ppermute | solution.py:22
  9.2 0.6 %copy-start.4 = (bf16[256,128]{1,0:T(8,128)(2,1)}, bf16[256,128]{1,0:T(8,128)(2,1)S(1)}, u32[]{:S(2)}) copy-start(bf16[256,128]{1,0:T(8,128)(2,1)S(1)} %collective-permute-done.next_hbm) | copy-start | bytes 196612
  13.6 18.1 %copy-start = (bf16[256,172]{0,1:T(8,128)(2,1)S(1)}, bf16[256,172]{0,1:T(8,128)(2,1)}, u32[]{:S(2)}) copy-start(bf16[256,172]{0,1:T(8,128)(2,1)} %param.17) | copy-start | bytes 264196
  13.6 18.1 %copy-start.1 = (bf16[128,256]{1,0:T(8,128)(2,1)S(1)}, bf16[128,256]{1,0:T(8,128)(2,1)}, u32[]{:S(2)}) copy-start(bf16[128,256]{1,0:T(8,128)(2,1)} %refs_2_.1) | copy-start | bytes 196612
  13.7 18.1 %copy-start.2 = (f32[256]{0:T(256)S(1)}, f32[256]{0:T(256)}, u32[]{:S(2)}) copy-start(f32[256]{0:T(256)} %param.16) | copy-start | bytes 3076
  13.7 1.7 %collective-permute-start.4 = (bf16[1056,128]{1,0:T(8,128)(2,1)S(1)}, bf16[1056,128]{1,0:T(8,128)(2,1)S(1)}, u32[]{:S(2)}, u32[]{:S(2)}) collective-permute-start(bf16[1056,128]{1,0:T(8,128)(2,1)S(1)} %get-tuple-element.46), channel_id=1, source_target_pairs={{0,1},{1,0},{2,3},{3,2},{4,5},{5,4},{6,7},{7,6},{8,9},{9,8},{10,11... | collective-permute-start | bytes 811016 | tf_op jit(solution)/shard_map/ppermute | solution.py:22
  13.8 8.5 %collective-permute-start.5 = (bf16[2,172,256]{2,1,0:T(8,128)(2,1)S(1)}, bf16[2,172,256]{2,1,0:T(8,128)(2,1)S(1)}, u32[]{:S(2)}, u32[]{:S(2)}) collective-permute-start(bf16[2,172,256]{2,1,0:T(8,128)(2,1)S(1)} %get-tuple-element.50.left_ref), channel_id=1, source_target_pairs={{0,2},{1,3},{2,0},{3,1},{4,6},{5,7},{6,4},{7,5},{8,10},{9,11},{10,... | collective-permute-start | bytes 528392 | tf_op jit(solution)/shard_map/ppermute | solution.py:22
  15.4 8.1 %collective-permute-start.6 = (bf16[288,128]{1,0:T(8,128)(2,1)S(1)}, bf16[288,128]{1,0:T(8,128)(2,1)S(1)}, u32[]{:S(2)}, u32[]{:S(2)}) collective-permute-start(bf16[288,128]{1,0:T(8,128)(2,1)S(1)} %get-tuple-element.51), channel_id=1, source_target_pairs={{0,2},{1,3},{2,0},{3,1},{4,6},{5,7},{6,4},{7,5},{8,10},{9,11},{10,... | collective-permute-start | bytes 221192 | tf_op jit(solution)/shard_map/ppermute | solution.py:22
  17.0 8.9 %collective-permute-start.7 = (bf16[288,128]{1,0:T(8,128)(2,1)S(1)}, bf16[288,128]{1,0:T(8,128)(2,1)S(1)}, u32[]{:S(2)}, u32[]{:S(2)}) collective-permute-start(bf16[288,128]{1,0:T(8,128)(2,1)S(1)} %get-tuple-element.52), channel_id=1, source_target_pairs={{0,4},{1,5},{2,6},{3,7},{4,0},{5,1},{6,2},{7,3},{8,12},{9,13},{10,... | collective-permute-start | bytes 221192 | tf_op jit(solution)/shard_map/ppermute | solution.py:22
  17.4 8.4 %collective-permute-start.8 = (bf16[288,128]{1,0:T(8,128)(2,1)S(1)}, bf16[288,128]{1,0:T(8,128)(2,1)S(1)}, u32[]{:S(2)}, u32[]{:S(2)}) collective-permute-start(bf16[288,128]{1,0:T(8,128)(2,1)S(1)} %get-tuple-element.53), channel_id=1, source_target_pairs={{0,6},{1,7},{2,4},{3,5},{4,2},{5,3},{6,0},{7,1},{8,14},{9,15},{10,... | collective-permute-start | bytes 221192 | tf_op jit(solution)/shard_map/ppermute | solution.py:22
  26.1 3.7 %collective-permute-start.9 = (bf16[4,172,256]{2,1,0:T(8,128)(2,1)S(1)}, bf16[4,172,256]{2,1,0:T(8,128)(2,1)S(1)}, u32[]{:S(2)}, u32[]{:S(2)}) collective-permute-start(bf16[4,172,256]{2,1,0:T(8,128)(2,1)S(1)} %get-tuple-element.55.near_ref), channel_id=1, source_target_pairs={{0,1},{1,0},{2,3},{3,2},{4,5},{5,4},{6,7},{7,6},{8,9},{9,8},{10,11... | collective-permute-start | bytes 1056776 | tf_op jit(solution)/shard_map/ppermute | solution.py:22
  26.2 5.6 %collective-permute-start.10 = (bf16[256,128]{1,0:T(8,128)(2,1)S(1)}, bf16[256,128]{1,0:T(8,128)(2,1)S(1)}, u32[]{:S(2)}, u32[]{:S(2)}) collective-permute-start(bf16[256,128]{1,0:T(8,128)(2,1)S(1)} %get-tuple-element.56.own_ref), channel_id=1, source_target_pairs={{0,24},{8,16},{16,8},{24,0},{1,25},{9,17},{17,9},{25,1},{2,26},{10... | collective-permute-start | bytes 196616 | tf_op jit(solution)/shard_map/ppermute | solution.py:22
  29.1 4.3 %collective-permute-start.12 = (bf16[256,128]{1,0:T(8,128)(2,1)S(1)}, bf16[256,128]{1,0:T(8,128)(2,1)S(1)}, u32[]{:S(2)}, u32[]{:S(2)}) collective-permute-start(bf16[256,128]{1,0:T(8,128)(2,1)S(1)} %get-tuple-element.56.own_ref), channel_id=1, source_target_pairs={{0,16},{8,24},{16,0},{24,8},{1,17},{9,25},{17,1},{25,9},{2,18},{10... | collective-permute-start | bytes 196616 | tf_op jit(solution)/shard_map/ppermute | solution.py:22
  29.6 4.3 %collective-permute-start.11 = (bf16[256,128]{1,0:T(8,128)(2,1)S(1)}, bf16[256,128]{1,0:T(8,128)(2,1)S(1)}, u32[]{:S(2)}, u32[]{:S(2)}) collective-permute-start(bf16[256,128]{1,0:T(8,128)(2,1)S(1)} %get-tuple-element.56.own_ref), channel_id=1, source_target_pairs={{0,8},{8,0},{16,24},{24,16},{1,9},{9,1},{17,25},{25,17},{2,10},{10... | collective-permute-start | bytes 196616 | tf_op jit(solution)/shard_map/ppermute | solution.py:22
  32.8 27.6 %copy-start.3 = (f32[172]{0:T(256)S(1)}, f32[172]{0:T(256)}, u32[]{:S(2)}) copy-start(f32[172]{0:T(256)} %param.18) | copy-start | bytes 2068
  34.9 5.7 %collective-permute-start.14 = (bf16[96,256]{1,0:T(8,128)(2,1)S(1)}, bf16[96,256]{1,0:T(8,128)(2,1)S(1)}, u32[]{:S(2)}, u32[]{:S(2)}) collective-permute-start(bf16[96,256]{1,0:T(8,128)(2,1)S(1)} %get-tuple-element.66), channel_id=1, source_target_pairs={{0,8},{8,0},{16,24},{24,16},{1,9},{9,1},{17,25},{25,17},{2,10},{10... | collective-permute-start | bytes 147464 | tf_op jit(solution)/shard_map/ppermute | solution.py:22
  36.0 4.6 %collective-permute-start.15 = (bf16[96,256]{1,0:T(8,128)(2,1)S(1)}, bf16[96,256]{1,0:T(8,128)(2,1)S(1)}, u32[]{:S(2)}, u32[]{:S(2)}) collective-permute-start(bf16[96,256]{1,0:T(8,128)(2,1)S(1)} %get-tuple-element.67), channel_id=1, source_target_pairs={{0,16},{8,24},{16,0},{24,8},{1,17},{9,25},{17,1},{25,9},{2,18},{10... | collective-permute-start | bytes 147464 | tf_op jit(solution)/shard_map/ppermute | solution.py:22
  37.6 5.0 %collective-permute-start.16 = (bf16[96,256]{1,0:T(8,128)(2,1)S(1)}, bf16[96,256]{1,0:T(8,128)(2,1)S(1)}, u32[]{:S(2)}, u32[]{:S(2)}) collective-permute-start(bf16[96,256]{1,0:T(8,128)(2,1)S(1)} %get-tuple-element.68), channel_id=1, source_target_pairs={{0,24},{8,16},{16,8},{24,0},{1,25},{9,17},{17,9},{25,1},{2,26},{10... | collective-permute-start | bytes 147464 | tf_op jit(solution)/shard_map/ppermute | solution.py:22
  40.5 3.5 %collective-permute-start.13 = (bf16[4,176,256]{2,1,0:T(8,128)(2,1)S(1)}, bf16[4,176,256]{2,1,0:T(8,128)(2,1)S(1)}, u32[]{:S(2)}, u32[]{:S(2)}) collective-permute-start(bf16[4,176,256]{2,1,0:T(8,128)(2,1)S(1)} %get-tuple-element.65), channel_id=1, source_target_pairs={{0,1},{1,0},{2,3},{3,2},{4,5},{5,4},{6,7},{7,6},{8,9},{9,8},{10,11... | collective-permute-start | bytes 1081352 | tf_op jit(solution)/shard_map/ppermute | solution.py:22
  42.6 1.4 %collective-permute-start.17 = (f32[96,256]{1,0:T(8,128)S(1)}, f32[96,256]{1,0:T(8,128)S(1)}, u32[]{:S(2)}, u32[]{:S(2)}) collective-permute-start(f32[96,256]{1,0:T(8,128)S(1)} %convert_add_fusion.mine_ref), channel_id=1, source_target_pairs={{0,1},{1,0},{2,3},{3,2},{4,5},{5,4},{6,7},{7,6},{8,9},{9,8},{10,11... | collective-permute-start | bytes 294920 | tf_op jit(solution)/shard_map/ppermute | solution.py:22
  44.1 8.0 %collective-permute-start.23 = (bf16[96,256]{1,0:T(8,128)(2,1)S(1)}, bf16[96,256]{1,0:T(8,128)(2,1)S(1)}, u32[]{:S(2)}, u32[]{:S(2)}) collective-permute-start(bf16[96,256]{1,0:T(8,128)(2,1)S(1)} %get-tuple-element.73), channel_id=1, source_target_pairs={{0,6},{1,7},{2,4},{3,5},{4,2},{5,3},{6,0},{7,1},{8,14},{9,15},{10,... | collective-permute-start | bytes 147464 | tf_op jit(solution)/shard_map/ppermute | solution.py:22
  47.1 6.5 %collective-permute-start.22 = (bf16[96,256]{1,0:T(8,128)(2,1)S(1)}, bf16[96,256]{1,0:T(8,128)(2,1)S(1)}, u32[]{:S(2)}, u32[]{:S(2)}) collective-permute-start(bf16[96,256]{1,0:T(8,128)(2,1)S(1)} %get-tuple-element.73), channel_id=1, source_target_pairs={{0,4},{1,5},{2,6},{3,7},{4,0},{5,1},{6,2},{7,3},{8,12},{9,13},{10,... | collective-permute-start | bytes 147464 | tf_op jit(solution)/shard_map/ppermute | solution.py:22
  47.1 6.7 %collective-permute-start.21 = (bf16[96,256]{1,0:T(8,128)(2,1)S(1)}, bf16[96,256]{1,0:T(8,128)(2,1)S(1)}, u32[]{:S(2)}, u32[]{:S(2)}) collective-permute-start(bf16[96,256]{1,0:T(8,128)(2,1)S(1)} %get-tuple-element.73), channel_id=1, source_target_pairs={{0,2},{1,3},{2,0},{3,1},{4,6},{5,7},{6,4},{7,5},{8,10},{9,11},{10,... | collective-permute-start | bytes 147464 | tf_op jit(solution)/shard_map/ppermute | solution.py:22
  48.5 7.7 %collective-permute-start.18 = (bf16[176,256]{1,0:T(8,128)(2,1)S(1)}, bf16[176,256]{1,0:T(8,128)(2,1)S(1)}, u32[]{:S(2)}, u32[]{:S(2)}) collective-permute-start(bf16[176,256]{1,0:T(8,128)(2,1)S(1)} %get-tuple-element.70), channel_id=1, source_target_pairs={{0,2},{1,3},{2,0},{3,1},{4,6},{5,7},{6,4},{7,5},{8,10},{9,11},{10,... | collective-permute-start | bytes 270344 | tf_op jit(solution)/shard_map/ppermute | solution.py:22
  49.1 9.8 %collective-permute-start.19 = (bf16[176,256]{1,0:T(8,128)(2,1)S(1)}, bf16[176,256]{1,0:T(8,128)(2,1)S(1)}, u32[]{:S(2)}, u32[]{:S(2)}) collective-permute-start(bf16[176,256]{1,0:T(8,128)(2,1)S(1)} %get-tuple-element.71), channel_id=1, source_target_pairs={{0,4},{1,5},{2,6},{3,7},{4,0},{5,1},{6,2},{7,3},{8,12},{9,13},{10,... | collective-permute-start | bytes 270344 | tf_op jit(solution)/shard_map/ppermute | solution.py:22
  52.1 6.9 %collective-permute-start.20 = (bf16[176,256]{1,0:T(8,128)(2,1)S(1)}, bf16[176,256]{1,0:T(8,128)(2,1)S(1)}, u32[]{:S(2)}, u32[]{:S(2)}) collective-permute-start(bf16[176,256]{1,0:T(8,128)(2,1)S(1)} %get-tuple-element.72), channel_id=1, source_target_pairs={{0,6},{1,7},{2,4},{3,5},{4,2},{5,3},{6,0},{7,1},{8,14},{9,15},{10,... | collective-permute-start | bytes 270344 | tf_op jit(solution)/shard_map/ppermute | solution.py:22
  53.8 5.2 %collective-permute-start.26 = (bf16[96,256]{1,0:T(8,128)(2,1)S(1)}, bf16[96,256]{1,0:T(8,128)(2,1)S(1)}, u32[]{:S(2)}, u32[]{:S(2)}) collective-permute-start(bf16[96,256]{1,0:T(8,128)(2,1)S(1)} %add_convert_fusion.refs_3_), channel_id=1, source_target_pairs={{0,24},{8,16},{16,8},{24,0},{1,25},{9,17},{17,9},{25,1},{2,26},{10... | collective-permute-start | bytes 147464 | tf_op jit(solution)/shard_map/ppermute | solution.py:22
  54.7 4.6 %collective-permute-start.25 = (bf16[96,256]{1,0:T(8,128)(2,1)S(1)}, bf16[96,256]{1,0:T(8,128)(2,1)S(1)}, u32[]{:S(2)}, u32[]{:S(2)}) collective-permute-start(bf16[96,256]{1,0:T(8,128)(2,1)S(1)} %add_convert_fusion.refs_3_), channel_id=1, source_target_pairs={{0,16},{8,24},{16,0},{24,8},{1,17},{9,25},{17,1},{25,9},{2,18},{10... | collective-permute-start | bytes 147464 | tf_op jit(solution)/shard_map/ppermute | solution.py:22
  56.2 4.1 %collective-permute-start.24 = (bf16[96,256]{1,0:T(8,128)(2,1)S(1)}, bf16[96,256]{1,0:T(8,128)(2,1)S(1)}, u32[]{:S(2)}, u32[]{:S(2)}) collective-permute-start(bf16[96,256]{1,0:T(8,128)(2,1)S(1)} %add_convert_fusion.refs_3_), channel_id=1, source_target_pairs={{0,8},{8,0},{16,24},{24,16},{1,9},{9,1},{17,25},{25,17},{2,10},{10... | collective-permute-start | bytes 147464 | tf_op jit(solution)/shard_map/ppermute | solution.py:22

commit v7 on v6

--- a/solution.py
+++ b/solution.py
@@ -49,7 +49,7 @@
     return high, (value - high.astype(F32)).astype(BF16)
 
 
-def dense_kernel(own, row_hbm, col_hbm, live_hbm, tiles_hbm, features_hbm, g_hbm, next_hbm, *refs):
+def dense_kernel(own, row_hbm, col_hbm, live_hbm, tiles_hbm, features_hbm, g_hbm, *refs):
     dense_ref, held_ref, g_ref, row_ref, col_ref, live_ref, tiles_ref, done = refs
     pairs = (
         (row_hbm, row_ref),
@@ -57,7 +57,6 @@
         (live_hbm, live_ref),
         (tiles_hbm, tiles_ref),
         (features_hbm, held_ref.at[0]),
-        (next_hbm, held_ref.at[1]),
         (g_hbm, g_ref),
     )
     copies = [pltpu.make_async_copy(a, b, done.at[n]) for n, (a, b) in enumerate(pairs)]
@@ -88,14 +87,14 @@
 
 
 def first_kernel(spans, dense_ref, g_ref, far_ref, pair_in_ref, *refs):
-    pieces, (send_ref, keep_ref, degree_ref, pair_ref, held) = refs[: spans - 2], refs[spans - 2 :]
+    pieces, (send_ref, keep_ref, degree_ref, pair_ref, held) = refs[: spans - 1], refs[spans - 1 :]
     pair_ref[0] = g_ref[...]
     pair_ref[1] = far_ref[...]
     nodes = g_ref.shape[1]
     fin = pair_in_ref.shape[2]
     block = LANES
     for s in range(spans):
-        held[pl.ds(s * nodes, nodes), :fin] = pair_in_ref[s] if s < 2 else pieces[s - 2][...]
+        held[pl.ds(s * nodes, nodes), :fin] = pair_in_ref[0] if s == 0 else pieces[s - 1][...]
     held[:, fin:] = jnp.ones((held.shape[0], block), BF16)
     half = keep_ref.shape[0] // nodes
     blocks = degree_ref.shape[0]
@@ -347,17 +346,17 @@
         "dense_adjacency",
         [
             keep_in((rows, columns), BF16),
-            keep_in((2, nodes, fin), BF16),
+            keep_in((1, nodes, fin), BF16),
             keep_in(g_own.shape, BF16),
         ],
-        [HBM] * 7,
-        [tile_row, tile_col, tile_live, tiles, features, g_own, inputs[1]],
+        [HBM] * 6,
+        [tile_row, tile_col, tile_live, tiles, features, g_own],
         scratch=[
             pltpu.SMEM(tile_row.shape, jnp.int32),
             pltpu.SMEM(tile_col.shape, jnp.int32),
             pltpu.SMEM(tile_live.shape, jnp.int32),
             pltpu.VMEM(tiles.shape, BF16),
-            pltpu.SemaphoreType.DMA((7,)),
+            pltpu.SemaphoreType.DMA((6,)),
         ],
         grant=GRANT if whole else 60 << 20,
     )
@@ -370,8 +369,8 @@
             shaped((blocks, block), F32),
             shaped((2, classes, nodes), BF16),
         ],
-        [VMEM] * (2 + row_count),
-        [dense, own_g, far_g, held] + inputs[2:],
+        [VMEM] * (3 + row_count),
+        [dense, own_g, far_g, held] + inputs[1:],
         scratch=[pltpu.VMEM((columns, fin + LANES), BF16)],
     )
     other = exchange(send, "col", 1)

time: 61.1 us -> 60.2 us (0.985)
  Pallas kernels: 10.1 us -> 9.43 us
  local copies, waits for them, and re-layouts: 0.65 us -> 0.03 us
    pallas_call x10, Pallas kernels: 10.1 us -> 9.43 us  [call(): pl.pallas_call(kernel, out_shape=tuple(outs), in_specs=in_specs, out_spec...]
    unnamed x10 -> x8, local copies, waits for them, and re-layouts: 0.65 us -> 0.03 us
  transfers between devices with their start and end apart: 27 -> 27, of which waited for: 14 -> 15; matrix products, arithmetic and copies ran while one was open for 0% -> 0% of each run, Pallas kernels for 10% -> 10%
where the time goes in v7:
time: 60.2 us; the launch traced here: 60 us
  starting transfers between devices  34.1 us (57%)
  waiting for transfers between devices  14.9 us (25%)
  Pallas kernels  9.43 us (16%)
  between operations  1.46 us (2%)
    ppermute x27, starting transfers between devices, exchange(): return lax.ppermute(value, axis, [(i, i ^ mask) for i in range(count)])  34.1 us
    ppermute x27, waiting for transfers between devices, exchange(): return lax.ppermute(value, axis, [(i, i ^ mask) for i in range(count)])  14.9 us
    pallas_call x10, Pallas kernels, call(): pl.pallas_call(kernel, out_shape=tuple(outs), in_specs=in_specs, out_spec...  9.43 us
  transfers between devices with their start and end apart: 27, of which 15 were waited for; matrix products, arithmetic and copies ran while one was open for 0% of the time, Pallas kernels for 10%

profile of v7, /device:TPU:0, one launch (start us, length us, event | category | flops | bytes accessed | tf_op | source)
XLA Modules:
  0.0 60.0 jit_solution(18235544665196979202)
XLA Ops:
  0.6 4.1 %collective-permute-start = (bf16[172,256]{1,0:T(8,128)(2,1)}, bf16[172,256]{1,0:T(8,128)(2,1)S(1)}, u32[]{:S(2)}, u32[]{:S(2)}) collective-permute-start(bf16[172,256]{1,0:T(8,128)(2,1)} %bitcast.13), channel_id=1, source_target_pairs={{0,4},{1,5},{2,6},{3,7},{4,0},{5,1},{6,2},{7,3},{8,12},{9,13},{10,... | collective-permute-start | bytes 264200 | tf_op jit(solution)/shard_map/ppermute | solution.py:22
  4.7 1.5 %collective-permute-start.1 = (bf16[256,128]{1,0:T(8,128)(2,1)}, bf16[256,128]{1,0:T(8,128)(2,1)S(1)}, u32[]{:S(2)}, u32[]{:S(2)}) collective-permute-start(bf16[256,128]{1,0:T(8,128)(2,1)} %features_hbm.1), channel_id=1, source_target_pairs={{0,8},{8,0},{16,24},{24,16},{1,9},{9,1},{17,25},{25,17},{2,10},{10... | collective-permute-start | bytes 196616 | tf_op jit(solution)/shard_map/ppermute | solution.py:22
  6.2 1.5 %collective-permute-start.3 = (bf16[256,128]{1,0:T(8,128)(2,1)}, bf16[256,128]{1,0:T(8,128)(2,1)S(1)}, u32[]{:S(2)}, u32[]{:S(2)}) collective-permute-start(bf16[256,128]{1,0:T(8,128)(2,1)} %features_hbm.1), channel_id=1, source_target_pairs={{0,24},{8,16},{16,8},{24,0},{1,25},{9,17},{17,9},{25,1},{2,26},{10... | collective-permute-start | bytes 196616 | tf_op jit(solution)/shard_map/ppermute | solution.py:22
  8.9 1.8 %dense_adjacency.1 = (bf16[2048,1024]{1,0:T(8,128)(2,1)S(1)}, bf16[1,256,128]{2,1,0:T(8,128)(2,1)S(1)}, bf16[172,256]{1,0:T(8,128)(2,1)S(1)}) custom-call(s32[1,1,48]{2,1,0:T(1,128)} %row_hbm.1, s32[1,1,48]{2,1,0:T(1,128)} %col_hbm.1, s32[1,1]{1,0:T(1,128)S(6)} %copy.15.live_hbm, bf16[1,1,48,128,128]{4,3,2,1,0:T(8,128)(2,1)} %tiles_hbm.1, ...), custom_call_target="tpu_custom_call" | custom-call | tf_op jit(solution)/shard_map/dense_adjacency/pallas_call | solution.py:28
  10.7 1.0 %collective-permute-done.3.refs_2_ = bf16[256,128]{1,0:T(8,128)(2,1)S(1)} collective-permute-done((bf16[256,128]{1,0:T(8,128)(2,1)}, bf16[256,128]{1,0:T(8,128)(2,1)S(1)}, u32[]{:S(2)}, u32[]{:S(2)}) %collective-permute-start.3) | collective-permute-done | bytes 65568 | tf_op jit(solution)/shard_map/ppermute | solution.py:22
  12.3 1.3 %first_product.1 = (bf16[1056,128]{1,0:T(8,128)(2,1)S(1)}, f32[1024,128]{1,0:T(8,128)S(1)}, f32[16,128]{1,0:T(8,128)S(1)}, bf16[2,172,256]{2,1,0:T(8,128)(2,1)S(1)}) custom-call(bf16[2048,1024]{1,0:T(8,128)(2,1)S(1)} %get-tuple-element.42.dense_ref, bf16[172,256]{1,0:T(8,128)(2,1)S(1)} %get-tuple-element.43.g_ref, ...), custom_call_target="tpu_custom_call" | custom-call | tf_op jit(solution)/shard_map/first_product/pallas_call | solution.py:28
  13.8 1.6 %collective-permute-start.5 = (bf16[2,172,256]{2,1,0:T(8,128)(2,1)S(1)}, bf16[2,172,256]{2,1,0:T(8,128)(2,1)S(1)}, u32[]{:S(2)}, u32[]{:S(2)}) collective-permute-start(bf16[2,172,256]{2,1,0:T(8,128)(2,1)S(1)} %get-tuple-element.50.left_ref), channel_id=1, source_target_pairs={{0,2},{1,3},{2,0},{3,1},{4,6},{5,7},{6,4},{7,5},{8,10},{9,11},{10,... | collective-permute-start | bytes 528392 | tf_op jit(solution)/shard_map/ppermute | solution.py:22
  15.4 1.5 %collective-permute-start.6 = (bf16[288,128]{1,0:T(8,128)(2,1)S(1)}, bf16[288,128]{1,0:T(8,128)(2,1)S(1)}, u32[]{:S(2)}, u32[]{:S(2)}) collective-permute-start(bf16[288,128]{1,0:T(8,128)(2,1)S(1)} %get-tuple-element.51), channel_id=1, source_target_pairs={{0,2},{1,3},{2,0},{3,1},{4,6},{5,7},{6,4},{7,5},{8,10},{9,11},{10,... | collective-permute-start | bytes 221192 | tf_op jit(solution)/shard_map/ppermute | solution.py:22
  17.3 2.6 %collective-permute-start.8 = (bf16[288,128]{1,0:T(8,128)(2,1)S(1)}, bf16[288,128]{1,0:T(8,128)(2,1)S(1)}, u32[]{:S(2)}, u32[]{:S(2)}) collective-permute-start(bf16[288,128]{1,0:T(8,128)(2,1)S(1)} %get-tuple-element.53), channel_id=1, source_target_pairs={{0,6},{1,7},{2,4},{3,5},{4,2},{5,3},{6,0},{7,1},{8,14},{9,15},{10,... | collective-permute-start | bytes 221192 | tf_op jit(solution)/shard_map/ppermute | solution.py:22
  19.9 2.3 %collective-permute-done.5.right_ref = bf16[2,172,256]{2,1,0:T(8,128)(2,1)S(1)} collective-permute-done((bf16[2,172,256]{2,1,0:T(8,128)(2,1)S(1)}, bf16[2,172,256]{2,1,0:T(8,128)(2,1)S(1)}, u32[]{:S(2)}, u32[]{:S(2)}) %collective-permute-start.5) | collective-permute-done | bytes 176160 | tf_op jit(solution)/shard_map/ppermute | solution.py:22
  22.2 1.4 %collective-permute-done.6.refs_0_ = bf16[288,128]{1,0:T(8,128)(2,1)S(1)} collective-permute-done((bf16[288,128]{1,0:T(8,128)(2,1)S(1)}, bf16[288,128]{1,0:T(8,128)(2,1)S(1)}, u32[]{:S(2)}, u32[]{:S(2)}) %collective-permute-start.6) | collective-permute-done | bytes 73760 | tf_op jit(solution)/shard_map/ppermute | solution.py:22
  23.6 2.3 %collective-permute-done.7.refs_1_ = bf16[288,128]{1,0:T(8,128)(2,1)S(1)} collective-permute-done((bf16[288,128]{1,0:T(8,128)(2,1)S(1)}, bf16[288,128]{1,0:T(8,128)(2,1)S(1)}, u32[]{:S(2)}, u32[]{:S(2)}) %collective-permute-start.7) | collective-permute-done | bytes 73760 | tf_op jit(solution)/shard_map/ppermute | solution.py:22
  26.2 1.6 %collective-permute-start.10 = (bf16[256,128]{1,0:T(8,128)(2,1)S(1)}, bf16[256,128]{1,0:T(8,128)(2,1)S(1)}, u32[]{:S(2)}, u32[]{:S(2)}) collective-permute-start(bf16[256,128]{1,0:T(8,128)(2,1)S(1)} %get-tuple-element.56.own_ref), channel_id=1, source_target_pairs={{0,24},{8,16},{16,8},{24,0},{1,25},{9,17},{17,9},{25,1},{2,26},{10... | collective-permute-start | bytes 196616 | tf_op jit(solution)/shard_map/ppermute | solution.py:22
  27.7 1.4 %collective-permute-start.12 = (bf16[256,128]{1,0:T(8,128)(2,1)S(1)}, bf16[256,128]{1,0:T(8,128)(2,1)S(1)}, u32[]{:S(2)}, u32[]{:S(2)}) collective-permute-start(bf16[256,128]{1,0:T(8,128)(2,1)S(1)} %get-tuple-element.56.own_ref), channel_id=1, source_target_pairs={{0,16},{8,24},{16,0},{24,8},{1,17},{9,25},{17,1},{25,9},{2,18},{10... | collective-permute-start | bytes 196616 | tf_op jit(solution)/shard_map/ppermute | solution.py:22
  29.7 0.9 %back_product.1.back_ref = f32[4,176,256]{2,1,0:T(8,128)S(1)} custom-call(bf16[2048,1024]{1,0:T(8,128)(2,1)S(1)} %get-tuple-element.42.dense_ref, f32[16,128]{1,0:T(8,128)S(1)} %get-tuple-element.54.degree_ref, bf16[4,172,256]{2,1,0:T(8,128)(2,1)S(1)} %get-tuple-element.55.near_ref, bf16[4,172,256]{2,1,0:T(8,128)(2,1)S(1)} %collective-permute-done.9.other_ref), custom_call_target="tpu_custom_call" | custom-call | tf_op jit(solution)/shard_map/back_product/pallas_call | solution.py:28
  30.7 1.0 %collective-permute-done.10.last_ref = bf16[256,128]{1,0:T(8,128)(2,1)S(1)} collective-permute-done((bf16[256,128]{1,0:T(8,128)(2,1)S(1)}, bf16[256,128]{1,0:T(8,128)(2,1)S(1)}, u32[]{:S(2)}, u32[]{:S(2)}) %collective-permute-start.10) | collective-permute-done | bytes 65568 | tf_op jit(solution)/shard_map/ppermute | solution.py:22
  31.7 1.0 %gradients_early.1 = (f32[128,256]{1,0:T(8,128)S(1)}, f32[176,256]{1,0:T(8,128)S(1)}, f32[1,256]{1,0:T(1,128)S(1)}, bf16[176,512]{1,0:T(8,128)(2,1)S(1)}, f32[176,256]{1,0:T(8,128)S(1)}) custom-call(f32[4,176,256]{2,1,0:T(8,128)S(1)} %back_product.1.back_ref, bf16[256,128]{1,0:T(8,128)(2,1)S(1)} %get-tuple-element.56.own_ref, ...), custom_call_target="tpu_custom_call" | custom-call | tf_op jit(solution)/shard_map/gradients_early/pallas_call | solution.py:28
  33.4 1.0 %gradients.1 = (f32[96,256]{1,0:T(8,128)S(1)}, bf16[176,512]{1,0:T(8,128)(2,1)S(1)}, bf16[96,256]{1,0:T(8,128)(2,1)S(1)}, bf16[96,256]{1,0:T(8,128)(2,1)S(1)}, bf16[96,256]{1,0:T(8,128)(2,1)S(1)}) custom-call(f32[4,176,256]{2,1,0:T(8,128)S(1)} %back_product.1.back_ref, bf16[172,256]{1,0:T(8,128)(2,1)S(1)} %get-tuple-element.43.g_ref, ...), custom_call_target="tpu_custom_call" | custom-call | tf_op jit(solution)/shard_map/gradients/pallas_call | solution.py:28
  34.4 1.1 %collective-permute-start.14 = (bf16[96,256]{1,0:T(8,128)(2,1)S(1)}, bf16[96,256]{1,0:T(8,128)(2,1)S(1)}, u32[]{:S(2)}, u32[]{:S(2)}) collective-permute-start(bf16[96,256]{1,0:T(8,128)(2,1)S(1)} %get-tuple-element.66), channel_id=1, source_target_pairs={{0,8},{8,0},{16,24},{24,16},{1,9},{9,1},{17,25},{25,17},{2,10},{10... | collective-permute-start | bytes 147464 | tf_op jit(solution)/shard_map/ppermute | solution.py:22
  36.2 1.8 %collective-permute-start.16 = (bf16[96,256]{1,0:T(8,128)(2,1)S(1)}, bf16[96,256]{1,0:T(8,128)(2,1)S(1)}, u32[]{:S(2)}, u32[]{:S(2)}) collective-permute-start(bf16[96,256]{1,0:T(8,128)(2,1)S(1)} %get-tuple-element.68), channel_id=1, source_target_pairs={{0,24},{8,16},{16,8},{24,0},{1,25},{9,17},{17,9},{25,1},{2,26},{10... | collective-permute-start | bytes 147464 | tf_op jit(solution)/shard_map/ppermute | solution.py:22
  37.9 2.1 %second_product.1 = (bf16[4,176,256]{2,1,0:T(8,128)(2,1)S(1)}, f32[4,176,256]{2,1,0:T(8,128)S(1)}) custom-call(bf16[2048,1024]{1,0:T(8,128)(2,1)S(1)} %get-tuple-element.42.dense_ref, bf16[176,512]{1,0:T(8,128)(2,1)S(1)} %get-tuple-element.57.outer_ref, bf16[176,512]{1,0:T(8,128)(2,1)S(1)} %get-tuple-element.61.inner_ref, ...), custom_call_target="tpu_custom_call" | custom-call | tf_op jit(solution)/shard_map/second_product/pallas_call | solution.py:28
  40.1 1.0 %collective-permute-done.16 = bf16[96,256]{1,0:T(8,128)(2,1)S(1)} collective-permute-done((bf16[96,256]{1,0:T(8,128)(2,1)S(1)}, bf16[96,256]{1,0:T(8,128)(2,1)S(1)}, u32[]{:S(2)}, u32[]{:S(2)}) %collective-permute-start.16) | collective-permute-done | bytes 49184 | tf_op jit(solution)/shard_map/ppermute | solution.py:22
  41.3 1.3 %collective-permute-done.17.far_ref = f32[96,256]{1,0:T(8,128)S(1)} collective-permute-done((f32[96,256]{1,0:T(8,128)S(1)}, f32[96,256]{1,0:T(8,128)S(1)}, u32[]{:S(2)}, u32[]{:S(2)}) %collective-permute-start.17) | collective-permute-done | bytes 98336 | tf_op jit(solution)/shard_map/ppermute | solution.py:22
  42.7 3.0 %collective-permute-start.23 = (bf16[96,256]{1,0:T(8,128)(2,1)S(1)}, bf16[96,256]{1,0:T(8,128)(2,1)S(1)}, u32[]{:S(2)}, u32[]{:S(2)}) collective-permute-start(bf16[96,256]{1,0:T(8,128)(2,1)S(1)} %get-tuple-element.73), channel_id=1, source_target_pairs={{0,6},{1,7},{2,4},{3,5},{4,2},{5,3},{6,0},{7,1},{8,14},{9,15},{10,... | collective-permute-start | bytes 147464 | tf_op jit(solution)/shard_map/ppermute | solution.py:22
  45.7 1.4 %collective-permute-start.21 = (bf16[96,256]{1,0:T(8,128)(2,1)S(1)}, bf16[96,256]{1,0:T(8,128)(2,1)S(1)}, u32[]{:S(2)}, u32[]{:S(2)}) collective-permute-start(bf16[96,256]{1,0:T(8,128)(2,1)S(1)} %get-tuple-element.73), channel_id=1, source_target_pairs={{0,2},{1,3},{2,0},{3,1},{4,6},{5,7},{6,4},{7,5},{8,10},{9,11},{10,... | collective-permute-start | bytes 147464 | tf_op jit(solution)/shard_map/ppermute | solution.py:22
  47.7 2.9 %collective-permute-start.19 = (bf16[176,256]{1,0:T(8,128)(2,1)S(1)}, bf16[176,256]{1,0:T(8,128)(2,1)S(1)}, u32[]{:S(2)}, u32[]{:S(2)}) collective-permute-start(bf16[176,256]{1,0:T(8,128)(2,1)S(1)} %get-tuple-element.71), channel_id=1, source_target_pairs={{0,4},{1,5},{2,6},{3,7},{4,0},{5,1},{6,2},{7,3},{8,12},{9,13},{10,... | collective-permute-start | bytes 270344 | tf_op jit(solution)/shard_map/ppermute | solution.py:22
  50.7 1.5 %collective-permute-start.20 = (bf16[176,256]{1,0:T(8,128)(2,1)S(1)}, bf16[176,256]{1,0:T(8,128)(2,1)S(1)}, u32[]{:S(2)}, u32[]{:S(2)}) collective-permute-start(bf16[176,256]{1,0:T(8,128)(2,1)S(1)} %get-tuple-element.72), channel_id=1, source_target_pairs={{0,6},{1,7},{2,4},{3,5},{4,2},{5,3},{6,0},{7,1},{8,14},{9,15},{10,... | collective-permute-start | bytes 270344 | tf_op jit(solution)/shard_map/ppermute | solution.py:22
  52.4 1.8 %collective-permute-start.26 = (bf16[96,256]{1,0:T(8,128)(2,1)S(1)}, bf16[96,256]{1,0:T(8,128)(2,1)S(1)}, u32[]{:S(2)}, u32[]{:S(2)}) collective-permute-start(bf16[96,256]{1,0:T(8,128)(2,1)S(1)} %add_convert_fusion.refs_3_), channel_id=1, source_target_pairs={{0,24},{8,16},{16,8},{24,0},{1,25},{9,17},{17,9},{25,1},{2,26},{10... | collective-permute-start | bytes 147464 | tf_op jit(solution)/shard_map/ppermute | solution.py:22
  54.2 0.7 %collective-permute-start.25 = (bf16[96,256]{1,0:T(8,128)(2,1)S(1)}, bf16[96,256]{1,0:T(8,128)(2,1)S(1)}, u32[]{:S(2)}, u32[]{:S(2)}) collective-permute-start(bf16[96,256]{1,0:T(8,128)(2,1)S(1)} %add_convert_fusion.refs_3_), channel_id=1, source_target_pairs={{0,16},{8,24},{16,0},{24,8},{1,17},{9,25},{17,1},{25,9},{2,18},{10... | collective-permute-start | bytes 147464 | tf_op jit(solution)/shard_map/ppermute | solution.py:22
  55.0 1.0 %collective-permute-start.24 = (bf16[96,256]{1,0:T(8,128)(2,1)S(1)}, bf16[96,256]{1,0:T(8,128)(2,1)S(1)}, u32[]{:S(2)}, u32[]{:S(2)}) collective-permute-start(bf16[96,256]{1,0:T(8,128)(2,1)S(1)} %add_convert_fusion.refs_3_), channel_id=1, source_target_pairs={{0,8},{8,0},{16,24},{24,16},{1,9},{9,1},{17,25},{25,17},{2,10},{10... | collective-permute-start | bytes 147464 | tf_op jit(solution)/shard_map/ppermute | solution.py:22
  56.0 1.6 %collective-permute-done.19.refs_1_ = bf16[176,256]{1,0:T(8,128)(2,1)S(1)} collective-permute-done((bf16[176,256]{1,0:T(8,128)(2,1)S(1)}, bf16[176,256]{1,0:T(8,128)(2,1)S(1)}, u32[]{:S(2)}, u32[]{:S(2)}) %collective-permute-start.19) | collective-permute-done | bytes 90144 | tf_op jit(solution)/shard_map/ppermute | solution.py:22
  59.0 1.0 %results.1 = (bf16[172,256]{1,0:T(8,128)(2,1)}, f32[128,256]{1,0:T(8,128)}, f32[1,256]{1,0:T(1,128)}, f32[172,256]{1,0:T(8,128)}, f32[1,172]{1,0:T(1,128)}) custom-call(f32[176,256]{1,0:T(8,128)S(1)} %get-tuple-element.69.total_ref, f32[16,128]{1,0:T(8,128)S(1)} %get-tuple-element.54.degree_ref, f32[1,172]{1,0:T(1,128)S(1)} %bitcast.12, ...), custom_call_target="tpu_custom_call" | custom-call | tf_op jit(solution)/shard_map/results/pallas_call | solution.py:28
  (42 shorter events, 6.6 us)
Async XLA Ops:
  0.6 11.7 %collective-permute-start = (bf16[172,256]{1,0:T(8,128)(2,1)}, bf16[172,256]{1,0:T(8,128)(2,1)S(1)}, u32[]{:S(2)}, u32[]{:S(2)}) collective-permute-start(bf16[172,256]{1,0:T(8,128)(2,1)} %bitcast.13), channel_id=1, source_target_pairs={{0,4},{1,5},{2,6},{3,7},{4,0},{5,1},{6,2},{7,3},{8,12},{9,13},{10,... | collective-permute-start | bytes 264200 | tf_op jit(solution)/shard_map/ppermute | solution.py:22
  4.7 5.9 %collective-permute-start.1 = (bf16[256,128]{1,0:T(8,128)(2,1)}, bf16[256,128]{1,0:T(8,128)(2,1)S(1)}, u32[]{:S(2)}, u32[]{:S(2)}) collective-permute-start(bf16[256,128]{1,0:T(8,128)(2,1)} %features_hbm.1), channel_id=1, source_target_pairs={{0,8},{8,0},{16,24},{24,16},{1,9},{9,1},{17,25},{25,17},{2,10},{10... | collective-permute-start | bytes 196616 | tf_op jit(solution)/shard_map/ppermute | solution.py:22
  6.2 5.4 %collective-permute-start.3 = (bf16[256,128]{1,0:T(8,128)(2,1)}, bf16[256,128]{1,0:T(8,128)(2,1)S(1)}, u32[]{:S(2)}, u32[]{:S(2)}) collective-permute-start(bf16[256,128]{1,0:T(8,128)(2,1)} %features_hbm.1), channel_id=1, source_target_pairs={{0,24},{8,16},{16,8},{24,0},{1,25},{9,17},{17,9},{25,1},{2,26},{10... | collective-permute-start | bytes 196616 | tf_op jit(solution)/shard_map/ppermute | solution.py:22
  7.7 4.6 %collective-permute-start.2 = (bf16[256,128]{1,0:T(8,128)(2,1)}, bf16[256,128]{1,0:T(8,128)(2,1)S(1)}, u32[]{:S(2)}, u32[]{:S(2)}) collective-permute-start(bf16[256,128]{1,0:T(8,128)(2,1)} %features_hbm.1), channel_id=1, source_target_pairs={{0,16},{8,24},{16,0},{24,8},{1,17},{9,25},{17,1},{25,9},{2,18},{10... | collective-permute-start | bytes 196616 | tf_op jit(solution)/shard_map/ppermute | solution.py:22
  13.6 18.0 %copy-start = (bf16[256,172]{0,1:T(8,128)(2,1)S(1)}, bf16[256,172]{0,1:T(8,128)(2,1)}, u32[]{:S(2)}) copy-start(bf16[256,172]{0,1:T(8,128)(2,1)} %param.17) | copy-start | bytes 264196
  13.6 18.0 %copy-start.1 = (bf16[128,256]{1,0:T(8,128)(2,1)S(1)}, bf16[128,256]{1,0:T(8,128)(2,1)}, u32[]{:S(2)}) copy-start(bf16[128,256]{1,0:T(8,128)(2,1)} %refs_2_.1) | copy-start | bytes 196612
  13.7 18.0 %copy-start.2 = (f32[256]{0:T(256)S(1)}, f32[256]{0:T(256)}, u32[]{:S(2)}) copy-start(f32[256]{0:T(256)} %param.16) | copy-start | bytes 3076
  13.7 1.7 %collective-permute-start.4 = (bf16[1056,128]{1,0:T(8,128)(2,1)S(1)}, bf16[1056,128]{1,0:T(8,128)(2,1)S(1)}, u32[]{:S(2)}, u32[]{:S(2)}) collective-permute-start(bf16[1056,128]{1,0:T(8,128)(2,1)S(1)} %get-tuple-element.46), channel_id=1, source_target_pairs={{0,1},{1,0},{2,3},{3,2},{4,5},{5,4},{6,7},{7,6},{8,9},{9,8},{10,11... | collective-permute-start | bytes 811016 | tf_op jit(solution)/shard_map/ppermute | solution.py:22
  13.8 8.4 %collective-permute-start.5 = (bf16[2,172,256]{2,1,0:T(8,128)(2,1)S(1)}, bf16[2,172,256]{2,1,0:T(8,128)(2,1)S(1)}, u32[]{:S(2)}, u32[]{:S(2)}) collective-permute-start(bf16[2,172,256]{2,1,0:T(8,128)(2,1)S(1)} %get-tuple-element.50.left_ref), channel_id=1, source_target_pairs={{0,2},{1,3},{2,0},{3,1},{4,6},{5,7},{6,4},{7,5},{8,10},{9,11},{10,... | collective-permute-start | bytes 528392 | tf_op jit(solution)/shard_map/ppermute | solution.py:22
  15.4 8.2 %collective-permute-start.6 = (bf16[288,128]{1,0:T(8,128)(2,1)S(1)}, bf16[288,128]{1,0:T(8,128)(2,1)S(1)}, u32[]{:S(2)}, u32[]{:S(2)}) collective-permute-start(bf16[288,128]{1,0:T(8,128)(2,1)S(1)} %get-tuple-element.51), channel_id=1, source_target_pairs={{0,2},{1,3},{2,0},{3,1},{4,6},{5,7},{6,4},{7,5},{8,10},{9,11},{10,... | collective-permute-start | bytes 221192 | tf_op jit(solution)/shard_map/ppermute | solution.py:22
  17.0 8.9 %collective-permute-start.7 = (bf16[288,128]{1,0:T(8,128)(2,1)S(1)}, bf16[288,128]{1,0:T(8,128)(2,1)S(1)}, u32[]{:S(2)}, u32[]{:S(2)}) collective-permute-start(bf16[288,128]{1,0:T(8,128)(2,1)S(1)} %get-tuple-element.52), channel_id=1, source_target_pairs={{0,4},{1,5},{2,6},{3,7},{4,0},{5,1},{6,2},{7,3},{8,12},{9,13},{10,... | collective-permute-start | bytes 221192 | tf_op jit(solution)/shard_map/ppermute | solution.py:22
  17.3 8.5 %collective-permute-start.8 = (bf16[288,128]{1,0:T(8,128)(2,1)S(1)}, bf16[288,128]{1,0:T(8,128)(2,1)S(1)}, u32[]{:S(2)}, u32[]{:S(2)}) collective-permute-start(bf16[288,128]{1,0:T(8,128)(2,1)S(1)} %get-tuple-element.53), channel_id=1, source_target_pairs={{0,6},{1,7},{2,4},{3,5},{4,2},{5,3},{6,0},{7,1},{8,14},{9,15},{10,... | collective-permute-start | bytes 221192 | tf_op jit(solution)/shard_map/ppermute | solution.py:22
  26.1 3.6 %collective-permute-start.9 = (bf16[4,172,256]{2,1,0:T(8,128)(2,1)S(1)}, bf16[4,172,256]{2,1,0:T(8,128)(2,1)S(1)}, u32[]{:S(2)}, u32[]{:S(2)}) collective-permute-start(bf16[4,172,256]{2,1,0:T(8,128)(2,1)S(1)} %get-tuple-element.55.near_ref), channel_id=1, source_target_pairs={{0,1},{1,0},{2,3},{3,2},{4,5},{5,4},{6,7},{7,6},{8,9},{9,8},{10,11... | collective-permute-start | bytes 1056776 | tf_op jit(solution)/shard_map/ppermute | solution.py:22
  26.2 5.5 %collective-permute-start.10 = (bf16[256,128]{1,0:T(8,128)(2,1)S(1)}, bf16[256,128]{1,0:T(8,128)(2,1)S(1)}, u32[]{:S(2)}, u32[]{:S(2)}) collective-permute-start(bf16[256,128]{1,0:T(8,128)(2,1)S(1)} %get-tuple-element.56.own_ref), channel_id=1, source_target_pairs={{0,24},{8,16},{16,8},{24,0},{1,25},{9,17},{17,9},{25,1},{2,26},{10... | collective-permute-start | bytes 196616 | tf_op jit(solution)/shard_map/ppermute | solution.py:22
  27.7 5.3 %collective-permute-start.12 = (bf16[256,128]{1,0:T(8,128)(2,1)S(1)}, bf16[256,128]{1,0:T(8,128)(2,1)S(1)}, u32[]{:S(2)}, u32[]{:S(2)}) collective-permute-start(bf16[256,128]{1,0:T(8,128)(2,1)S(1)} %get-tuple-element.56.own_ref), channel_id=1, source_target_pairs={{0,16},{8,24},{16,0},{24,8},{1,17},{9,25},{17,1},{25,9},{2,18},{10... | collective-permute-start | bytes 196616 | tf_op jit(solution)/shard_map/ppermute | solution.py:22
  29.1 4.3 %collective-permute-start.11 = (bf16[256,128]{1,0:T(8,128)(2,1)S(1)}, bf16[256,128]{1,0:T(8,128)(2,1)S(1)}, u32[]{:S(2)}, u32[]{:S(2)}) collective-permute-start(bf16[256,128]{1,0:T(8,128)(2,1)S(1)} %get-tuple-element.56.own_ref), channel_id=1, source_target_pairs={{0,8},{8,0},{16,24},{24,16},{1,9},{9,1},{17,25},{25,17},{2,10},{10... | collective-permute-start | bytes 196616 | tf_op jit(solution)/shard_map/ppermute | solution.py:22
  32.7 26.4 %copy-start.3 = (f32[172]{0:T(256)S(1)}, f32[172]{0:T(256)}, u32[]{:S(2)}) copy-start(f32[172]{0:T(256)} %param.18) | copy-start | bytes 2068
  34.4 5.7 %collective-permute-start.14 = (bf16[96,256]{1,0:T(8,128)(2,1)S(1)}, bf16[96,256]{1,0:T(8,128)(2,1)S(1)}, u32[]{:S(2)}, u32[]{:S(2)}) collective-permute-start(bf16[96,256]{1,0:T(8,128)(2,1)S(1)} %get-tuple-element.66), channel_id=1, source_target_pairs={{0,8},{8,0},{16,24},{24,16},{1,9},{9,1},{17,25},{25,17},{2,10},{10... | collective-permute-start | bytes 147464 | tf_op jit(solution)/shard_map/ppermute | solution.py:22
  35.5 4.7 %collective-permute-start.15 = (bf16[96,256]{1,0:T(8,128)(2,1)S(1)}, bf16[96,256]{1,0:T(8,128)(2,1)S(1)}, u32[]{:S(2)}, u32[]{:S(2)}) collective-permute-start(bf16[96,256]{1,0:T(8,128)(2,1)S(1)} %get-tuple-element.67), channel_id=1, source_target_pairs={{0,16},{8,24},{16,0},{24,8},{1,17},{9,25},{17,1},{25,9},{2,18},{10... | collective-permute-start | bytes 147464 | tf_op jit(solution)/shard_map/ppermute | solution.py:22
  36.2 5.0 %collective-permute-start.16 = (bf16[96,256]{1,0:T(8,128)(2,1)S(1)}, bf16[96,256]{1,0:T(8,128)(2,1)S(1)}, u32[]{:S(2)}, u32[]{:S(2)}) collective-permute-start(bf16[96,256]{1,0:T(8,128)(2,1)S(1)} %get-tuple-element.68), channel_id=1, source_target_pairs={{0,24},{8,16},{16,8},{24,0},{1,25},{9,17},{17,9},{25,1},{2,26},{10... | collective-permute-start | bytes 147464 | tf_op jit(solution)/shard_map/ppermute | solution.py:22
  40.0 2.5 %collective-permute-start.13 = (bf16[4,176,256]{2,1,0:T(8,128)(2,1)S(1)}, bf16[4,176,256]{2,1,0:T(8,128)(2,1)S(1)}, u32[]{:S(2)}, u32[]{:S(2)}) collective-permute-start(bf16[4,176,256]{2,1,0:T(8,128)(2,1)S(1)} %get-tuple-element.65), channel_id=1, source_target_pairs={{0,1},{1,0},{2,3},{3,2},{4,5},{5,4},{6,7},{7,6},{8,9},{9,8},{10,11... | collective-permute-start | bytes 1081352 | tf_op jit(solution)/shard_map/ppermute | solution.py:22
  41.2 1.4 %collective-permute-start.17 = (f32[96,256]{1,0:T(8,128)S(1)}, f32[96,256]{1,0:T(8,128)S(1)}, u32[]{:S(2)}, u32[]{:S(2)}) collective-permute-start(f32[96,256]{1,0:T(8,128)S(1)} %convert_add_fusion.mine_ref), channel_id=1, source_target_pairs={{0,1},{1,0},{2,3},{3,2},{4,5},{5,4},{6,7},{7,6},{8,9},{9,8},{10,11... | collective-permute-start | bytes 294920 | tf_op jit(solution)/shard_map/ppermute | solution.py:22
  42.7 8.0 %collective-permute-start.23 = (bf16[96,256]{1,0:T(8,128)(2,1)S(1)}, bf16[96,256]{1,0:T(8,128)(2,1)S(1)}, u32[]{:S(2)}, u32[]{:S(2)}) collective-permute-start(bf16[96,256]{1,0:T(8,128)(2,1)S(1)} %get-tuple-element.73), channel_id=1, source_target_pairs={{0,6},{1,7},{2,4},{3,5},{4,2},{5,3},{6,0},{7,1},{8,14},{9,15},{10,... | collective-permute-start | bytes 147464 | tf_op jit(solution)/shard_map/ppermute | solution.py:22
  45.7 6.5 %collective-permute-start.22 = (bf16[96,256]{1,0:T(8,128)(2,1)S(1)}, bf16[96,256]{1,0:T(8,128)(2,1)S(1)}, u32[]{:S(2)}, u32[]{:S(2)}) collective-permute-start(bf16[96,256]{1,0:T(8,128)(2,1)S(1)} %get-tuple-element.73), channel_id=1, source_target_pairs={{0,4},{1,5},{2,6},{3,7},{4,0},{5,1},{6,2},{7,3},{8,12},{9,13},{10,... | collective-permute-start | bytes 147464 | tf_op jit(solution)/shard_map/ppermute | solution.py:22
  45.7 6.7 %collective-permute-start.21 = (bf16[96,256]{1,0:T(8,128)(2,1)S(1)}, bf16[96,256]{1,0:T(8,128)(2,1)S(1)}, u32[]{:S(2)}, u32[]{:S(2)}) collective-permute-start(bf16[96,256]{1,0:T(8,128)(2,1)S(1)} %get-tuple-element.73), channel_id=1, source_target_pairs={{0,2},{1,3},{2,0},{3,1},{4,6},{5,7},{6,4},{7,5},{8,10},{9,11},{10,... | collective-permute-start | bytes 147464 | tf_op jit(solution)/shard_map/ppermute | solution.py:22
  47.1 7.8 %collective-permute-start.18 = (bf16[176,256]{1,0:T(8,128)(2,1)S(1)}, bf16[176,256]{1,0:T(8,128)(2,1)S(1)}, u32[]{:S(2)}, u32[]{:S(2)}) collective-permute-start(bf16[176,256]{1,0:T(8,128)(2,1)S(1)} %get-tuple-element.70), channel_id=1, source_target_pairs={{0,2},{1,3},{2,0},{3,1},{4,6},{5,7},{6,4},{7,5},{8,10},{9,11},{10,... | collective-permute-start | bytes 270344 | tf_op jit(solution)/shard_map/ppermute | solution.py:22
  47.7 9.8 %collective-permute-start.19 = (bf16[176,256]{1,0:T(8,128)(2,1)S(1)}, bf16[176,256]{1,0:T(8,128)(2,1)S(1)}, u32[]{:S(2)}, u32[]{:S(2)}) collective-permute-start(bf16[176,256]{1,0:T(8,128)(2,1)S(1)} %get-tuple-element.71), channel_id=1, source_target_pairs={{0,4},{1,5},{2,6},{3,7},{4,0},{5,1},{6,2},{7,3},{8,12},{9,13},{10,... | collective-permute-start | bytes 270344 | tf_op jit(solution)/shard_map/ppermute | solution.py:22
  50.7 6.9 %collective-permute-start.20 = (bf16[176,256]{1,0:T(8,128)(2,1)S(1)}, bf16[176,256]{1,0:T(8,128)(2,1)S(1)}, u32[]{:S(2)}, u32[]{:S(2)}) collective-permute-start(bf16[176,256]{1,0:T(8,128)(2,1)S(1)} %get-tuple-element.72), channel_id=1, source_target_pairs={{0,6},{1,7},{2,4},{3,5},{4,2},{5,3},{6,0},{7,1},{8,14},{9,15},{10,... | collective-permute-start | bytes 270344 | tf_op jit(solution)/shard_map/ppermute | solution.py:22
  52.4 5.6 %collective-permute-start.26 = (bf16[96,256]{1,0:T(8,128)(2,1)S(1)}, bf16[96,256]{1,0:T(8,128)(2,1)S(1)}, u32[]{:S(2)}, u32[]{:S(2)}) collective-permute-start(bf16[96,256]{1,0:T(8,128)(2,1)S(1)} %add_convert_fusion.refs_3_), channel_id=1, source_target_pairs={{0,24},{8,16},{16,8},{24,0},{1,25},{9,17},{17,9},{25,1},{2,26},{10... | collective-permute-start | bytes 147464 | tf_op jit(solution)/shard_map/ppermute | solution.py:22
  54.2 4.2 %collective-permute-start.25 = (bf16[96,256]{1,0:T(8,128)(2,1)S(1)}, bf16[96,256]{1,0:T(8,128)(2,1)S(1)}, u32[]{:S(2)}, u32[]{:S(2)}) collective-permute-start(bf16[96,256]{1,0:T(8,128)(2,1)S(1)} %add_convert_fusion.refs_3_), channel_id=1, source_target_pairs={{0,16},{8,24},{16,0},{24,8},{1,17},{9,25},{17,1},{25,9},{2,18},{10... | collective-permute-start | bytes 147464 | tf_op jit(solution)/shard_map/ppermute | solution.py:22
  55.0 4.1 %collective-permute-start.24 = (bf16[96,256]{1,0:T(8,128)(2,1)S(1)}, bf16[96,256]{1,0:T(8,128)(2,1)S(1)}, u32[]{:S(2)}, u32[]{:S(2)}) collective-permute-start(bf16[96,256]{1,0:T(8,128)(2,1)S(1)} %add_convert_fusion.refs_3_), channel_id=1, source_target_pairs={{0,8},{8,0},{16,24},{24,16},{1,9},{9,1},{17,25},{25,17},{2,10},{10... | collective-permute-start | bytes 147464 | tf_op jit(solution)/shard_map/ppermute | solution.py:22
